TPU v7x, 32 devices: a whole 2x2x4 slice. The times are simulated.
32 devices in a mesh: dp: 4 (over x, core), fsdp: 8 (over z, y).
Axes of the slice: x: 2, y: 2, z: 4, core: 2. Of those that a mesh axis runs over, the one named last changes fastest.
Arguments:
- tokens: bfloat16 [8192, 1024], P(('dp', 'fsdp')), may hold values from -6 to 6
- seq_lengths: int32 [128], P(('dp', 'fsdp')), may hold values from 0 to 256, as said below
- cotangent: bfloat16 [8192, 1024], P(('dp', 'fsdp')), may hold values from -6 to 6
- w_query: bfloat16 [1024, 1024], P(('dp', 'fsdp')), may hold values from -0.1875 to 0.1875
- w_latent: bfloat16 [1024, 512], P(('dp', 'fsdp')), may hold values from -0.1875 to 0.1875
- w_keyup: bfloat16 [512, 512], P(('dp', 'fsdp')), may hold values from -0.375 to 0.375
- w_valup: bfloat16 [512, 512], P(('dp', 'fsdp')), may hold values from -0.375 to 0.375
- w_output: bfloat16 [1024, 1024], P(('dp', 'fsdp')), may hold values from -1 to 1
- norm_attn: bfloat16 [1024], P(('dp', 'fsdp')), may hold values from 0.5 to 1.5
- norm_ffn: bfloat16 [1024], P(('dp', 'fsdp')), may hold values from 0.5 to 1.5
- w_gate: bfloat16 [1024, 2816], P(('dp', 'fsdp')), may hold values from -0.1875 to 0.1875
- w_up: bfloat16 [1024, 2816], P(('dp', 'fsdp')), may hold values from -0.1875 to 0.1875
- w_down: bfloat16 [2816, 1024], P(('dp', 'fsdp')), may hold values from -0.109375 to 0.109375
Outputs:
- block_out: bfloat16 [8192, 1024], P(('dp', 'fsdp'))
- grad_tokens: float32 [8192, 1024], P(('dp', 'fsdp'))
- grad_query: float32 [1024, 1024], P(('dp', 'fsdp'))
- grad_latent: float32 [1024, 512], P(('dp', 'fsdp'))
- grad_keyup: float32 [512, 512], P(('dp', 'fsdp'))
- grad_valup: float32 [512, 512], P(('dp', 'fsdp'))
- grad_output: float32 [1024, 1024], P(('dp', 'fsdp'))
- grad_norm_attn: float32 [1024], P(('dp', 'fsdp'))
- grad_norm_ffn: float32 [1024], P(('dp', 'fsdp'))
- grad_gate: float32 [1024, 2816], P(('dp', 'fsdp'))
- grad_up: float32 [1024, 2816], P(('dp', 'fsdp'))
- grad_down: float32 [2816, 1024], P(('dp', 'fsdp'))
Inputs may be any that keep to these rules, and one draw needn't show every extreme that they name: `seq_lengths`: each device's 4 entries are sequence lengths that sum to at most 256; unused slots hold 0; in every draw some device holds one sequence of 256.
All inputs are finite; a program needn't handle non-finite values.
Results may differ from a plain program's by a relative error of at most 0.014.
Values may be sent and summed in bfloat16 or wider, within the bound.
A program may use at most 192 MiB of HBM per device.

v0:
```python
import jax
import jax.numpy as jnp
from jax import lax
from jax.sharding import PartitionSpec as P

HEADS = 16
HEAD_DIM = 64
GROUPS = 2
LATENT = 256


EPSILON = 1e-06


def matmul(left, right):
    return jnp.dot(left, right, preferred_element_type=jnp.float32)


def matmul_left(left, right):
    return lax.dot_general(
        left, right, (((0,), (0,)), ((), ())), preferred_element_type=jnp.float32
    )


def matmul_right(left, right):
    return lax.dot_general(
        left, right, (((1,), (1,)), ((), ())), preferred_element_type=jnp.float32
    )


def segment_mask(lengths, rows):
    position = jnp.arange(rows, dtype=jnp.int32)
    ends = jnp.cumsum(lengths)
    segment = jnp.sum((position[None, :] >= ends[:, None]).astype(jnp.int32), axis=0)
    allowed = (segment[:, None] == segment[None, :]) & (position[None, :] <= position[:, None])
    valid = (position < ends[-1]).astype(jnp.float32)
    return (allowed, valid)


def head_forward(allowed, scale):

    def one_head(operands):
        query, key_rows, value_rows = operands
        scores = jnp.where(allowed, matmul_right(query, key_rows) * scale, -1e30)
        peak = jnp.max(scores, axis=1, keepdims=True)
        expo = jnp.exp(scores - peak)
        total = jnp.sum(expo, axis=1, keepdims=True)
        weights = (expo / total).astype(jnp.bfloat16)
        result = matmul(weights, value_rows).astype(jnp.bfloat16)
        return (result, peak[:, 0] + jnp.log(total[:, 0]))

    return one_head


def head_backward(allowed, scale):

    def one_head(operands):
        query, key_rows, value_rows, grad_out, logsum = operands
        scores = jnp.where(allowed, matmul_right(query, key_rows) * scale, -1e30)
        probs = jnp.exp(scores - logsum[:, None])
        grad_value = matmul_left(probs.astype(jnp.bfloat16), grad_out)
        grad_probs = matmul_right(grad_out, value_rows)
        inner = jnp.sum(probs * grad_probs, axis=1, keepdims=True)
        grad_scores = (probs * (grad_probs - inner)).astype(jnp.bfloat16)
        grad_query = matmul(grad_scores, key_rows) * scale
        grad_key = matmul_left(grad_scores, query) * scale
        return (grad_query, grad_key, grad_value)

    return one_head


def norm_back(grad_normed, inputs, rstd, gain):
    scaled = grad_normed * gain
    grad_in = rstd * (
        scaled - inputs * rstd * rstd * jnp.mean(scaled * inputs, axis=1, keepdims=True)
    )
    grad_gain = jnp.sum(grad_normed * inputs * rstd, axis=0)
    return (grad_in, grad_gain)


def column_term(left, right):
    return matmul_left(left, right)


def forward(tokens, allowed, attn_w, ffn_w):
    w_query, w_latent, w_keyup, w_valup, w_output, gain_one = attn_w
    gain_two, w_gate, w_up, w_down = ffn_w
    rows = tokens.shape[0]
    inputs = tokens.astype(jnp.float32)
    rstd_one = lax.rsqrt(jnp.mean(inputs * inputs, axis=1, keepdims=True) + EPSILON)
    normed = (inputs * rstd_one * gain_one.astype(jnp.float32)).astype(jnp.bfloat16)
    query = matmul(normed, w_query).astype(jnp.bfloat16)
    latent = matmul(normed, w_latent).astype(jnp.bfloat16)
    lat3 = latent.reshape(rows, GROUPS, LATENT)
    keys = jnp.einsum(
        "tgl,glf->tgf",
        lat3,
        w_keyup.reshape(GROUPS, LATENT, -1),
        preferred_element_type=jnp.float32,
    ).astype(jnp.bfloat16)
    values = jnp.einsum(
        "tgl,glf->tgf",
        lat3,
        w_valup.reshape(GROUPS, LATENT, -1),
        preferred_element_type=jnp.float32,
    ).astype(jnp.bfloat16)
    heads_query = query.reshape(rows, HEADS, HEAD_DIM).transpose(1, 0, 2)
    heads_key = keys.reshape(rows, HEADS, HEAD_DIM).transpose(1, 0, 2)
    heads_value = values.reshape(rows, HEADS, HEAD_DIM).transpose(1, 0, 2)
    attended, logsum = lax.map(
        head_forward(allowed, HEAD_DIM ** (-0.5)), (heads_query, heads_key, heads_value)
    )
    merged = attended.transpose(1, 0, 2).reshape(rows, HEADS * HEAD_DIM)
    middle = inputs + matmul(merged, w_output)
    rstd_two = lax.rsqrt(jnp.mean(middle * middle, axis=1, keepdims=True) + EPSILON)
    normed_two = (middle * rstd_two * gain_two.astype(jnp.float32)).astype(jnp.bfloat16)
    gate = matmul(normed_two, w_gate)
    upper = matmul(normed_two, w_up)
    mixed = (jax.nn.silu(gate) * upper).astype(jnp.bfloat16)
    result = middle + matmul(mixed, w_down)
    return (
        result,
        inputs,
        rstd_one,
        normed,
        lat3,
        heads_query,
        heads_key,
        heads_value,
        logsum,
        merged,
        middle,
        rstd_two,
        normed_two,
        gate,
        upper,
        mixed,
    )


def on_device(
    tokens,
    seq_lengths,
    cotangent,
    w_query,
    w_latent,
    w_keyup,
    w_valup,
    w_output,
    norm_attn,
    norm_ffn,
    w_gate,
    w_up,
    w_down,
):
    rows = tokens.shape[0]
    allowed, valid = segment_mask(seq_lengths, rows)
    attn_w = (
        lax.all_gather(w_query, ("dp", "fsdp"), axis=0, tiled=True),
        lax.all_gather(w_latent, ("dp", "fsdp"), axis=0, tiled=True),
        lax.all_gather(w_keyup, ("dp", "fsdp"), axis=0, tiled=True),
        lax.all_gather(w_valup, ("dp", "fsdp"), axis=0, tiled=True),
        lax.all_gather(w_output, ("dp", "fsdp"), axis=0, tiled=True),
        lax.all_gather(norm_attn, ("dp", "fsdp"), axis=0, tiled=True),
    )
    ffn_w = (
        lax.all_gather(norm_ffn, ("dp", "fsdp"), axis=0, tiled=True),
        lax.all_gather(w_gate, ("dp", "fsdp"), axis=0, tiled=True),
        lax.all_gather(w_up, ("dp", "fsdp"), axis=0, tiled=True),
        lax.all_gather(w_down, ("dp", "fsdp"), axis=0, tiled=True),
    )
    saved = forward(tokens, allowed, attn_w, ffn_w)
    block_out = saved[0].astype(jnp.bfloat16)
    attn_w = (
        lax.all_gather(w_query, ("dp", "fsdp"), axis=0, tiled=True),
        lax.all_gather(w_latent, ("dp", "fsdp"), axis=0, tiled=True),
        lax.all_gather(w_keyup, ("dp", "fsdp"), axis=0, tiled=True),
        lax.all_gather(w_valup, ("dp", "fsdp"), axis=0, tiled=True),
        lax.all_gather(w_output, ("dp", "fsdp"), axis=0, tiled=True),
        lax.all_gather(norm_attn, ("dp", "fsdp"), axis=0, tiled=True),
    )
    ffn_w = (
        lax.all_gather(norm_ffn, ("dp", "fsdp"), axis=0, tiled=True),
        lax.all_gather(w_gate, ("dp", "fsdp"), axis=0, tiled=True),
        lax.all_gather(w_up, ("dp", "fsdp"), axis=0, tiled=True),
        lax.all_gather(w_down, ("dp", "fsdp"), axis=0, tiled=True),
    )
    saved = forward(tokens, allowed, attn_w, ffn_w)
    (
        result,
        inputs,
        rstd_one,
        normed,
        lat3,
        heads_query,
        heads_key,
        heads_value,
        logsum,
        merged,
        middle,
        rstd_two,
        normed_two,
        gate,
        upper,
        mixed,
    ) = saved
    full_query, full_latent, full_keyup, full_valup, full_output, gain_one = attn_w
    gain_two, full_gate, full_up, full_down = ffn_w
    ff_width = full_gate.shape[1]
    grad_out = cotangent.astype(jnp.float32) * valid[:, None]
    grad_low = grad_out.astype(jnp.bfloat16)
    grad_mixed = matmul_right(grad_low, full_down)
    sigmoid_gate = jax.nn.sigmoid(gate)
    grad_gate_low = (
        grad_mixed * upper * sigmoid_gate * (1.0 + gate * (1.0 - sigmoid_gate))
    ).astype(jnp.bfloat16)
    grad_upper_low = (grad_mixed * jax.nn.silu(gate)).astype(jnp.bfloat16)
    grad_normed_two = matmul_right(grad_gate_low, full_gate) + matmul_right(grad_upper_low, full_up)
    grad_mid_norm, grad_gain_two = norm_back(
        grad_normed_two, middle, rstd_two, gain_two.astype(jnp.float32)
    )
    grad_middle = grad_out + grad_mid_norm
    down_own = lax.psum_scatter(
        column_term(mixed, grad_low), ("dp", "fsdp"), scatter_dimension=0, tiled=True
    )
    packed_ffn = jnp.concatenate([grad_gate_low, grad_upper_low], axis=1)
    ffn_own = lax.psum_scatter(
        column_term(normed_two, packed_ffn), ("dp", "fsdp"), scatter_dimension=0, tiled=True
    )
    grad_branch = grad_middle.astype(jnp.bfloat16)
    grad_merged = matmul_right(grad_branch, full_output).astype(jnp.bfloat16)
    output_own = lax.psum_scatter(
        column_term(merged, grad_branch), ("dp", "fsdp"), scatter_dimension=0, tiled=True
    )
    heads_grad = grad_merged.reshape(rows, HEADS, HEAD_DIM).transpose(1, 0, 2)
    grad_hq, grad_hk, grad_hv = lax.map(
        head_backward(allowed, HEAD_DIM ** (-0.5)),
        (heads_query, heads_key, heads_value, heads_grad, logsum),
    )
    grad_query_low = grad_hq.transpose(1, 0, 2).reshape(rows, HEADS * HEAD_DIM).astype(jnp.bfloat16)
    grad_keys_low = grad_hk.transpose(1, 0, 2).reshape(rows, GROUPS, -1).astype(jnp.bfloat16)
    grad_values_low = grad_hv.transpose(1, 0, 2).reshape(rows, GROUPS, -1).astype(jnp.bfloat16)
    head_cols = grad_keys_low.shape[2]
    keyup3 = full_keyup.reshape(GROUPS, LATENT, -1)
    valup3 = full_valup.reshape(GROUPS, LATENT, -1)
    grad_lat = jnp.einsum("tgf,glf->tgl", grad_keys_low, keyup3, preferred_element_type=jnp.float32)
    grad_lat = grad_lat + jnp.einsum(
        "tgf,glf->tgl", grad_values_low, valup3, preferred_element_type=jnp.float32
    )
    grad_latent_low = grad_lat.reshape(rows, GROUPS * LATENT).astype(jnp.bfloat16)
    latent_flat = lat3.reshape(rows, GROUPS * LATENT)
    paired = jnp.concatenate([grad_keys_low, grad_values_low], axis=2).reshape(
        rows, GROUPS * 2 * head_cols
    )
    count = w_keyup.shape[0] * lax.axis_size(("dp", "fsdp"))
    product = matmul_left(latent_flat, paired).reshape(count, GROUPS, 2 * head_cols)
    owner = jnp.arange(count, dtype=jnp.int32) // LATENT
    picker = (owner[:, None] == jnp.arange(GROUPS, dtype=jnp.int32)[None, :]).astype(jnp.float32)
    latent_own = lax.psum_scatter(
        jnp.sum(product * picker[:, :, None], axis=1),
        ("dp", "fsdp"),
        scatter_dimension=0,
        tiled=True,
    )
    grad_normed = matmul_right(grad_query_low, full_query) + matmul_right(
        grad_latent_low, full_latent
    )
    packed_attn = jnp.concatenate([grad_query_low, grad_latent_low], axis=1)
    attn_own = lax.psum_scatter(
        column_term(normed, packed_attn), ("dp", "fsdp"), scatter_dimension=0, tiled=True
    )
    grad_in_norm, grad_gain_one = norm_back(
        grad_normed, inputs, rstd_one, gain_one.astype(jnp.float32)
    )
    grad_tokens = grad_middle + grad_in_norm
    gains_own = (
        lax.psum_scatter(grad_gain_one, ("dp", "fsdp"), scatter_dimension=0, tiled=True),
        lax.psum_scatter(grad_gain_two, ("dp", "fsdp"), scatter_dimension=0, tiled=True),
    )
    query_cols = HEADS * HEAD_DIM
    return (
        block_out,
        grad_tokens,
        attn_own[:, :query_cols],
        attn_own[:, query_cols:],
        latent_own[:, :head_cols],
        latent_own[:, head_cols:],
        output_own,
        gains_own[0],
        gains_own[1],
        ffn_own[:, :ff_width],
        ffn_own[:, ff_width:],
        down_own,
    )


def solution(mesh):
    return jax.shard_map(
        on_device,
        mesh=mesh,
        in_specs=(
            P(("dp", "fsdp"), None),
            P(("dp", "fsdp")),
            P(("dp", "fsdp"), None),
            P(("dp", "fsdp"), None),
            P(("dp", "fsdp"), None),
            P(("dp", "fsdp"), None),
            P(("dp", "fsdp"), None),
            P(("dp", "fsdp"), None),
            P(("dp", "fsdp")),
            P(("dp", "fsdp")),
            P(("dp", "fsdp"), None),
            P(("dp", "fsdp"), None),
            P(("dp", "fsdp"), None),
        ),
        out_specs=(
            P(("dp", "fsdp"), None),
            P(("dp", "fsdp"), None),
            P(("dp", "fsdp"), None),
            P(("dp", "fsdp"), None),
            P(("dp", "fsdp"), None),
            P(("dp", "fsdp"), None),
            P(("dp", "fsdp"), None),
            P(("dp", "fsdp")),
            P(("dp", "fsdp")),
            P(("dp", "fsdp"), None),
            P(("dp", "fsdp"), None),
            P(("dp", "fsdp"), None),
        ),
        check_vma=False,
    )
```

profile of v0, /device:TPU:0, one launch (start us, length us, event | category | flops | bytes accessed | tf_op | source)
XLA Modules:
  0.0 1678.0 jit_solution(2810994576037242797)
XLA Ops:
  12.9 42.0 %all-reduce.5 = (bf16[1024]{0:T(1024)(128)(2,1)S(1)}, bf16[1024]{0:T(1024)(128)(2,1)S(1)}) all-reduce(bf16[1024]{0:T(1024)(128)(2,1)S(1)} %dynamic-update-slice, bf16[1024]{0:T(1024)(128)(2,1)S(1)} %dynamic-update-slice.1), channel_id=1, replica_groups=mesh['dp'=4,'fsdp'=8] {'dp','fsdp'}, use_global_device_ids=true, to_apply=%add | all-reduce | flops 2048 | bytes 8192
  56.2 69.9 %all_gather.43 = bf16[512,512]{1,0:T(8,128)(2,1)S(1)} all-gather(bf16[16,512]{1,0:T(8,128)(2,1)} %param.24), channel_id=1, replica_groups=mesh['dp'=4,'fsdp'=8] {'dp','fsdp'}, dimensions={0}, use_global_device_ids=true | all-gather | bytes 540672 | tf_op jit(solution)/shard_map/all_gather | solution.py:161
  126.1 67.4 %all_gather.44 = bf16[512,512]{1,0:T(8,128)(2,1)S(1)} all-gather(bf16[16,512]{1,0:T(8,128)(2,1)} %param.25), channel_id=1, replica_groups=mesh['dp'=4,'fsdp'=8] {'dp','fsdp'}, dimensions={0}, use_global_device_ids=true | all-gather | bytes 540672 | tf_op jit(solution)/shard_map/all_gather | solution.py:162
  195.6 1.9 convolution_convert_fusion.6
  201.3 2.4 convolution_convert_fusion.5
  205.2 37.0 %while.40 = (s32[]{:T(128)}, bf16[16,256,64]{1,2,0:T(8,128)(2,1)S(1)}, f32[16,256]{1,0:T(8,128)S(1)}, bf16[16,256,64]{2,1,0:T(8,128)(2,1)}, bf16[16,256,64]{2,1,...) while((s32[]{:T(128)}, ...), condition=%wide.region_11.12_spmd.clone, body=%wide.region_8.11_spmd.clone.sunk | while | flops 17514240 | bytes 1030249 | solution.py:110
  242.3 2.6 multiply_reduce_fusion.4
  245.0 10.2 all-gather.13.cloned.1.call-done
  255.2 5.9 fusion.130
  261.1 62.6 %all-gather.15.cloned.1.call-done = bf16[1024,2816]{1,0:T(8,128)(2,1)} async-done(((bf16[32,2816]{1,0:T(8,128)(2,1)}), bf16[1024,2816]{1,0:T(8,128)(2,1)}) %all-gather.15.cloned.1.call-update) | async-done | bytes 5767184 | tf_op jit(solution)/shard_map/all_gather | solution.py:169
  323.7 5.9 fusion.129
  329.6 63.2 %all-gather.17.cloned.1.call-done = bf16[2816,1024]{1,0:T(8,128)(2,1)} async-done(((bf16[88,1024]{1,0:T(8,128)(2,1)}), bf16[2816,1024]{1,0:T(8,128)(2,1)}) %all-gather.17.cloned.1.call-update) | async-done | bytes 5767184 | tf_op jit(solution)/shard_map/all_gather | solution.py:170
  392.7 6.7 multiply_convert_fusion.2
  399.5 5.4 fusion.131
  404.9 1.9 multiply_reduce_fusion.2
  411.2 2.0 copy.81
  413.3 113.0 %while.41 = (s32[]{:T(128)}, bf16[16,256,64]{1,2,0:T(8,128)(2,1)}, bf16[16,256,64]{1,2,0:T(8,128)(2,1)}, bf16[16,256,64]{1,2,0:T(8,128)(2,1)}, bf16[16,256,64]{2...) while((s32[]{:T(128)}, bf16[16,256,64]{1,2,0:T(8,128)(2,1)}, ...), condition=%wide.region_16.17_spmd.clone, body=%wide.region_14.16_spmd.clone.sunk | while | flops 42761984 | bytes 2568313 | solution.py:236
  526.3 3.8 multiply_reduce_fusion.1
  533.3 3.8 fusion.91
  538.2 11.2 fusion.67
  550.4 3.9 fusion.106
  555.3 8.8 fusion.72
  565.0 45.3 %while.39 = (s32[]{:T(128)}, bf16[16,256,64]{1,2,0:T(8,128)(2,1)}, bf16[16,256,64]{2,1,0:T(8,128)(2,1)}, bf16[16,256,64]{2,1,0:T(8,128)(2,1)}, bf16[16,256,64]{2,1,0:T(8,128)(2,1)}, /*index=5*/s32[256]{0:T(256)S(1)}, s32[]{:T(128)}) while((s32[]{:T(128)}, bf16[16,256,64]{1,2,0:T(8,128)(2,1)}, bf16[16,256,64]{2,1,0:T(8,128)(2,1)}, ...), condition=%wide.region_6.7_spmd.clone, body=%wide.region_3.6_spmd.clone.sunk | while | flops 17513984 | bytes 1025109 | solution.py:110
  610.3 2.9 multiply_reduce_fusion.5
  615.1 40.9 %all-reduce.4 = (f32[1024]{0:T(1024)S(1)}, f32[1024]{0:T(1024)S(1)}) all-reduce(f32[1024]{0:T(1024)S(1)} %get-tuple-element.268, f32[1024]{0:T(1024)S(1)} %get-tuple-element.266), channel_id=5, replica_groups=mesh['dp'=4,'fsdp'=8] {'dp','fsdp'}, use_global_device_ids=true, to_apply=%region_23.24.clone | all-reduce | flops 2048 | bytes 16384
  658.5 6.1 fusion.95
  664.6 9.3 fusion.73
  675.3 109.7 %reduce-scatter.6.cloned.1.call-done = f32[32,1536]{1,0:T(8,128)} async-done(((f32[1024,1536]{1,0:T(8,128)}), f32[32,1536]{1,0:T(8,128)}) %reduce-scatter.6.cloned.1.call-update) | async-done | bytes 196624 | tf_op jit(solution)/shard_map/reduce_scatter | solution.py:269
  788.0 486.6 %reduce-scatter.12.cloned.1.call-done = f32[32,5632]{1,0:T(8,128)} async-done(((f32[1024,5632]{1,0:T(8,128)}), f32[32,5632]{1,0:T(8,128)}) %reduce-scatter.12.cloned.1.call-update) | async-done | bytes 720912 | tf_op jit(solution)/shard_map/reduce_scatter | solution.py:227
  1274.6 2.0 fusion.127
  1276.6 144.9 %reduce-scatter.10.cloned.1.call-done = f32[32,1024]{1,0:T(8,128)} async-done(((f32[1024,1024]{1,0:T(8,128)}), f32[32,1024]{1,0:T(8,128)}) %reduce-scatter.10.cloned.1.call-update) | async-done | bytes 131088 | tf_op jit(solution)/shard_map/reduce_scatter | solution.py:232
  1421.5 250.0 %reduce-scatter.14.cloned.1.call-done = f32[88,1024]{1,0:T(8,128)} async-done(((f32[2816,1024]{1,0:T(8,128)}), f32[88,1024]{1,0:T(8,128)}) %reduce-scatter.14.cloned.1.call-update) | async-done | bytes 360464 | tf_op jit(solution)/shard_map/reduce_scatter | solution.py:223
  (355 shorter events, 229.0 us)
Async XLA Ops:
  7.2 188.4 %all-gather.9.cloned.1.call-start = ((), (), s32[]{:S(2)}) async-start(), calls=%async_computation.6 | async-start | bytes 1081344 | tf_op jit(solution)/shard_map/all_gather | solution.py:160
  7.9 193.4 %all-gather.7.cloned.1.call-start = ((), (), s32[]{:S(2)}) async-start(), calls=%async_computation.5 | async-start | bytes 2162688 | tf_op jit(solution)/shard_map/all_gather | solution.py:159
  8.7 233.6 %all-gather.11.cloned.1.call-start = ((), (), s32[]{:S(2)}) async-start(), calls=%async_computation.7 | async-start | bytes 2162688 | tf_op jit(solution)/shard_map/all_gather | solution.py:163
  9.4 245.8 %all-gather.13.cloned.1.call-start = ((), (), s32[]{:S(2)}) async-start(), calls=%async_computation.8 | async-start | bytes 5947392 | tf_op jit(solution)/shard_map/all_gather | solution.py:168
  10.0 313.7 %all-gather.15.cloned.1.call-start = ((), (), s32[]{:S(2)}) async-start(), calls=%async_computation.9 | async-start | bytes 5947392 | tf_op jit(solution)/shard_map/all_gather | solution.py:169
  10.6 382.2 %all-gather.17.cloned.1.call-start = ((), (), s32[]{:S(2)}) async-start(), calls=%async_computation.10 | async-start | bytes 5947392 | tf_op jit(solution)/shard_map/all_gather | solution.py:170
  11.1 662.8 %reduce-scatter.8.cloned.1.call-start = ((), (), s32[]{:S(2)}) async-start(), calls=%async_computation.12 | async-start | bytes 2162688 | tf_op jit(solution)/shard_map/reduce_scatter | solution.py:259
  126.1 71.8 %copy-start.5 = (bf16[512,512]{1,0:T(8,128)(2,1)}, bf16[512,512]{1,0:T(8,128)(2,1)S(1)}, u32[]{:S(2)}) copy-start(bf16[512,512]{1,0:T(8,128)(2,1)S(1)} %all_gather.43) | copy-start | bytes 1572868
  198.1 3.2 copy-start
  242.2 2.8 copy-start.6
  244.8 160.0 %copy-start.4 = (f32[256,1024]{1,0:T(8,128)}, f32[256,1024]{1,0:T(8,128)S(1)}, u32[]{:S(2)}) copy-start(f32[256,1024]{1,0:T(8,128)S(1)} %get-tuple-element.335) | copy-start | bytes 3145732
  245.0 78.7 %copy-start.14 = (bf16[256,1024]{1,0:T(8,128)(2,1)}, bf16[256,1024]{1,0:T(8,128)(2,1)S(1)}, u32[]{:S(2)}) copy-start(bf16[256,1024]{1,0:T(8,128)(2,1)S(1)} %multiply_convert_fusion.5) | copy-start | bytes 1572868
  261.1 131.6 %copy-start.11 = (bf16[256,1024]{1,0:T(8,128)(2,1)S(1)}, bf16[256,1024]{1,0:T(8,128)(2,1)}, u32[]{:S(2)}) copy-start(bf16[256,1024]{1,0:T(8,128)(2,1)} %param.21) | copy-start | bytes 1572868
  399.4 5.4 copy-start.17
  399.5 5.4 copy-start.16
  399.5 5.4 copy-start.21
  404.9 1.9 copy-start.12
  406.8 2.8 copy-start.1
  530.1 254.8 %reduce-scatter.6.cloned.1.call-start = ((), (), s32[]{:S(2)}) async-start(), calls=%async_computation.11 | async-start | bytes 6488064 | tf_op jit(solution)/shard_map/reduce_scatter | solution.py:269
  530.4 2.9 copy-start.8
  537.1 1.0 copy-start.15
  537.1 737.5 %reduce-scatter.12.cloned.1.call-start = ((), (), s32[]{:S(2)}) async-start(), calls=%async_computation.14 | async-start | bytes 23789568 | tf_op jit(solution)/shard_map/reduce_scatter | solution.py:227
  549.3 1.0 copy-start.7
  549.4 872.1 %reduce-scatter.10.cloned.1.call-start = ((), (), s32[]{:S(2)}) async-start(), calls=%async_computation.13 | async-start | bytes 4325376 | tf_op jit(solution)/shard_map/reduce_scatter | solution.py:232
  554.3 1.0 copy-start.13
  554.3 1117.2 %reduce-scatter.14.cloned.1.call-start = ((), (), s32[]{:S(2)}) async-start(), calls=%async_computation.15 | async-start | bytes 11894784 | tf_op jit(solution)/shard_map/reduce_scatter | solution.py:223
  610.3 2.9 copy-start.9
  610.3 2.9 copy-start.10
  613.2 1.2 copy-start.18
  614.4 42.7 %copy-start.3 = (f32[256,1024]{1,0:T(8,128)S(1)}, f32[256,1024]{1,0:T(8,128)}, u32[]{:S(2)}) copy-start(f32[256,1024]{1,0:T(8,128)} %copy-done.2) | copy-start | bytes 3145732
  656.0 2.5 copy-start.19
  658.5 6.1 copy-start.20
  (1 other events, 1.0 us)
Sparse Core Ops, SparseCore 0:
  11.1 56.5 all-gather.8
  70.7 55.6 all-gather.6
  129.3 56.3 all-gather.10
  188.5 66.6 all-gather.12
  258.0 65.7 all-gather.14
  326.5 66.2 all-gather.16
  530.3 136.7 reduce-scatter.7
  673.6 111.2 reduce-scatter.5
  787.3 487.3 reduce-scatter.11
  1277.3 144.1 reduce-scatter.9
  1424.4 247.0 reduce-scatter.13
where the time goes:
time: 1690 us; the launch traced here: 1680 us
  waiting for transfers between devices  1130 us (67%)
  matrix products  279 us (17%)
  blocking collectives  220 us (13%)
  local copies, waits for them, and re-layouts  22.7 us (1%)
    reduce_scatter x1, waiting for transfers between devices, on_device(): lax.psum_scatter(column_term(normed_two, packed_ffn), ('dp', 'fsdp'), sca...  487 us
    reduce_scatter x1, waiting for transfers between devices, on_device(): lax.psum_scatter(column_term(mixed, grad_low), ('dp', 'fsdp'), scatter_di...  250 us
    reduce_scatter x1, waiting for transfers between devices, on_device(): lax.psum_scatter(column_term(merged, grad_branch), ('dp', 'fsdp'), scatte...  145 us
    reduce_scatter x1, waiting for transfers between devices, on_device(): lax.psum_scatter(column_term(normed, packed_attn), ('dp', 'fsdp'), scatte...  110 us
    dot_general x56, matrix products, matmul(): return jnp.dot(left, right, preferred_element_type=jnp.float32)  107 us
    dot_general x70, matrix products, matmul_right(): lax.dot_general(left, right, (((1,), (1,)), ((), ())), preferred_element_...  86 us
    unnamed x2, blocking collectives  82.9 us
    dot_general x37, matrix products, matmul_left(): lax.dot_general(left, right, (((0,), (0,)), ((), ())), preferred_element_...  82.8 us
  transfers between devices with their start and end apart: 11, of which 7 were waited for; matrix products, arithmetic and copies ran while one was open for 10% of the time, Pallas kernels for 0%

commit v1 on v0

--- a/solution.py
+++ b/solution.py
@@ -79,7 +79,7 @@
 
 
 def column_term(left, right):
-    return matmul_left(left, right)
+    return matmul_left(left, right).astype(jnp.bfloat16)
 
 
 def forward(tokens, allowed, attn_w, ffn_w):
@@ -171,21 +171,6 @@
     )
     saved = forward(tokens, allowed, attn_w, ffn_w)
     block_out = saved[0].astype(jnp.bfloat16)
-    attn_w = (
-        lax.all_gather(w_query, ("dp", "fsdp"), axis=0, tiled=True),
-        lax.all_gather(w_latent, ("dp", "fsdp"), axis=0, tiled=True),
-        lax.all_gather(w_keyup, ("dp", "fsdp"), axis=0, tiled=True),
-        lax.all_gather(w_valup, ("dp", "fsdp"), axis=0, tiled=True),
-        lax.all_gather(w_output, ("dp", "fsdp"), axis=0, tiled=True),
-        lax.all_gather(norm_attn, ("dp", "fsdp"), axis=0, tiled=True),
-    )
-    ffn_w = (
-        lax.all_gather(norm_ffn, ("dp", "fsdp"), axis=0, tiled=True),
-        lax.all_gather(w_gate, ("dp", "fsdp"), axis=0, tiled=True),
-        lax.all_gather(w_up, ("dp", "fsdp"), axis=0, tiled=True),
-        lax.all_gather(w_down, ("dp", "fsdp"), axis=0, tiled=True),
-    )
-    saved = forward(tokens, allowed, attn_w, ffn_w)
     (
         result,
         inputs,
@@ -257,7 +242,7 @@
     owner = jnp.arange(count, dtype=jnp.int32) // LATENT
     picker = (owner[:, None] == jnp.arange(GROUPS, dtype=jnp.int32)[None, :]).astype(jnp.float32)
     latent_own = lax.psum_scatter(
-        jnp.sum(product * picker[:, :, None], axis=1),
+        jnp.sum(product * picker[:, :, None], axis=1).astype(jnp.bfloat16),
         ("dp", "fsdp"),
         scatter_dimension=0,
         tiled=True,
@@ -281,16 +266,16 @@
     return (
         block_out,
         grad_tokens,
-        attn_own[:, :query_cols],
-        attn_own[:, query_cols:],
-        latent_own[:, :head_cols],
-        latent_own[:, head_cols:],
-        output_own,
+        attn_own[:, :query_cols].astype(jnp.float32),
+        attn_own[:, query_cols:].astype(jnp.float32),
+        latent_own[:, :head_cols].astype(jnp.float32),
+        latent_own[:, head_cols:].astype(jnp.float32),
+        output_own.astype(jnp.float32),
         gains_own[0],
         gains_own[1],
-        ffn_own[:, :ff_width],
-        ffn_own[:, ff_width:],
-        down_own,
+        ffn_own[:, :ff_width].astype(jnp.float32),
+        ffn_own[:, ff_width:].astype(jnp.float32),
+        down_own.astype(jnp.float32),
     )
 
 

time: 1690 us -> 1320 us (0.78)
  waiting for transfers between devices: 1130 us -> 828 us
  matrix products: 279 us -> 218 us
    reduce_scatter x1, waiting for transfers between devices: 487 us -> 248 us  [on_device(): lax.psum_scatter(column_term(normed_two, packed_ffn), ('dp', 'fsdp'), sca...]
    reduce_scatter x1, waiting for transfers between devices: 250 us -> 147 us  [on_device(): lax.psum_scatter(column_term(mixed, grad_low), ('dp', 'fsdp'), scatter_di...]
    reduce_scatter x1, waiting for transfers between devices: 0.01 us -> 55.6 us  [on_device(): lax.psum_scatter(jnp.sum(product * picker[:, :, None], axis=1).astype(jnp...]
    dot_general x56 -> x38, matrix products: 107 us -> 67.2 us  [matmul(): return jnp.dot(left, right, preferred_element_type=jnp.float32)]
    dot_general x70 -> x54, matrix products: 86 us -> 73.3 us  [matmul_right(): lax.dot_general(left, right, (((1,), (1,)), ((), ())), preferred_element_...]
  transfers between devices with their start and end apart: 11 -> 11, of which waited for: 7 -> 8; matrix products, arithmetic and copies ran while one was open for 10% -> 8% of each run, Pallas kernels for 0% -> 0%
where the time goes in v1:
time: 1320 us; the launch traced here: 1310 us
  waiting for transfers between devices  828 us (63%)
  blocking collectives  219 us (17%)
  matrix products  218 us (17%)
  other arithmetic  17.2 us (1%)
  local copies, waits for them, and re-layouts  15.2 us (1%)
  between operations  14.2 us (1%)
    reduce_scatter x1, waiting for transfers between devices, on_device(): lax.psum_scatter(column_term(normed_two, packed_ffn), ('dp', 'fsdp'), sca...  248 us
    reduce_scatter x1, waiting for transfers between devices, on_device(): lax.psum_scatter(column_term(mixed, grad_low), ('dp', 'fsdp'), scatter_di...  147 us
    reduce_scatter x1, waiting for transfers between devices, on_device(): lax.psum_scatter(column_term(merged, grad_branch), ('dp', 'fsdp'), scatte...  134 us
    reduce_scatter x1, waiting for transfers between devices, on_device(): lax.psum_scatter(column_term(normed, packed_attn), ('dp', 'fsdp'), scatte...  102 us
    unnamed x2, blocking collectives  82.1 us
    dot_general x37, matrix products, matmul_left(): lax.dot_general(left, right, (((0,), (0,)), ((), ())), preferred_element_...  74.4 us
    dot_general x54, matrix products, matmul_right(): lax.dot_general(left, right, (((1,), (1,)), ((), ())), preferred_element_...  73.3 us
    all_gather x1, blocking collectives, on_device(): lax.all_gather(w_keyup, ('dp', 'fsdp'), axis=0, tiled=True)  69.7 us
  transfers between devices with their start and end apart: 11, of which 8 were waited for; matrix products, arithmetic and copies ran while one was open for 8% of the time, Pallas kernels for 0%

profile of v1, /device:TPU:0, one launch (start us, length us, event | category | flops | bytes accessed | tf_op | source)
XLA Modules:
  0.0 1313.2 jit_solution(17332656176338326467)
XLA Ops:
  13.0 42.0 %all-reduce.5 = (bf16[1024]{0:T(1024)(128)(2,1)S(1)}, bf16[1024]{0:T(1024)(128)(2,1)S(1)}) all-reduce(bf16[1024]{0:T(1024)(128)(2,1)S(1)} %dynamic-update-slice, bf16[1024]{0:T(1024)(128)(2,1)S(1)} %dynamic-update-slice.1), channel_id=1, replica_groups=mesh['dp'=4,'fsdp'=8] {'dp','fsdp'}, use_global_device_ids=true, to_apply=%add | all-reduce | flops 2048 | bytes 8192
  56.2 69.7 %all_gather.33 = bf16[512,512]{1,0:T(8,128)(2,1)S(1)} all-gather(bf16[16,512]{1,0:T(8,128)(2,1)} %param.22), channel_id=1, replica_groups=mesh['dp'=4,'fsdp'=8] {'dp','fsdp'}, dimensions={0}, use_global_device_ids=true | all-gather | bytes 540672 | tf_op jit(solution)/shard_map/all_gather | solution.py:161
  125.9 67.5 %all_gather.34 = bf16[512,512]{1,0:T(8,128)(2,1)S(1)} all-gather(bf16[16,512]{1,0:T(8,128)(2,1)} %param.23), channel_id=1, replica_groups=mesh['dp'=4,'fsdp'=8] {'dp','fsdp'}, dimensions={0}, use_global_device_ids=true | all-gather | bytes 540672 | tf_op jit(solution)/shard_map/all_gather | solution.py:162
  195.6 1.9 convolution_convert_fusion.9
  201.3 2.4 convolution_convert_fusion.8
  205.2 36.7 %while.28 = (s32[]{:T(128)}, bf16[16,256,64]{1,2,0:T(8,128)(2,1)S(1)}, f32[16,256]{1,0:T(8,128)S(1)}, bf16[16,256,64]{2,1,0:T(8,128)(2,1)}, bf16[16,256,64]{2,1,...) while((s32[]{:T(128)}, ...), condition=%wide.region_6.7_spmd.clone, body=%wide.region_3.6_spmd.clone.sunk | while | flops 17514240 | bytes 1030249 | solution.py:110
  241.9 2.6 multiply_reduce_fusion.4
  244.7 10.3 all-gather.13.cloned.1.call-done
  255.0 5.9 fusion.94
  260.9 62.6 %all-gather.15.cloned.1.call-done = bf16[1024,2816]{1,0:T(8,128)(2,1)} async-done(((bf16[32,2816]{1,0:T(8,128)(2,1)}), bf16[1024,2816]{1,0:T(8,128)(2,1)}) %all-gather.15.cloned.1.call-update) | async-done | bytes 5767184 | tf_op jit(solution)/shard_map/all_gather | solution.py:169
  323.5 5.9 fusion.95
  329.4 63.1 %all-gather.17.cloned.1.call-done = bf16[2816,1024]{1,0:T(8,128)(2,1)} async-done(((bf16[88,1024]{1,0:T(8,128)(2,1)}), bf16[2816,1024]{1,0:T(8,128)(2,1)}) %all-gather.17.cloned.1.call-update) | async-done | bytes 5767184 | tf_op jit(solution)/shard_map/all_gather | solution.py:170
  392.6 8.9 multiply_convert_fusion.1
  401.5 5.4 fusion.96
  406.9 1.9 multiply_reduce_fusion.2
  412.0 2.1 copy.72
  414.1 113.1 %while.29 = (s32[]{:T(128)}, bf16[16,256,64]{1,2,0:T(8,128)(2,1)}, bf16[16,256,64]{1,2,0:T(8,128)(2,1)}, bf16[16,256,64]{1,2,0:T(8,128)(2,1)}, bf16[16,256,64]{2...) while((s32[]{:T(128)}, bf16[16,256,64]{1,2,0:T(8,128)(2,1)}, ...), condition=%wide.region_11.12_spmd.clone, body=%wide.region_9.11_spmd.clone.sunk | while | flops 42761984 | bytes 2568313 | solution.py:221
  527.2 3.5 multiply_reduce_fusion.1
  530.7 3.2 convolution_convert_fusion.4
  537.1 2.9 convolution_convert_fusion.3
  541.1 5.6 convolution_convert_fusion.2
  547.7 7.8 convolution_convert_fusion.1
  556.6 2.4 fusion.97
  560.7 40.0 %all-reduce.4 = (f32[1024]{0:T(1024)S(1)}, f32[1024]{0:T(1024)S(1)}) all-reduce(f32[1024]{0:T(1024)S(1)} %get-tuple-element.202, f32[1024]{0:T(1024)S(1)} %get-tuple-element.200), channel_id=5, replica_groups=mesh['dp'=4,'fsdp'=8] {'dp','fsdp'}, use_global_device_ids=true, to_apply=%region_18.19.clone | all-reduce | flops 2048 | bytes 16384
  601.9 2.5 fusion.63
  604.4 5.2 fusion.53
  609.6 55.6 %reduce-scatter.8.cloned.1.call-done = bf16[16,1024]{1,0:T(8,128)(2,1)} async-done(((bf16[512,1024]{1,0:T(8,128)(2,1)}), bf16[16,1024]{1,0:T(8,128)(2,1)}) %reduce-scatter.8.cloned.1.call-update) | async-done | bytes 32784 | tf_op jit(solution)/shard_map/reduce_scatter | solution.py:244
  666.6 134.5 %reduce-scatter.10.cloned.1.call-done = bf16[32,1024]{1,0:T(8,128)(2,1)} async-done(((bf16[1024,1024]{1,0:T(8,128)(2,1)}), bf16[32,1024]{1,0:T(8,128)(2,1)}) %reduce-scatter.10.cloned.1.call-update) | async-done | bytes 65552 | tf_op jit(solution)/shard_map/reduce_scatter | solution.py:217
  802.5 102.5 %reduce-scatter.6.cloned.1.call-done = bf16[32,1536]{1,0:T(8,128)(2,1)} async-done(((bf16[1024,1536]{1,0:T(8,128)(2,1)}), bf16[32,1536]{1,0:T(8,128)(2,1)}) %reduce-scatter.6.cloned.1.call-update) | async-done | bytes 98320 | tf_op jit(solution)/shard_map/reduce_scatter | solution.py:254
  907.9 146.7 %reduce-scatter.14.cloned.1.call-done = bf16[88,1024]{1,0:T(8,128)(2,1)} async-done(((bf16[2816,1024]{1,0:T(8,128)(2,1)}), bf16[88,1024]{1,0:T(8,128)(2,1)}) %reduce-scatter.14.cloned.1.call-update) | async-done | bytes 180240 | tf_op jit(solution)/shard_map/reduce_scatter | solution.py:208
  1056.3 248.4 %reduce-scatter.12.cloned.1.call-done = bf16[32,5632]{1,0:T(8,128)(2,1)} async-done(((bf16[1024,5632]{1,0:T(8,128)(2,1)}), bf16[32,5632]{1,0:T(8,128)(2,1)}) %reduce-scatter.12.cloned.1.call-update) | async-done | bytes 360464 | tf_op jit(solution)/shard_map/reduce_scatter | solution.py:212
  1304.8 1.9 slice_convert_fusion
  (292 shorter events, 183.1 us)
Async XLA Ops:
  7.2 188.4 %all-gather.9.cloned.1.call-start = ((), (), s32[]{:S(2)}) async-start(), calls=%async_computation.6 | async-start | bytes 1081344 | tf_op jit(solution)/shard_map/all_gather | solution.py:160
  7.9 193.4 %all-gather.7.cloned.1.call-start = ((), (), s32[]{:S(2)}) async-start(), calls=%async_computation.5 | async-start | bytes 2162688 | tf_op jit(solution)/shard_map/all_gather | solution.py:159
  8.7 233.3 %all-gather.11.cloned.1.call-start = ((), (), s32[]{:S(2)}) async-start(), calls=%async_computation.7 | async-start | bytes 2162688 | tf_op jit(solution)/shard_map/all_gather | solution.py:163
  9.4 245.6 %all-gather.13.cloned.1.call-start = ((), (), s32[]{:S(2)}) async-start(), calls=%async_computation.8 | async-start | bytes 5947392 | tf_op jit(solution)/shard_map/all_gather | solution.py:168
  10.0 313.6 %all-gather.15.cloned.1.call-start = ((), (), s32[]{:S(2)}) async-start(), calls=%async_computation.9 | async-start | bytes 5947392 | tf_op jit(solution)/shard_map/all_gather | solution.py:169
  10.6 382.0 %all-gather.17.cloned.1.call-start = ((), (), s32[]{:S(2)}) async-start(), calls=%async_computation.10 | async-start | bytes 5947392 | tf_op jit(solution)/shard_map/all_gather | solution.py:170
  11.1 654.1 %reduce-scatter.8.cloned.1.call-start = ((), (), s32[]{:S(2)}) async-start(), calls=%async_computation.12 | async-start | bytes 1081344 | tf_op jit(solution)/shard_map/reduce_scatter | solution.py:244
  125.9 71.9 %copy-start.2 = (bf16[512,512]{1,0:T(8,128)(2,1)}, bf16[512,512]{1,0:T(8,128)(2,1)S(1)}, u32[]{:S(2)}) copy-start(bf16[512,512]{1,0:T(8,128)(2,1)S(1)} %all_gather.33) | copy-start | bytes 1572868
  198.1 3.2 copy-start
  241.9 2.6 copy-start.6
  244.7 78.8 %copy-start.4 = (bf16[256,1024]{1,0:T(8,128)(2,1)}, bf16[256,1024]{1,0:T(8,128)(2,1)S(1)}, u32[]{:S(2)}) copy-start(bf16[256,1024]{1,0:T(8,128)(2,1)S(1)} %multiply_convert_fusion.4) | copy-start | bytes 1572868
  260.9 131.6 %copy-start.7 = (bf16[256,1024]{1,0:T(8,128)(2,1)S(1)}, bf16[256,1024]{1,0:T(8,128)(2,1)}, u32[]{:S(2)}) copy-start(bf16[256,1024]{1,0:T(8,128)(2,1)} %param.19) | copy-start | bytes 1572868
  401.5 5.4 copy-start.13
  401.5 5.4 copy-start.12
  401.5 5.4 copy-start.15
  406.9 1.9 copy-start.8
  408.8 1.6 copy-start.1
  530.7 270.3 %reduce-scatter.10.cloned.1.call-start = ((), (), s32[]{:S(2)}) async-start(), calls=%async_computation.13 | async-start | bytes 2162688 | tf_op jit(solution)/shard_map/reduce_scatter | solution.py:217
  533.9 371.1 %reduce-scatter.6.cloned.1.call-start = ((), (), s32[]{:S(2)}) async-start(), calls=%async_computation.11 | async-start | bytes 3244032 | tf_op jit(solution)/shard_map/reduce_scatter | solution.py:254
  534.2 2.9 copy-start.10
  540.0 1.0 copy-start.9
  540.1 514.6 %reduce-scatter.14.cloned.1.call-start = ((), (), s32[]{:S(2)}) async-start(), calls=%async_computation.15 | async-start | bytes 5947392 | tf_op jit(solution)/shard_map/reduce_scatter | solution.py:208
  546.7 1.0 copy-start.5
  546.7 758.1 %reduce-scatter.12.cloned.1.call-start = ((), (), s32[]{:S(2)}) async-start(), calls=%async_computation.14 | async-start | bytes 11894784 | tf_op jit(solution)/shard_map/reduce_scatter | solution.py:212
  555.6 1.0 copy-start.11
  556.6 2.4 copy-start.14
  600.7 3.7 copy-start.3
Sparse Core Ops, SparseCore 0:
  11.1 56.5 all-gather.8
  70.7 55.8 all-gather.6
  129.5 56.3 all-gather.10
  188.7 66.2 all-gather.12
  257.8 65.6 all-gather.14
  326.3 66.2 all-gather.16
  530.8 134.3 reduce-scatter.7
  667.6 133.4 reduce-scatter.9
  806.5 98.5 reduce-scatter.5
  907.2 147.4 reduce-scatter.13
  1057.0 247.7 reduce-scatter.11

commit v2 on v1

--- a/solution.py
+++ b/solution.py
@@ -1,6 +1,8 @@
 import jax
 import jax.numpy as jnp
 from jax import lax
+from jax.experimental import pallas as pl
+from jax.experimental.pallas import tpu as pltpu
 from jax.sharding import PartitionSpec as P
 
 HEADS = 16
@@ -279,9 +281,869 @@
     )
 
 
+MESH = pl.DeviceIdType.MESH
+F32 = jnp.float32
+BF16 = jnp.bfloat16
+SCALE = HEAD_DIM ** (-0.5)
+ROWS = 256
+WIDTH = 1024
+HALF = 1408
+DOWN = 88
+PAD = 96
+CHUNKS = ((0, 512), (512, 512), (1024, 384))
+
+
+class Slots:
+    def __init__(self):
+        self.count = 0
+
+    def take(self, number):
+        first = self.count
+        self.count += number
+        return first
+
+
+SLOTS = Slots()
+S_GAIN = SLOTS.take(5)
+S_AY = SLOTS.take(1)
+S_AZ = SLOTS.take(12)
+S_AX = SLOTS.take(8)
+S_AS = SLOTS.take(16)
+S_HALF = SLOTS.take(2)
+S_FZ = [SLOTS.take(6) for _ in range(3)]
+S_FY = [SLOTS.take(4) for _ in range(3)]
+S_FS = [SLOTS.take(8) for _ in range(3)]
+S_COT = SLOTS.take(1)
+S_N2 = SLOTS.take(1)
+S_DN2 = SLOTS.take(1)
+S_OUT = SLOTS.take(1)
+S_RS = [SLOTS.take(2) for _ in range(3)]
+S_RY = [SLOTS.take(4) for _ in range(3)]
+S_RZ = [SLOTS.take(8) for _ in range(3)]
+S_RX = SLOTS.take(2)
+S_BS = [SLOTS.take(2) for _ in range(2)]
+S_BX = [SLOTS.take(4) for _ in range(2)]
+S_BZ = [SLOTS.take(8) for _ in range(2)]
+S_BY = [SLOTS.take(1) for _ in range(2)]
+S_SUM = SLOTS.take(5)
+S_LOCAL = 8
+
+
+def nn(left, right):
+    return jnp.dot(left, right, preferred_element_type=F32)
+
+
+def nt(left, right):
+    return lax.dot_general(left, right, (((1,), (1,)), ((), ())), preferred_element_type=F32)
+
+
+def tn(left, right):
+    return lax.dot_general(left, right, (((0,), (0,)), ((), ())), preferred_element_type=F32)
+
+
+def layer_kernel(
+    tok_hbm, len_ref, cot_hbm, wq_hbm, wl_hbm, wk_hbm, wv_hbm, wo_hbm, gain_ref, wg_hbm, wu_hbm, wd_ref,
+    out_ref, gtok_ref, gq_ref, gl_ref, gk_ref, gv_ref, go_ref, gain_out, gg_ref, gu_ref, gd_ref,
+    attn, gate_w, up_w, down_w, down_c, gains, gain_full,
+    tok, bias, normed, query, latent, keys, values, merged, lse, middle, normed2, dout,
+    mixed, dgate, dup, tmp, rcv_out,
+    dmid_low, dmerged, dquery, dkeys, dvalues, dlatent,
+    pattn, s_d, s_g, s_u, y_d, y_g, y_u, z_d, z_g, z_u, x_g, x_u,
+    s_a, x_a, z_a, y_a, sum_own, sum_rcv,
+    send_sem, recv_sem, local_sem,
+):
+    snd_dn2, snd_out, rcv_dn2 = dquery, dkeys, dvalues
+    dmid = gtok_ref
+    dp = lax.axis_index("dp")
+    fs = lax.axis_index("fsdp")
+    x, c, z, y = lax.div(dp, 2), lax.rem(dp, 2), lax.div(fs, 2), lax.rem(fs, 2)
+    sib = (x * 2 + 1 - c, fs)
+    xp = ((1 - x) * 2 + c, fs)
+    yp = (dp, z * 2 + 1 - y)
+    zr = (dp, (z + 1) * 2 + y)
+    zl = (dp, (z - 1) * 2 + y)
+    z_one = (dp, (z + 1 - 2 * lax.rem(z, 2)) * 2 + y)
+    z_two = (dp, lax.rem(z + 2, 4) * 2 + y)
+
+    sends = {}
+
+    def copy(src, dst, slot, target):
+        return pltpu.make_async_remote_copy(
+            src_ref=src, dst_ref=dst, send_sem=send_sem.at[slot], recv_sem=recv_sem.at[slot],
+            device_id=target, device_id_type=MESH,
+        )
+
+    def when(cond, fn):
+        if cond is True:
+            fn()
+        else:
+            pl.when(cond)(fn)
+
+    def send(group, src, dst, slot, target, cond=True):
+        when(cond, lambda: copy(src, dst, slot, target).start())
+        sends.setdefault(group, []).append((cond, lambda: copy(src, dst, slot, target).wait_send()))
+
+    def drain(group):
+        for cond, fn in sends.pop(group, []):
+            when(cond, fn)
+
+    def arrive(dst, slot, target=None):
+        copy(dst, dst, slot, sib).wait_recv()
+
+    loads = [
+        (wq_hbm, attn.at[0, x, c, z, y]),
+        (wl_hbm, attn.at[2, x, c, z, y, :, pl.ds(0, 512)]),
+        (wk_hbm, attn.at[2, x, c, z, y, pl.ds(0, 16), pl.ds(512, 512)]),
+        (wv_hbm, attn.at[2, x, c, z, y, pl.ds(16, 16), pl.ds(512, 512)]),
+        (wo_hbm, attn.at[1, x, c, z, y]),
+        (wg_hbm.at[:, pl.ds(pl.multiple_of(x * HALF, 128), HALF)], gate_w.at[c, z, y, x]),
+        (wu_hbm.at[:, pl.ds(pl.multiple_of(x * HALF, 128), HALF)], up_w.at[c, z, y, x]),
+        (tok_hbm, tok),
+        (cot_hbm, dout.at[x]),
+    ]
+    loads = [pltpu.make_async_copy(s, d, local_sem.at[i]) for i, (s, d) in enumerate(loads)]
+    for load in loads:
+        load.start()
+    bar = pltpu.get_barrier_semaphore()
+    for target, cond in ((sib, True), (xp, True), (yp, True), (z_two, True), (zr, z < 3), (zl, z > 0)):
+        when(cond, lambda target=target: pl.semaphore_signal(bar, inc=1, device_id=target, device_id_type=MESH))
+    down_w[c, z, y] = jnp.concatenate(
+        [wd_ref[...].astype(F32), jnp.zeros((PAD - DOWN, WIDTH), F32)], axis=0
+    ).astype(BF16)
+    lane = lax.broadcasted_iota(jnp.int32, (16, 128), 1)
+    mine = lax.div(lane, 32) == lax.rem(fs, 4)
+    gains[x, c, z, y] = jnp.where(mine, gain_ref[...].astype(F32), 0.0).astype(BF16)
+    pl.semaphore_wait(bar, 5 + jnp.where((z > 0) & (z < 3), 1, 0))
+
+    def attn_blk(xx, zz, yy, cc=c):
+        return attn.at[:, xx, cc, zz, yy]
+
+    def attn_out(zz, yy):
+        blk = attn_blk(x, zz, yy)
+        send("attn", blk, blk, S_AX + zz * 2 + yy, xp)
+        send("attn", blk, blk, S_AS + x * 8 + zz * 2 + yy, sib)
+
+    def attn_z(s, k, yy):
+        right, left = attn_blk(x, z - s, yy), attn_blk(x, z + s, yy)
+        send("attn", right, right, S_AZ + k * 6 + s, zr, (z < 3) & (z - s >= 0))
+        send("attn", left, left, S_AZ + k * 6 + 3 + s, zl, (z > 0) & (z + s <= 3))
+
+    def attn_z_step(s, yy):
+        def from_left():
+            blk = attn_blk(x, z - 1 - s, yy)
+            arrive(blk, S_AZ + yy * 6 + s)
+
+        def from_right():
+            blk = attn_blk(x, z + 1 + s, yy)
+            arrive(blk, S_AZ + yy * 6 + 3 + s)
+
+        for cond, fn, zz in ((z - 1 - s >= 0, from_left, z - 1 - s), (z + 1 + s <= 3, from_right, z + 1 + s)):
+            pl.when(cond)(fn)
+            blk = attn_blk(x, zz, yy)
+            if s < 2:
+                if fn is from_left:
+                    send("attn", blk, blk, S_AZ + yy * 6 + s + 1, zr, cond & (z < 3))
+                else:
+                    send("attn", blk, blk, S_AZ + yy * 6 + 3 + s + 1, zl, cond & (z > 0))
+            send("attn", blk, blk, S_AX + zz * 2 + yy, xp, cond)
+            send("attn", blk, blk, S_AS + x * 8 + zz * 2 + yy, sib, cond)
+
+    for load in loads[:5]:
+        load.wait()
+    own = attn_blk(x, z, y)
+    send("attn", own, own, S_AY, yp)
+    attn_z(0, y, y)
+    attn_out(z, y)
+
+    other_cols = pl.ds(pl.multiple_of((1 - x) * HALF, 128), HALF)
+    send("half", wg_hbm.at[:, other_cols], gate_w.at[c, z, y, x], S_HALF, xp)
+    send("half", wu_hbm.at[:, other_cols], up_w.at[c, z, y, x], S_HALF + 1, xp)
+
+    gain_steps = (
+        (gains.at[x, c, z, y], sib),
+        (gains.at[x, :, z, y], yp),
+        (gains.at[x, :, z], xp),
+        (gains.at[:, :, z], z_one),
+        (gains.at[:, :, pl.ds(lax.div(z, 2) * 2, 2)], z_two),
+    )
+    gain_from = (
+        gains.at[x, 1 - c, z, y],
+        gains.at[x, :, z, 1 - y],
+        gains.at[1 - x, :, z],
+        gains.at[:, :, z + 1 - 2 * lax.rem(z, 2)],
+        gains.at[:, :, pl.ds(2 - lax.div(z, 2) * 2, 2)],
+    )
+
+    def gain_send(i):
+        ref, target = gain_steps[i]
+        send("gain", ref, ref, S_GAIN + i, target)
+
+    def gain_recv(i):
+        arrive(gain_from[i], S_GAIN + i)
+
+    gain_send(0)
+
+    ffn = (down_w, gate_w, up_w)
+
+    def ffn_own(t):
+        blk = ffn[t].at[c, z, y]
+        send("ffn%d" % t, blk, blk, S_FY[t] + z, yp)
+        send("ffn%d" % t, blk, blk, S_FS[t] + z * 2 + y, sib)
+
+    def ffn_own_z(t):
+        blk = ffn[t].at[c, z, y]
+        send("ffn%d" % t, blk, blk, S_FZ[t], zr, z < 3)
+        send("ffn%d" % t, blk, blk, S_FZ[t] + 3, zl, z > 0)
+
+    def ffn_z_step(t, s):
+        for right, cond, zz in ((True, z - 1 - s >= 0, z - 1 - s), (False, z + 1 + s <= 3, z + 1 + s)):
+            blk = ffn[t].at[c, zz, y]
+            slot = S_FZ[t] + (0 if right else 3) + s
+            pl.when(cond)(lambda blk=blk, slot=slot: arrive(blk, slot))
+            if s < 2:
+                on = (z < 3) if right else (z > 0)
+                send("ffn%d" % t, blk, blk, slot + 1, zr if right else zl, cond & on)
+            send("ffn%d" % t, blk, blk, S_FY[t] + zz, yp, cond)
+            send("ffn%d" % t, blk, blk, S_FS[t] + zz * 2 + y, sib, cond)
+
+    def ffn_y_step(t, zz):
+        blk = ffn[t].at[c, zz, 1 - y]
+        arrive(blk, S_FY[t] + zz)
+        send("ffn%d" % t, blk, blk, S_FS[t] + zz * 2 + 1 - y, sib)
+
+    def ffn_sib(t):
+        for k in range(8):
+            arrive(ffn[t].at[1 - c, k // 2, k % 2], S_FS[t] + k)
+
+    ffn_own(0)
+    gain_recv(0)
+    gain_send(1)
+
+    e0 = len_ref[0]
+    e1 = e0 + len_ref[1]
+    e2 = e1 + len_ref[2]
+    e3 = e2 + len_ref[3]
+
+    def segment(position):
+        return sum((position >= e).astype(jnp.int32) for e in (e0, e1, e2, e3))
+
+    row = lax.broadcasted_iota(jnp.int32, (ROWS, ROWS), 0)
+    col = lax.broadcasted_iota(jnp.int32, (ROWS, ROWS), 1)
+    bias[...] = jnp.where((segment(row) == segment(col)) & (col <= row), 0.0, -1e30)
+
+    for load in loads[5:]:
+        load.wait()
+
+    def mask_rows(k, carry):
+        rows = pl.ds(pl.multiple_of(k * 64, 64), 64)
+        position = lax.broadcasted_iota(jnp.int32, (64, WIDTH), 0) + k * 64
+        dout[x, rows] = jnp.where(position < e3, dout[x, rows].astype(F32), 0.0).astype(BF16)
+        return carry
+
+    lax.fori_loop(0, 4, mask_rows, 0)
+
+    arrive(attn_blk(x, z, 1 - y), S_AY)
+    attn_z(0, 1 - y, 1 - y)
+    attn_out(z, 1 - y)
+    gain_recv(1)
+    gain_send(2)
+    attn_z_step(0, y)
+    gain_recv(2)
+    gain_send(3)
+    attn_z_step(0, 1 - y)
+    arrive(gate_w.at[c, z, y, 1 - x], S_HALF)
+    arrive(up_w.at[c, z, y, 1 - x], S_HALF + 1)
+    ffn_own(1)
+    ffn_own(2)
+    gain_recv(3)
+    gain_send(4)
+    attn_z_step(1, y)
+    attn_z_step(1, 1 - y)
+    attn_z_step(2, y)
+    attn_z_step(2, 1 - y)
+    for t in range(3):
+        ffn_own_z(t)
+    send("cot", dout.at[x], dout.at[x], S_COT, xp)
+    gain_recv(4)
+
+    def gain_rows(k, carry):
+        g = gains.at[lax.div(k, 4), lax.div(lax.rem(k, 4), 2)]
+        part = g[pl.ds(lax.rem(k, 2) * 2, 2)].astype(F32)
+        gain_full[:, pl.ds(pl.multiple_of(k * 128, 128), 128)] = part[0, 0] + part[0, 1] + part[1, 0] + part[1, 1]
+        return carry
+
+    lax.fori_loop(0, 8, gain_rows, 0)
+
+    def norm_rows(k, carry):
+        rows = pl.ds(pl.multiple_of(k * 64, 64), 64)
+        val = tok[rows].astype(F32)
+        r1 = lax.rsqrt(jnp.mean(val * val, axis=1, keepdims=True) + EPSILON)
+        normed[rows] = (val * r1 * gain_full[0:1, :]).astype(BF16)
+        return carry
+
+    lax.fori_loop(0, 4, norm_rows, 0)
+
+    for zz in range(4):
+        for yy in range(2):
+            blk = attn_blk(1 - x, zz, yy)
+            arrive(blk, S_AX + zz * 2 + yy)
+            send("attn", blk, blk, S_AS + (1 - x) * 8 + zz * 2 + yy, sib)
+    for k in range(16):
+        arrive(attn_blk(k // 8, (k % 8) // 2, k % 2, 1 - c), S_AS + k)
+
+    def cols(n, width=256):
+        return pl.ds(pl.multiple_of(n * width, width), width)
+
+    def query_cols(n, carry):
+        w = attn[0, :, :, :, :, :, cols(n)].reshape(WIDTH, 256)
+        query[:, cols(n)] = nn(normed[...], w).astype(BF16)
+        return carry
+
+    lax.fori_loop(0, 4, query_cols, 0)
+
+    def latent_cols(n, carry):
+        w = attn[2, :, :, :, :, :, cols(n)].reshape(WIDTH, 256)
+        latent[:, cols(n)] = nn(normed[...], w).astype(BF16)
+        return carry
+
+    lax.fori_loop(0, 2, latent_cols, 0)
+
+    def up_weight(g, first):
+        return attn[2, g, :, :, :, pl.ds(first, 16), pl.ds(512, 512)].reshape(256, 512)
+
+    def key_cols(g, carry):
+        lat = latent[:, cols(g)]
+        keys[:, cols(g, 512)] = nn(lat, up_weight(g, 0)).astype(BF16)
+        values[:, cols(g, 512)] = nn(lat, up_weight(g, 16)).astype(BF16)
+        return carry
+
+    lax.fori_loop(0, GROUPS, key_cols, 0)
+    ffn_z_step(0, 0)
+
+    low_half = lax.broadcasted_iota(jnp.int32, (ROWS, 128), 1) < HEAD_DIM
+    head_lane = lax.broadcasted_iota(jnp.int32, (ROWS, 128), 1)
+    lse[...] = jnp.zeros((ROWS, 128), F32)
+
+    def halves(v):
+        zero = jnp.zeros_like(v)
+        return (jnp.where(low_half, v, zero), jnp.where(low_half, zero, v))
+
+    def attend(j, carry):
+        pair = cols(j, 128)
+        k_pair, v_pair = keys[:, pair], values[:, pair]
+        res = []
+        for h, q in enumerate(halves(query[:, pair])):
+            s = nt(q, k_pair) * SCALE + bias[...]
+            peak = jnp.max(s, axis=1, keepdims=True)
+            expo = jnp.exp(s - peak)
+            total = jnp.sum(expo, axis=1, keepdims=True)
+            res.append(nn((expo / total).astype(BF16), v_pair))
+            lse[...] = jnp.where(head_lane == j * 2 + h, peak + jnp.log(total), lse[...])
+        merged[:, pair] = jnp.where(low_half, res[0], res[1]).astype(BF16)
+        return carry
+
+    lax.fori_loop(0, 4, attend, 0)
+    ffn_z_step(0, 1)
+    lax.fori_loop(4, 8, attend, 0)
+    ffn_z_step(0, 2)
+
+    def middle_cols(n, carry):
+        w = attn[1, :, :, :, :, :, cols(n)].reshape(WIDTH, 256)
+        middle[:, cols(n)] = tok[:, cols(n)].astype(F32) + nn(merged[...], w)
+        return carry
+
+    lax.fori_loop(0, 4, middle_cols, 0)
+
+    def norm2_rows(k, carry):
+        rows = pl.ds(pl.multiple_of(k * 64, 64), 64)
+        val = middle[rows]
+        r2 = lax.rsqrt(jnp.mean(val * val, axis=1, keepdims=True) + EPSILON)
+        normed2[x, rows] = (val * r2 * gain_full[1:2, :]).astype(BF16)
+        return carry
+
+    lax.fori_loop(0, 4, norm2_rows, 0)
+    send("n2", normed2.at[x], normed2.at[x], S_N2, xp)
+
+    ffn_z_step(1, 0)
+    for zz in range(4):
+        ffn_y_step(0, zz)
+    ffn_z_step(1, 1)
+    ffn_z_step(1, 2)
+    ffn_z_step(2, 0)
+    ffn_sib(0)
+
+    def compact(k, carry):
+        pair = down_w.at[lax.div(k, 4), lax.rem(k, 4)]
+        joined = jnp.concatenate([pair[0, 0:DOWN].astype(F32), pair[1, 0:DOWN].astype(F32)], axis=0)
+        down_c[pl.ds(pl.multiple_of(k * 2 * DOWN, 16), 2 * DOWN)] = joined.astype(BF16)
+        return carry
+
+    lax.fori_loop(0, 8, compact, 0)
+    for zz in range(4):
+        ffn_y_step(1, zz)
+    ffn_z_step(2, 1)
+    ffn_z_step(2, 2)
+    arrive(dout.at[1 - x], S_COT)
+    arrive(normed2.at[1 - x], S_N2)
+    ffn_sib(1)
+    for zz in range(4):
+        ffn_y_step(2, zz)
+    ffn_sib(2)
+
+    def ffn_w(ref, half, sl):
+        return ref[:, :, :, half, :, sl].reshape(512, sl.size)
+
+    for first, width in CHUNKS:
+        sl = pl.ds(first, width)
+
+        def hidden(m, carry, sl=sl):
+            n2 = normed2[m]
+            gate = nn(n2[:, 0:512], ffn_w(gate_w, 0, sl)) + nn(n2[:, 512:1024], ffn_w(gate_w, 1, sl))
+            upper = nn(n2[:, 0:512], ffn_w(up_w, 0, sl)) + nn(n2[:, 512:1024], ffn_w(up_w, 1, sl))
+            dmix = nt(dout[m], down_c[sl])
+            sig = jax.nn.sigmoid(gate)
+            silu = gate * sig
+            rows = pl.ds(pl.multiple_of(m * ROWS, ROWS), ROWS)
+            mixed[rows, sl] = (silu * upper).astype(BF16)
+            dgate[rows, sl] = (dmix * upper * sig * (1.0 + gate * (1.0 - sig))).astype(BF16)
+            dup[rows, sl] = (dmix * silu).astype(BF16)
+            return carry
+
+        lax.fori_loop(0, 2, hidden, 0)
+
+    grads = (down_w, gate_w, up_w)
+    s_bufs, y_bufs, z_bufs = (s_d, s_g, s_u), (y_d, y_g, y_u), (z_d, z_g, z_u)
+
+    def add(dst, src):
+        dst[...] = dst[...] + src[...]
+
+    def rs_sib_send(t):
+        for k, yy in enumerate((1 - y, y)):
+            send("rs%d" % t, grads[t].at[1 - c, :, yy], s_bufs[t].at[yy], S_RS[t] + yy, sib)
+
+    def rs_sib_recv(t, yy):
+        arrive(s_bufs[t].at[yy], S_RS[t] + yy)
+
+        def one(zz, carry):
+            add(grads[t].at[c, zz, yy], s_bufs[t].at[yy, zz])
+            return carry
+
+        lax.fori_loop(0, 4, one, 0)
+
+    def rs_y_send(t):
+        for zz in (3, 0, 2, 1):
+            send("rs%d" % t, grads[t].at[c, zz, 1 - y], y_bufs[t].at[zz], S_RY[t] + zz, yp)
+
+    def rs_y_recv(t):
+        for zz in (3, 0, 2, 1):
+            arrive(y_bufs[t].at[zz], S_RY[t] + zz)
+            add(grads[t].at[c, zz, y], y_bufs[t].at[zz])
+
+    end = (z == 0) | (z == 3)
+    inner = (z == 1) | (z == 2)
+    lower = z < 2
+
+    def real(m):
+        return jnp.where(lower, m, 3 - m)
+
+    far = (dp, jnp.where(lower, z + 1, z - 1) * 2 + y)
+    near = (dp, jnp.where(lower, z - 1, z + 1) * 2 + y)
+    far_way = jnp.where(lower, 0, 4)
+    near_way = jnp.where(lower, 4, 0)
+
+    def slot_at(way, dest, receiver):
+        return jnp.where((way == 4) & (dest == receiver), 4, dest)
+
+    def chain_send(group, blk, buf, base, m, to_far, cond):
+        d = real(m)
+        way = far_way if to_far else near_way
+        receiver = jnp.where(lower == to_far, z + 1, z - 1)
+        send(group, blk(d), buf(slot_at(way, d, receiver)), base + way + d, far if to_far else near, cond)
+
+    def chain_take(blk, buf, base, m, from_far):
+        d = real(m)
+        way = near_way if from_far else far_way
+        src = buf(slot_at(way, d, z))
+        arrive(src, base + way + d)
+        add(blk(d), src)
+
+    def chain_start(group, blk, buf, base):
+        for m in (3, 2, 1):
+            chain_send(group, blk, buf, base, m, True, end)
+
+    def chain_pass(group, blk, buf, base):
+        for m in (3, 2):
+            pl.when(inner)(lambda m=m: chain_take(blk, buf, base, m, False))
+            chain_send(group, blk, buf, base, m, True, inner)
+
+    def chain_back(group, blk, buf, base):
+        pl.when(inner)(lambda: chain_take(blk, buf, base, 0, True))
+        chain_send(group, blk, buf, base, 0, False, inner)
+
+    def chain_end(blk, buf, base):
+        pl.when(inner)(lambda: chain_take(blk, buf, base, 1, False))
+        pl.when(inner)(lambda: chain_take(blk, buf, base, 1, True))
+        pl.when(end)(lambda: chain_take(blk, buf, base, 0, True))
+
+    def rs_chain(t):
+        return ("rs%d" % t, lambda d: grads[t].at[c, d, y], lambda k: z_bufs[t].at[k], S_RZ[t])
+
+    def dn_half(it, carry):
+        m = jnp.where(it == 0, 1 - x, x)
+        rows = pl.ds(pl.multiple_of(m * ROWS, ROWS), ROWS)
+        for half in range(2):
+            full = pl.ds(0, HALF)
+            tmp[pl.ds(0, ROWS), pl.ds(half * 512, 512)] = nt(dgate[rows], ffn_w(gate_w, half, full)) + nt(
+                dup[rows], ffn_w(up_w, half, full)
+            )
+
+        @pl.when(it == 0)
+        def _():
+            snd_dn2[...] = tmp[0:ROWS].astype(BF16)
+            copy(snd_dn2, rcv_dn2, S_DN2, xp).start()
+
+        return carry
+
+    lax.fori_loop(0, 2, dn_half, 0)
+    sends["dn2"] = [(True, lambda: copy(snd_dn2, rcv_dn2, S_DN2, xp).wait_send())]
+
+    drain("ffn0")
+
+    def grad_down(it, carry):
+        cc = jnp.where(it == 0, 1 - c, c)
+        wide = pl.ds(pl.multiple_of(cc * 640, 128), 768)
+        mt = mixed[:, wide].T
+        tmp[pl.ds(ROWS, 768)] = nn(mt[:, 0:256], dout[0]) + nn(mt[:, 256:512], dout[1])
+
+        def split(k, inner_carry):
+            rows = tmp[pl.ds(pl.multiple_of(ROWS + cc * 64 + k * DOWN, 8), DOWN)]
+            down_w[cc, lax.div(k, 2), lax.rem(k, 2)] = jnp.concatenate(
+                [rows, jnp.zeros((PAD - DOWN, WIDTH), F32)], axis=0
+            ).astype(BF16)
+            return inner_carry
+
+        lax.fori_loop(0, 8, split, 0)
+        return carry
+
+    lax.fori_loop(0, 2, grad_down, 0)
+    rs_sib_send(0)
+
+    drain("ffn1")
+    drain("ffn2")
+
+    def grad_gate_up(it, carry):
+        cc = jnp.where(it < 2, 1 - c, c)
+        half = lax.rem(it, 2)
+        sl = pl.ds(pl.multiple_of(half * 512 + cc * 256, 256), 256)
+        for src, dst in ((dgate, gate_w), (dup, up_w)):
+            g = nn(normed2[0, :, sl].T, src[pl.ds(0, ROWS)]) + nn(normed2[1, :, sl].T, src[pl.ds(ROWS, ROWS)])
+            dst[cc, :, :, half] = g.astype(BF16).reshape(4, 2, 32, HALF)
+        return carry
+
+    lax.fori_loop(0, 4, grad_gate_up, 0)
+    rs_sib_send(1)
+    rs_sib_send(2)
+
+    rs_sib_recv(0, 1 - y)
+    rs_y_send(0)
+    rs_sib_recv(0, y)
+
+    def out_half(it, carry):
+        m = jnp.where(it == 0, 1 - x, x)
+        rows = pl.ds(pl.multiple_of(m * ROWS, ROWS), ROWS)
+        part = nn(mixed[rows], down_c[...])
+        tmp[pl.ds(ROWS, ROWS)] = part
+
+        @pl.when(it == 0)
+        def _():
+            snd_out[...] = tmp[pl.ds(ROWS, ROWS)].astype(BF16)
+            copy(snd_out, rcv_out, S_OUT, xp).start()
+
+        return carry
+
+    lax.fori_loop(0, 2, out_half, 0)
+    sends["out"] = [(True, lambda: copy(snd_out, rcv_out, S_OUT, xp).wait_send())]
+
+    for t in (1, 2):
+        rs_sib_recv(t, 1 - y)
+        rs_y_send(t)
+        rs_sib_recv(t, y)
+
+    sum_own[...] = jnp.zeros((8, WIDTH), F32)
+    arrive(rcv_dn2, S_DN2)
+
+    def back_two(k, carry):
+        rows = pl.ds(pl.multiple_of(k * 32, 32), 32)
+        mid = middle[rows]
+        r2 = lax.rsqrt(jnp.mean(mid * mid, axis=1, keepdims=True) + EPSILON)
+        grad = tmp[rows] + rcv_dn2[rows].astype(F32)
+        sum_own[1:2] = sum_own[1:2] + jnp.sum(grad * mid * r2, axis=0, keepdims=True)
+        s = grad * gain_full[1:2, :]
+        res = dout[x, rows].astype(F32) + r2 * (s - mid * r2 * r2 * jnp.mean(s * mid, axis=1, keepdims=True))
+        dmid[rows] = res
+        dmid_low[rows] = res.astype(BF16)
+        return carry
+
+    lax.fori_loop(0, 8, back_two, 0)
+
+    def dmerged_cols(k, carry):
+        w = attn[1, lax.div(k, 2), lax.rem(k, 2)].reshape(256, WIDTH)
+        dmerged[:, cols(k)] = nt(dmid_low[...], w).astype(BF16)
+        return carry
+
+    lax.fori_loop(0, 4, dmerged_cols, 0)
+
+    def grad_output(it, carry):
+        cc = jnp.where(it < 2, 1 - c, c)
+        half = lax.rem(it, 2)
+        g = nn(merged[:, cols(half * 2 + cc)].T, dmid_low[...])
+        pattn[0, half, cc] = g.astype(BF16).reshape(4, 2, 32, WIDTH)
+        return carry
+
+    lax.fori_loop(0, 4, grad_output, 0)
+
+    parts = (pl.ds(0, 1), pl.ds(1, 2))
+
+    def at_sib_send(p):
+        for xx in (1 - x, x):
+            send("at", pattn.at[parts[p], xx, 1 - c], s_a.at[parts[p], xx], S_BS[p] + xx, sib)
+
+    def at_sib_recv(p, xx):
+        arrive(s_a.at[parts[p], xx], S_BS[p] + xx)
+
+        def one(zz, carry):
+            add(pattn.at[parts[p], xx, c, zz], s_a.at[parts[p], xx, zz])
+            return carry
+
+        lax.fori_loop(0, 4, one, 0)
+
+    def at_x_send(p):
+        for zz in (3, 0, 2, 1):
+            send("at", pattn.at[parts[p], 1 - x, c, zz], x_a.at[parts[p], zz], S_BX[p] + zz, xp)
+
+    def at_x_recv(p):
+        for zz in (3, 0, 2, 1):
+            arrive(x_a.at[parts[p], zz], S_BX[p] + zz)
+            add(pattn.at[parts[p], x, c, zz], x_a.at[parts[p], zz])
+
+    def at_chain(p):
+        return ("at", lambda d: pattn.at[parts[p], x, c, d], lambda k: z_a.at[parts[p], k], S_BZ[p])
+
+    def at_y_send(p):
+        send("at", pattn.at[parts[p], x, c, z, 1 - y], y_a.at[parts[p]], S_BY[p], yp)
+
+    def at_y_recv(p):
+        arrive(y_a.at[parts[p]], S_BY[p])
+        add(pattn.at[parts[p], x, c, z, y], y_a.at[parts[p]])
+
+    at_sib_send(0)
+
+    rs_y_recv(0)
+    chain_start(*rs_chain(0))
+    at_sib_recv(0, 1 - x)
+    at_x_send(0)
+    at_sib_recv(0, x)
+    chain_pass(*rs_chain(0))
+
+    drain("dn2")
+    drain("out")
+
+    def attend_back(j, carry):
+        pair = cols(j, 128)
+        q_pair, k_pair, v_pair, do_pair = query[:, pair], keys[:, pair], values[:, pair], dmerged[:, pair]
+        dq, dk, dv = [], [], []
+        for h, (q, do) in enumerate(zip(halves(q_pair), halves(do_pair))):
+            logsum = jnp.sum(jnp.where(head_lane == j * 2 + h, lse[...], 0.0), axis=1, keepdims=True)
+            probs = jnp.exp(nt(q, k_pair) * SCALE + bias[...] - logsum)
+            dv.append(tn(probs.astype(BF16), do_pair))
+            dprobs = nt(do, v_pair)
+            row_sum = jnp.sum(probs * dprobs, axis=1, keepdims=True)
+            dscores = (probs * (dprobs - row_sum)).astype(BF16)
+            dq.append(nn(dscores, k_pair))
+            dk.append(tn(dscores, q_pair))
+        dquery[:, pair] = (jnp.where(low_half, dq[0], dq[1]) * SCALE).astype(BF16)
+        dkeys[:, pair] = (jnp.where(low_half, dk[0], dk[1]) * SCALE).astype(BF16)
+        dvalues[:, pair] = jnp.where(low_half, dv[0], dv[1]).astype(BF16)
+        return carry
+
+    lax.fori_loop(0, 4, attend_back, 0)
+    rs_y_recv(1)
+    chain_start(*rs_chain(1))
+    chain_back(*rs_chain(0))
+    lax.fori_loop(4, 8, attend_back, 0)
+    chain_pass(*rs_chain(1))
+
+    def latent_back(g, carry):
+        dk, dv = dkeys[:, cols(g, 512)], dvalues[:, cols(g, 512)]
+        dlatent[:, cols(g)] = (nt(dk, up_weight(g, 0)) + nt(dv, up_weight(g, 16))).astype(BF16)
+        lat = latent[:, cols(g)].T
+        pattn[2, g, :, :, :, pl.ds(0, 16), pl.ds(512, 512)] = nn(lat, dk).astype(BF16).reshape(2, 4, 2, 16, 512)
+        pattn[2, g, :, :, :, pl.ds(16, 16), pl.ds(512, 512)] = nn(lat, dv).astype(BF16).reshape(2, 4, 2, 16, 512)
+        return carry
+
+    lax.fori_loop(0, GROUPS, latent_back, 0)
+
+    def grad_proj(it, carry):
+        cc = jnp.where(it < 2, 1 - c, c)
+        half = lax.rem(it, 2)
+        nt_ = normed[:, cols(half * 2 + cc)].T
+        pattn[1, half, cc] = nn(nt_, dquery[...]).astype(BF16).reshape(4, 2, 32, WIDTH)
+        pattn[2, half, cc, :, :, :, pl.ds(0, 512)] = nn(nt_, dlatent[...]).astype(BF16).reshape(4, 2, 32, 512)
+        return carry
+
+    lax.fori_loop(0, 4, grad_proj, 0)
+    at_sib_send(1)
+    at_sib_recv(1, 1 - x)
+    at_x_send(1)
+    at_sib_recv(1, x)
+
+    rs_y_recv(2)
+    chain_start(*rs_chain(2))
+    at_x_recv(0)
+    chain_start(*at_chain(0))
+
+    def dnormed_cols(k, carry):
+        xx, cc = lax.div(k, 2), lax.rem(k, 2)
+        part = nt(dquery[...], attn[0, xx, cc].reshape(256, WIDTH))
+        part = part + nt(dlatent[...], attn[2, xx, cc, :, :, :, pl.ds(0, 512)].reshape(256, 512))
+        tmp[pl.ds(0, ROWS), cols(k)] = part
+        return carry
+
+    lax.fori_loop(0, 4, dnormed_cols, 0)
+
+    def back_one(k, carry):
+        rows = pl.ds(pl.multiple_of(k * 32, 32), 32)
+        val = tok[rows].astype(F32)
+        r1 = lax.rsqrt(jnp.mean(val * val, axis=1, keepdims=True) + EPSILON)
+        grad = tmp[rows]
+        sum_own[0:1] = sum_own[0:1] + jnp.sum(grad * val * r1, axis=0, keepdims=True)
+        s = grad * gain_full[0:1, :]
+        gtok_ref[rows] = dmid[rows] + r1 * (s - val * r1 * r1 * jnp.mean(s * val, axis=1, keepdims=True))
+        return carry
+
+    lax.fori_loop(0, 8, back_one, 0)
+
+    sum_to = (sib, yp, xp, z_one, z_two)
+
+    def sum_send(i):
+        send("sum%d" % i, sum_own, sum_rcv.at[i], S_SUM + i, sum_to[i])
+
+    def sum_recv(i):
+        drain("sum%d" % i)
+        arrive(sum_rcv.at[i], S_SUM + i)
+        sum_own[...] = sum_own[...] + sum_rcv[i]
+
+    sum_send(0)
+    arrive(rcv_out, S_OUT)
+
+    def out_rows(k, carry):
+        rows = pl.ds(pl.multiple_of(k * 32, 32), 32)
+        part = tmp[pl.ds(pl.multiple_of(ROWS + k * 32, 32), 32)]
+        out_ref[rows] = (middle[rows] + (part + rcv_out[rows].astype(F32))).astype(BF16)
+        return carry
+
+    lax.fori_loop(0, 8, out_rows, 0)
+    sum_recv(0)
+    sum_send(1)
+
+    chain_end(*rs_chain(0)[1:])
+    gd_ref[...] = down_w[c, z, y].astype(F32)[0:DOWN]
+    chain_back(*rs_chain(1))
+    sum_recv(1)
+    sum_send(2)
+    chain_pass(*rs_chain(2))
+    chain_pass(*at_chain(0))
+    chain_end(*rs_chain(1)[1:])
+    send("rx", gate_w.at[c, z, y, 1 - x], x_g, S_RX, xp)
+    sum_recv(2)
+    sum_send(3)
+    chain_back(*rs_chain(2))
+    chain_back(*at_chain(0))
+    at_x_recv(1)
+    chain_start(*at_chain(1))
+    sum_recv(3)
+    sum_send(4)
+    chain_end(*rs_chain(2)[1:])
+    send("rx", up_w.at[c, z, y, 1 - x], x_u, S_RX + 1, xp)
+    chain_pass(*at_chain(1))
+    chain_end(*at_chain(0)[1:])
+    at_y_send(0)
+    chain_back(*at_chain(1))
+    sum_recv(4)
+    own_cols = pl.ds(pl.multiple_of(x * HALF, 128), HALF)
+    for w, ref, buf, k in ((gate_w, gg_ref, x_g, 0), (up_w, gu_ref, x_u, 1)):
+        ref[:, own_cols] = w[c, z, y, x].astype(F32)
+        arrive(buf, S_RX + k)
+        ref[:, other_cols] = buf[...].astype(F32)
+    gain_out[...] = sum_own[:, pl.ds(pl.multiple_of((dp * 2 + lax.div(fs, 4)) * 128, 128), 128)]
+    at_y_recv(0)
+    go_ref[...] = pattn[0, x, c, z, y].astype(F32)
+    chain_end(*at_chain(1)[1:])
+    at_y_send(1)
+    at_y_recv(1)
+    gq_ref[...] = pattn[1, x, c, z, y].astype(F32)
+    last = pattn.at[2, x, c, z, y]
+    gl_ref[...] = last[:, 0:512].astype(F32)
+    gk_ref[...] = last[0:16, 512:1024].astype(F32)
+    gv_ref[...] = last[16:32, 512:1024].astype(F32)
+    for group in list(sends):
+        drain(group)
+
+
+def kernel_on_device(
+    tokens, seq_lengths, cotangent, w_query, w_latent, w_keyup, w_valup, w_output, norm_attn, norm_ffn,
+    w_gate, w_up, w_down,
+):
+    gain_rows = jnp.concatenate(
+        [jnp.tile(norm_attn, 4)[None], jnp.tile(norm_ffn, 4)[None], jnp.zeros((14, 128), BF16)], axis=0
+    )
+    hbm, vmem = pl.BlockSpec(memory_space=pl.ANY), pl.BlockSpec(memory_space=pltpu.VMEM)
+    smem = pl.BlockSpec(memory_space=pltpu.SMEM)
+    shape = jax.ShapeDtypeStruct
+    outs = [
+        shape((ROWS, WIDTH), BF16), shape((ROWS, WIDTH), F32), shape((32, WIDTH), F32), shape((32, 512), F32),
+        shape((16, 512), F32), shape((16, 512), F32), shape((32, WIDTH), F32), shape((8, 128), F32),
+        shape((32, 2 * HALF), F32), shape((32, 2 * HALF), F32), shape((DOWN, WIDTH), F32),
+    ]
+    V = pltpu.VMEM
+    act = V((ROWS, WIDTH), BF16)
+    scratch = [
+        V((3, 2, 2, 4, 2, 32, WIDTH), BF16), V((2, 4, 2, 2, 32, HALF), BF16), V((2, 4, 2, 2, 32, HALF), BF16),
+        V((2, 4, 2, PAD, WIDTH), BF16), V((HALF, WIDTH), BF16), V((2, 2, 4, 2, 16, 128), BF16), V((16, WIDTH), F32),
+        act, V((ROWS, ROWS), F32), act, act, V((ROWS, 512), BF16), act, act, act, V((ROWS, 128), F32),
+        V((ROWS, WIDTH), F32), V((2, ROWS, WIDTH), BF16), V((2, ROWS, WIDTH), BF16),
+        V((512, HALF), BF16), V((512, HALF), BF16), V((512, HALF), BF16), V((ROWS + 768, WIDTH), F32),
+        act,
+        act, act, act, act, act, V((ROWS, 512), BF16),
+        V((3, 2, 2, 4, 2, 32, WIDTH), BF16),
+        V((2, 4, PAD, WIDTH), BF16), V((2, 4, 2, 32, HALF), BF16), V((2, 4, 2, 32, HALF), BF16),
+        V((4, PAD, WIDTH), BF16), V((4, 2, 32, HALF), BF16), V((4, 2, 32, HALF), BF16),
+        V((5, PAD, WIDTH), BF16), V((5, 2, 32, HALF), BF16), V((5, 2, 32, HALF), BF16),
+        V((32, HALF), BF16), V((32, HALF), BF16),
+        V((3, 2, 4, 2, 32, WIDTH), BF16), V((3, 4, 2, 32, WIDTH), BF16), V((3, 5, 2, 32, WIDTH), BF16),
+        V((3, 32, WIDTH), BF16), V((8, WIDTH), F32), V((5, 8, WIDTH), F32),
+        pltpu.SemaphoreType.DMA((SLOTS.count,)), pltpu.SemaphoreType.DMA((SLOTS.count,)), pltpu.SemaphoreType.DMA((9,)),
+    ]
+    res = pl.pallas_call(
+        layer_kernel,
+        out_shape=outs,
+        in_specs=[hbm, smem, hbm, hbm, hbm, hbm, hbm, hbm, vmem, hbm, hbm, vmem],
+        out_specs=[vmem] * len(outs),
+        scratch_shapes=scratch,
+        compiler_params=pltpu.CompilerParams(
+            collective_id=0, has_side_effects=True, vmem_limit_bytes=63 * 2**20
+        ),
+    )(tokens, seq_lengths, cotangent, w_query, w_latent, w_keyup, w_valup, w_output, gain_rows, w_gate, w_up, w_down)
+    out, gtok, gq, gl, gk, gv, go, gain, gg, gu, gd = res
+    first = lax.rem(lax.axis_index("fsdp"), 4) * 32
+    own = lax.dynamic_slice(gain, (0, first), (2, 32))
+    return (out, gtok, gq, gl, gk, gv, go, own[0], own[1], gg, gu, gd)
+
+
 def solution(mesh):
+    fits = dict(mesh.shape) == {"dp": 4, "fsdp": 8}
     return jax.shard_map(
-        on_device,
+        kernel_on_device if fits else on_device,
         mesh=mesh,
         in_specs=(
             P(("dp", "fsdp"), None),

time: 1320 us -> 224 us (0.17)
  waiting for transfers between devices: 828 us -> 0 us
  blocking collectives: 219 us -> 0 us
  matrix products: 218 us -> 0 us
  Pallas kernels: 0 us -> 211 us
  other arithmetic: 17.2 us -> 0.67 us
  between operations: 14.2 us -> 0.71 us
    reduce_scatter x5 -> x0, waiting for transfers between devices: 688 us -> none  [the longest x1 248 us: on_device(): lax.psum_scatter(column_term(normed_two, packed_ffn), ('dp', 'fsdp'), sca...]
    dot_general x133 -> x0, matrix products: 218 us -> none  [the longest x37 74.4 us: matmul_left(): lax.dot_general(left, right, (((0,), (0,)), ((), ())), preferred_element_...]
    pallas_call x0 -> x1, Pallas kernels: none -> 211 us  [kernel_on_device(): pl.pallas_call(layer_kernel, out_shape=outs, in_specs=[hbm, smem, hbm, hb...]
    all_gather x2 -> x0, blocking collectives: 137 us -> none  [the longest x1 69.7 us: on_device(): lax.all_gather(w_keyup, ('dp', 'fsdp'), axis=0, tiled=True)]
    all_gather x6 -> x0, waiting for transfers between devices: 136 us -> none  [the longest x1 63.1 us: on_device(): lax.all_gather(w_down, ('dp', 'fsdp'), axis=0, tiled=True)]
    unnamed x2 -> x0, blocking collectives: 82.1 us -> none
  transfers between devices with their start and end apart: 11 -> 0, of which waited for: 8 -> 0; matrix products, arithmetic and copies ran while one was open for 8% -> 0% of each run, Pallas kernels for 0% -> 0%
where the time goes in v2:
time: 224 us
  Pallas kernels  211 us (94%)
  local copies, waits for them, and re-layouts  11.8 us (5%)
    pallas_call x1, Pallas kernels, kernel_on_device(): pl.pallas_call(layer_kernel, out_shape=outs, in_specs=[hbm, smem, hbm, hb...  211 us
    unnamed x32, local copies, waits for them, and re-layouts  10.1 us

profile of v2, /device:TPU:0, one launch (start us, length us, event | category | flops | bytes accessed | tf_op | source)
XLA Modules:
  0.0 223.9 jit_solution(5453945483877636330)
XLA Ops:
  0.7 0.0 copy-start.9
  0.7 0.1 pad.2.clone
  0.8 0.6 copy-done.9
  1.3 0.0 copy-start.10
  1.3 0.1 broadcast_in_dim_tile.6
  1.4 0.6 copy-done.10
  2.0 0.1 broadcast_in_dim_tile.7
  2.1 0.7 maximum_maximum_fusion.gain_ref
  2.7 210.7 %shard_map.220 = (bf16[256,1024]{1,0:T(8,128)(2,1)}, f32[256,1024]{1,0:T(8,128)}, f32[32,1024]{1,0:T(8,128)}, f32[32,512]{1,0:T(8,128)}, f32[16,512]{1,0:T(8,128...) custom-call(bf16[256,1024]{1,0:T(8,128)(2,1)} %tok_hbm.1, ...), custom_call_target="tpu_custom_call" | custom-call | tf_op jit(solution)/shard_map/pallas_call | solution.py:1127
  213.5 0.0 copy-start
  213.5 0.8 constant_dynamic-slice_fusion
  214.3 0.5 slice_bitcast_fusion
  214.9 1.9 copy.35
  216.7 0.0 copy-done
  216.7 0.0 copy-start.7
  216.8 1.0 copy.36
  217.7 0.0 copy-done.5
  217.7 0.7 copy.37
  218.4 0.0 copy-done.6
  218.4 0.6 copy.38
  219.0 0.0 copy-done.8
  219.0 0.6 copy.39
  219.6 0.0 copy-done.7
  219.6 0.6 copy.40
  220.3 0.0 copy-done.4
  220.3 0.7 copy.41
  220.9 0.0 copy-done.3
  220.9 0.7 copy.42
  221.7 0.4 copy-done.2
  222.0 0.7 copy.43
  222.8 0.4 copy-done.1
  223.2 0.7 copy.44
  (10 shorter events, 0.0 us)
Async XLA Ops:
  0.7 0.7 copy-start.9
  1.3 0.7 copy-start.10
  213.5 3.2 %copy-start = (f32[256,1024]{1,0:T(8,128)S(1)}, f32[256,1024]{1,0:T(8,128)}, u32[]{:S(2)}) copy-start(f32[256,1024]{1,0:T(8,128)} %get-tuple-element.49) | copy-start | bytes 3145732
  216.7 1.0 copy-start.5
  216.7 1.7 copy-start.6
  216.7 2.3 %copy-start.8 = (f32[16,512]{1,0:T(8,128)S(1)}, f32[16,512]{1,0:T(8,128)}, u32[]{:S(2)}) copy-start(f32[16,512]{1,0:T(8,128)} %get-tuple-element.52) | copy-start | bytes 98308
  216.7 2.9 %copy-start.7 = (f32[16,512]{1,0:T(8,128)S(1)}, f32[16,512]{1,0:T(8,128)}, u32[]{:S(2)}) copy-start(f32[16,512]{1,0:T(8,128)} %get-tuple-element.53) | copy-start | bytes 98308
  217.7 3.2 %copy-start.3 = (f32[32,2816]{1,0:T(8,128)S(1)}, f32[32,2816]{1,0:T(8,128)}, u32[]{:S(2)}) copy-start(f32[32,2816]{1,0:T(8,128)} %get-tuple-element.57) | copy-start | bytes 1081348
  218.4 1.9 copy-start.4
  220.9 1.1 copy-start.2
  222.0 1.1 copy-start.1

commit v3 on v1

--- a/solution.py
+++ b/solution.py
@@ -1,6 +1,8 @@
 import jax
 import jax.numpy as jnp
 from jax import lax
+from jax.experimental import pallas as pl
+from jax.experimental.pallas import tpu as pltpu
 from jax.sharding import PartitionSpec as P
 
 HEADS = 16
@@ -279,9 +281,1130 @@
     )
 
 
+MESH = pl.DeviceIdType.MESH
+F32 = jnp.float32
+BF16 = jnp.bfloat16
+SCALE = HEAD_DIM ** (-0.5)
+ROWS = 256
+WIDTH = 1024
+HALF = 1408
+PARTS = (768, 640)
+FFN = 1 + 2 * len(PARTS)
+PUT = 20
+DOWN = 88
+
+
+ROUTE = ("y21xs", "y21xs", "21xys", "21yxs")
+SUM_X_FIRST = (True, False, True, True)
+
+
+class Slots:
+    def __init__(self):
+        self.count = 0
+
+    def take(self, number):
+        first = self.count
+        self.count += number
+        return first
+
+
+SLOTS = Slots()
+S_A = [SLOTS.take(32) for _ in range(4)]
+S_HALF = SLOTS.take(FFN)
+S_F = [SLOTS.take(16) for _ in range(FFN)]
+S_COT, S_TOK, S_DN2, S_OUT, S_END = (SLOTS.take(n) for n in (4, 4, 1, 4, 1))
+S_R = [SLOTS.take(10) for _ in range(FFN + 4)]
+S_SUM = SLOTS.take(5)
+
+
+def nn(left, right):
+    return jnp.dot(left, right, preferred_element_type=F32)
+
+
+def nt(left, right):
+    return lax.dot_general(left, right, (((1,), (1,)), ((), ())), preferred_element_type=F32)
+
+
+def tn(left, right):
+    return lax.dot_general(left, right, (((0,), (0,)), ((), ())), preferred_element_type=F32)
+
+
+(
+    AA, AG, AT, H_S, H_R, FA, FG, FT, COT_S, COT_R, TOK_S, TOK_R, END_S, END_R, DN2_S, DN2_R, OUT_S,
+    OUT_R, R_GO, R_S, R_B, R_A, R_1, R_2, R_L, R_E, SUM_S, SUM_R,
+) = range(28)
+(
+    G_START, G_WEIGHTS, G_ACROSS, G_DOWN_W, G_QUERY, G_OUTPUT_W, G_FFN_A, G_FFN_B, G_BACK, G_RESULT,
+    G_TAIL, G_MASK, G_NORM, G_LATENT, G_KEYS, G_NORM_P, G_LATENT_P, G_KEYS_P, G_COMPACT, G_ATTEND,
+    G_QUERY_P, G_ATTEND_P, G_MIDDLE, G_NORM2, G_MIDDLE_P, G_NORM2_P, G_HIDDEN_A, G_DN_A, G_GATEUP_A,
+    G_DN_B, G_HIDDEN_B, G_DOWN, G_GATEUP_B, G_OUT, G_OUTPUT, G_ATTENDB, G_PROJQ, G_PROJL, G_DNORMED,
+    G_NORM1B, G_GAIN, G_NORM2B, G_DMERGED, G_LATENTB,
+) = range(44)
+PLAN = {
+    G_START: (
+        (H_S, 2), (AA, 2, 0), (AG, 2, 0, 1), (H_S, 1), (H_S, 4), (H_S, 3), (FA, 0, 0), (AA, 0, 0),
+    ),
+    (G_MASK, 3): (
+        (TOK_S, 2), (AA, 1, 0), (FG, 0, 0, 0), (FG, 0, 0, 1),
+    ),
+    G_WEIGHTS: (
+        (AG, 1, 0, 0), (AG, 0, 0, 1), (H_R, 4), (AG, 0, 0, 2), (TOK_S, 1), (TOK_S, 0), (AA, 3, 0),
+        (FA, 4, 0), (AG, 0, 0, 0), (AA, 0, 1), (AG, 2, 0, 0), (AA, 1, 1), (AG, 3, 0, 1), (H_R, 2),
+        (H_R, 1), (TOK_S, 3), (FG, 0, 0, 2), (AG, 0, 1, 1), (FA, 0, 1), (FG, 0, 1, 2), (AG, 0, 1, 2),
+        (FA, 0, 2), (H_R, 3), (AG, 3, 0, 0), (AG, 0, 1, 3), (AA, 2, 1), (FA, 1, 0), (AA, 0, 2),
+        (AG, 0, 2, 2), (AG, 0, 0, 3), (AG, 2, 1, 2), (AG, 2, 1, 1), (FG, 1, 0, 2), (AA, 0, 3),
+        (FA, 2, 0), (AA, 3, 2), (AG, 1, 0, 1), (AG, 1, 0, 3), (FG, 2, 0, 2), (AG, 2, 1, 3),
+        (AG, 0, 2, 3), (AG, 3, 0, 2), (AA, 0, 4), (AG, 1, 0, 2), (AA, 2, 5), (FG, 4, 0, 2),
+        (AG, 0, 3, 2), (AA, 2, 2), (FA, 3, 0), (AG, 0, 3, 3), (AG, 1, 1, 1), (FA, 2, 4),
+        (FG, 0, 1, 1), (AG, 2, 5, 3), (AA, 1, 8), (FG, 1, 0, 0), (AA, 3, 1), (AA, 0, 8), (AA, 2, 3),
+        (AG, 2, 0, 2), (AG, 0, 4, 3), (FA, 0, 5), (AG, 1, 1, 2), (FG, 0, 2, 2), (AA, 0, 6),
+        (AA, 0, 5), (AG, 3, 1, 2), (AG, 0, 6, 3), (AA, 0, 7), (FA, 0, 4), (AA, 0, 11), (AG, 0, 5, 3),
+        (AG, 2, 3, 2), (AA, 0, 9), (AA, 3, 4), (AA, 1, 2), (AG, 3, 2, 2), (FA, 1, 4), (AA, 1, 3),
+        (AG, 3, 1, 1), (AG, 0, 7, 3), (AA, 0, 13), (AG, 2, 2, 3), (AG, 1, 1, 3), (AA, 1, 4),
+        (AA, 2, 9), (AA, 2, 4), (AG, 1, 2, 3), (AG, 1, 2, 2), (AG, 2, 2, 2), (AA, 2, 7), (AA, 2, 13),
+        (END_S,), (AA, 0, 10), (FA, 0, 3), (FG, 0, 3, 2), (AA, 0, 12), (AG, 1, 3, 2), (FA, 4, 4),
+        (AA, 0, 15), (FG, 2, 0, 0), (AA, 0, 14), (AG, 1, 3, 3), (TOK_R,), (AT, 0), (FG, 3, 0, 2),
+        (AA, 2, 10), (AA, 1, 5), (FA, 1, 1), (AG, 1, 4, 3), (FG, 1, 0, 1),
+    ),
+    (G_NORM, 3): (
+        (AA, 3, 3), (AA, 3, 5), (AG, 2, 3, 3), (AG, 2, 4, 3),
+    ),
+    (G_LATENT, 1): (
+        (FG, 4, 0, 0), (AA, 1, 6), (AG, 1, 5, 3), (AA, 3, 6),
+    ),
+    (G_KEYS, 1): (
+        (AG, 3, 3, 2), (FA, 0, 6), (AG, 2, 7, 3),
+    ),
+    G_ACROSS: (
+        (AA, 2, 6), (FA, 0, 7), (AA, 1, 7), (AG, 1, 6, 3), (FG, 2, 0, 1), (FG, 1, 1, 1),
+        (FG, 1, 1, 2), (END_R,), (AA, 1, 9),
+    ),
+    (G_NORM_P, 3): (
+        (AG, 1, 7, 3), (FT, 0),
+    ),
+    (G_LATENT_P, 1): (
+        (AA, 1, 12), (AA, 3, 7), (AG, 2, 0, 3), (AG, 3, 0, 3),
+    ),
+    (G_KEYS_P, 1): (
+        (AG, 3, 5, 3), (FA, 2, 1), (AA, 1, 14),
+    ),
+    G_DOWN_W: (
+        (AA, 1, 11), (AG, 3, 4, 3), (AG, 3, 3, 3), (FG, 3, 0, 0), (FG, 2, 1, 2), (FG, 2, 1, 1),
+        (AA, 1, 13), (AG, 2, 6, 3),
+    ),
+    (G_COMPACT, 7): (
+        (FG, 3, 0, 1), (AG, 3, 7, 3),
+    ),
+    G_QUERY: (
+        (AG, 3, 6, 3), (AA, 1, 15), (AA, 1, 10), (FA, 1, 5), (AG, 3, 2, 3), (FA, 1, 2),
+        (FG, 1, 2, 2), (AG, 3, 1, 3), (AA, 2, 8), (COT_S, 2), (COT_S, 1), (AT, 1), (FA, 4, 1),
+        (AA, 2, 15), (AA, 2, 11),
+    ),
+    (G_QUERY, 3): (
+        (AA, 2, 12),
+    ),
+    (G_ATTEND, 3): (
+        (AA, 2, 14), (FG, 4, 1, 2), (AA, 3, 8), (AA, 3, 13),
+    ),
+    (G_ATTEND, 7): (
+        (FA, 1, 3), (FG, 1, 3, 2), (FG, 4, 0, 1), (AA, 3, 12), (AA, 3, 10), (FA, 2, 2),
+    ),
+    (G_QUERY_P, 3): (
+        (FA, 1, 6), (AT, 2), (FG, 4, 1, 1), (AA, 3, 14), (FA, 2, 5), (AA, 3, 15), (COT_S, 3),
+        (AA, 3, 11), (FG, 2, 2, 2), (FA, 3, 1), (AA, 3, 9), (FG, 3, 1, 1),
+    ),
+    (G_ATTEND_P, 3): (
+        (FA, 2, 3), (AT, 3), (FG, 2, 3, 2),
+    ),
+    G_OUTPUT_W: (
+        (COT_S, 0), (FA, 1, 7),
+    ),
+    (G_MIDDLE, 3): (
+        (FA, 3, 2), (FG, 3, 2, 2),
+    ),
+    (G_NORM2, 3): (
+        (FG, 3, 1, 2), (FA, 4, 5), (FA, 2, 6), (FA, 4, 2),
+    ),
+    (G_MIDDLE_P, 3): (
+        (FA, 2, 7), (FG, 4, 2, 2),
+    ),
+    (G_NORM2_P, 3): (
+        (FA, 3, 4), (FT, 1),
+    ),
+    G_FFN_A: (
+        (FT, 2),
+    ),
+    (G_HIDDEN_A, 0): (
+        (FA, 3, 3), (FA, 4, 3), (FG, 3, 3, 2), (COT_R,),
+    ),
+    (G_DN_A, 0): (
+        (FG, 4, 3, 2),
+    ),
+    (G_GATEUP_A, 1): (
+        (R_GO, 1), (FA, 3, 5),
+    ),
+    (G_GATEUP_A, 3): (
+        (FA, 4, 6), (FA, 3, 7), (FA, 3, 6), (R_S, 1, 1), (R_B, 1, 3),
+    ),
+    G_FFN_B: (
+        (R_B, 1, 1), (FA, 4, 7), (R_B, 1, 2), (R_S, 1, 0), (R_GO, 2), (FT, 3), (FT, 4),
+    ),
+    (G_DN_B, 1): (
+        (DN2_S,), (R_S, 2, 1),
+    ),
+    (G_HIDDEN_B, 0): (
+        (R_B, 2, 3),
+    ),
+    (G_DN_B, 0): (
+        (R_B, 2, 1), (R_A, 1, 3),
+    ),
+    (G_DOWN, 0): (
+        (R_GO, 0), (R_A, 1, 1), (R_S, 2, 0),
+    ),
+    (G_GATEUP_B, 1): (
+        (R_S, 0, 1), (R_GO, 3), (R_B, 0, 3), (R_A, 2, 3), (R_A, 1, 2), (R_GO, 4), (R_S, 0, 0),
+    ),
+    (G_GATEUP_B, 3): (
+        (R_S, 3, 1), (R_A, 2, 1),
+    ),
+    (G_OUT, 0): (
+        (R_B, 2, 2), (OUT_S, 1), (OUT_S, 2), (R_S, 4, 1), (R_1, 1, 1), (R_B, 3, 1), (R_S, 3, 0),
+    ),
+    (G_OUT, 1): (
+        (R_B, 3, 3), (R_B, 0, 2), (OUT_S, 0), (R_B, 4, 3), (R_A, 0, 3), (R_B, 1, 0),
+    ),
+    G_BACK: (
+        (DN2_R,),
+    ),
+    (G_OUTPUT, 1): (
+        (R_A, 2, 2), (R_1, 2, 1), (OUT_S, 3),
+    ),
+    (G_OUTPUT, 3): (
+        (R_GO, 5),
+    ),
+    (G_ATTENDB, 3): (
+        (R_A, 3, 1), (R_A, 3, 3),
+    ),
+    (G_PROJQ, 1): (
+        (R_S, 5, 1), (R_A, 0, 2),
+    ),
+    (G_PROJQ, 3): (
+        (R_B, 5, 1), (R_1, 0, 1), (R_S, 4, 0), (R_A, 4, 3), (R_B, 4, 1),
+    ),
+    (G_PROJL, 1): (
+        (R_B, 5, 3), (R_B, 4, 2), (R_S, 5, 0), (R_GO, 6), (R_B, 3, 2),
+    ),
+    (G_PROJL, 3): (
+        (R_GO, 7), (R_B, 2, 0), (OUT_R,), (R_A, 5, 1), (R_B, 5, 0),
+    ),
+    (G_DNORMED, 3): (
+        (R_S, 6, 1),
+    ),
+    (G_NORM1B, 7): (
+        (R_B, 4, 0), (R_B, 3, 0), (R_A, 4, 2), (R_A, 5, 3), (R_GO, 8), (R_S, 7, 1), (R_S, 8, 0),
+        (R_B, 6, 3), (R_A, 1, 0),
+    ),
+    G_RESULT: (
+        (R_1, 4, 1), (R_1, 1, 0), (R_A, 4, 1), (R_B, 5, 2), (R_B, 6, 2), (R_B, 7, 1), (R_A, 2, 0),
+    ),
+    (G_RESULT, 7): (
+        (R_A, 3, 2), (SUM_S, 0), (R_B, 0, 0), (SUM_R, 0), (R_1, 3, 1), (R_A, 3, 0), (R_A, 4, 0),
+        (R_S, 8, 1), (R_S, 7, 0), (R_A, 5, 0), (R_B, 8, 3), (R_A, 5, 2), (SUM_S, 1), (R_B, 7, 2),
+        (R_B, 8, 0), (R_1, 3, 0), (R_S, 6, 0), (R_2, 1), (R_A, 6, 3), (R_1, 2, 0), (R_B, 6, 1),
+        (R_B, 8, 1), (R_B, 7, 0), (R_1, 5, 1), (R_A, 8, 3), (R_1, 5, 0), (R_A, 8, 0), (R_A, 6, 2),
+        (R_B, 0, 1), (R_B, 6, 0), (R_B, 8, 2), (R_B, 7, 3), (R_A, 8, 1), (R_2, 2),
+    ),
+    G_TAIL: (
+        (R_1, 6, 1), (R_A, 7, 1), (R_2, 3), (R_A, 8, 2), (R_1, 8, 0), (SUM_R, 1), (R_1, 4, 0),
+        (R_A, 7, 3), (SUM_S, 2), (R_1, 8, 1), (R_A, 6, 1), (R_L, 3), (R_A, 6, 0), (R_A, 7, 2),
+        (R_2, 4), (SUM_R, 2), (SUM_S, 3), (R_L, 1), (R_1, 7, 1), (R_2, 8), (R_A, 7, 0), (R_2, 5),
+        (R_L, 4), (R_L, 5), (R_L, 8), (R_E, 3), (R_A, 0, 0), (R_A, 0, 1), (R_L, 2), (SUM_R, 3),
+        (R_1, 7, 0), (R_E, 1), (R_1, 6, 0), (SUM_S, 4), (R_2, 6), (R_E, 2), (R_L, 6), (R_2, 7),
+        (R_L, 7), (R_1, 0, 0), (R_E, 4), (R_E, 5), (R_E, 8), (R_2, 0), (R_E, 7), (R_E, 6),
+        (SUM_R, 4), (R_L, 0),
+    ),
+}
+
+
+def layer_kernel(
+    tok_hbm, len_ref, cot_hbm, wq_hbm, wl_hbm, wk_hbm, wv_hbm, wo_hbm, gain_one, gain_two, wg_hbm, wu_hbm, wd_ref,
+    out_hbm, gtok_hbm, at_hbm, gain_hbm, gg_hbm, gu_hbm, gd_hbm,
+    attn, latw, gate_a, up_a, gate_b, up_b, down_w, down_c, gain_full,
+    tok, ends, bias, normed, query, latent, keys, values, merged, lse, middle, normed2, dout,
+    mixed, dgate, dup, tmp, rcv_dn2, snd_out, rcv_out,
+    dmid, dmid_low, dmerged, dquery, dkeys, dvalues, dlatent,
+    pattn,
+    s_d, s_ga, s_ua, s_gb, s_ub,
+    y_d, y_ga, y_ua, y_gb, y_ub,
+    z_d, z_ga, z_ua, z_gb, z_ub,
+    x_ga, x_ua, x_gb, x_ub,
+    s_a, x_a, z_a, y_a, sum_own, sum_rcv,
+    send_sem, recv_sem, local_sem,
+):
+    snd_dn2 = dquery
+    dp = lax.axis_index("dp")
+    fs = lax.axis_index("fsdp")
+    x, c, z, y = lax.div(dp, 2), lax.rem(dp, 2), lax.div(fs, 2), lax.rem(fs, 2)
+    zh, zl = lax.div(z, 2), lax.rem(z, 2)
+    sib = (x * 2 + 1 - c, fs)
+    xp = ((1 - x) * 2 + c, fs)
+    yp = (dp, z * 2 + 1 - y)
+    z1 = (dp, (zh * 2 + 1 - zl) * 2 + y)
+    z2 = (dp, ((1 - zh) * 2 + zl) * 2 + y)
+
+    def rel(v, other):
+        return 1 - v if other else v
+
+    def line(dh, dl):
+        return rel(zh, dh) * 2 + rel(zl, dl)
+
+    sent = {}
+    now = {"op": None, "wait": None}
+
+    def copy(src, dst, slot, target):
+        return pltpu.make_async_remote_copy(
+            src_ref=src, dst_ref=dst, send_sem=send_sem.at[slot], recv_sem=recv_sem.at[slot],
+            device_id=target, device_id_type=MESH,
+        )
+
+    def send(group, src, dst, slot, target):
+        if now["wait"] is None:
+            copy(src, dst, slot, target).start()
+            users = sent.setdefault(group, [])
+            if now["op"] not in users:
+                users.append(now["op"])
+        elif now["wait"] == group:
+            copy(src, dst, slot, target).wait_send()
+
+    def arrive(dst, slot):
+        if now["wait"] is None:
+            copy(dst, dst, slot, sib).wait_recv()
+
+    def local(src, dst, k):
+        return pltpu.make_async_copy(src, dst, local_sem.at[k])
+
+    def put(src, dst, k):
+        if now["wait"] is None:
+            local(src, dst, k).start()
+
+    def add(dst, src):
+        if now["wait"] is None:
+            dst[...] = dst[...] + src[...]
+
+    def cols(n, width=256):
+        return pl.ds(pl.multiple_of(n * width, width), width)
+
+    ops = {}
+
+    def op(code):
+        def enter(fn):
+            ops[code] = fn
+            return fn
+
+        return enter
+
+    def run(items, wait=None):
+        now["wait"] = wait
+        for name, *rest in items:
+            now["op"] = (name, *rest)
+            ops[name](*rest)
+        now["wait"] = None
+
+    def drain(group):
+        run(sent.pop(group, []), group)
+
+    def gap(name):
+        run(PLAN.get(name, ()))
+
+    def loop(count, *stages, at=(), unroll=1):
+        ends = [*at, count]
+        for first, last in zip([0, *at], ends):
+
+            def step(k, carry):
+                for _, body in stages:
+                    body(k)
+                return carry
+
+            if last - first == 1:
+                for name, body in stages:
+                    body(first)
+                    gap((name, first))
+            else:
+                lax.fori_loop(first, last, step, 0, unroll=unroll)
+                gap((stages[-1][0], last - 1))
+
+    ways = {"y": yp, "x": xp, "1": z1, "2": z2, "s": sib}
+
+    def a_blk(w, bits):
+        route = ROUTE[w]
+        across = {way: bits >> k & 1 for k, way in enumerate(route)}
+        xx, cc, yy = rel(x, across["x"]), rel(c, across["s"]), rel(y, across["y"])
+        zz = line(across["2"], across["1"])
+        if w == 0:
+            return latw.at[xx, cc, zz, yy]
+        if w == 1:
+            return attn.at[0, xx, cc, zz, yy]
+        return attn.at[1, xx, cc, zz, yy, :, pl.ds(512 * (w - 2), 512)]
+
+    def a_send(w, bits, k):
+        blk = a_blk(w, bits)
+        send("attn", blk, blk, S_A[w] + bits + (1 << k), ways[ROUTE[w][k]])
+
+    @op(AA)
+    def aa(w, bits):
+        if bits:
+            arrive(a_blk(w, bits), S_A[w] + bits)
+        a_send(w, bits, 4)
+
+    @op(AG)
+    def ag(w, bits, k):
+        a_send(w, bits, k)
+
+    @op(AT)
+    def at(w):
+        for bits in range(16, 32):
+            arrive(a_blk(w, bits), S_A[w] + bits)
+
+    ffn = (down_w, gate_a, up_a, gate_b, up_b)
+    ffn_hbm = (None, wg_hbm, wu_hbm, wg_hbm, wu_hbm)
+    starts = (None, 0, 0, 768, 768)
+
+    def half_cols(xx, t):
+        return pl.ds(pl.multiple_of(xx * HALF + starts[t], 128), ffn[t].shape[-1])
+
+    @op(H_S)
+    def h_s(t):
+        send("half", ffn_hbm[t].at[:, half_cols(1 - x, t)], ffn[t].at[c, z, y, x], S_HALF + t, xp)
+
+    @op(H_R)
+    def h_r(t):
+        arrive(ffn[t].at[c, z, y, 1 - x], S_HALF + t)
+
+    def f_blk(t, bits):
+        return ffn[t].at[rel(c, bits >> 3 & 1), line(bits & 1, bits >> 1 & 1), rel(y, bits >> 2 & 1)]
+
+    def f_send(t, bits, k):
+        blk = f_blk(t, bits)
+        send("ffn%d" % t, blk, blk, S_F[t] + bits + (1 << k), (z2, z1, yp, sib)[k])
+
+    @op(FA)
+    def fa(t, bits):
+        if bits:
+            arrive(f_blk(t, bits), S_F[t] + bits)
+        f_send(t, bits, 3)
+
+    @op(FG)
+    def fg(t, bits, k):
+        f_send(t, bits, k)
+
+    @op(FT)
+    def ft(t):
+        for bits in range(8, 16):
+            arrive(f_blk(t, bits), S_F[t] + bits)
+
+    def quarter(ref, k):
+        return ref.at[pl.ds(k * 64, 64)]
+
+    @op(COT_S)
+    def cot_s(k):
+        send("cot", quarter(dout.at[x], k), quarter(dout.at[x], k), S_COT + k, xp)
+
+    @op(COT_R)
+    def cot_r():
+        for k in range(4):
+            arrive(quarter(dout.at[1 - x], k), S_COT + k)
+
+    @op(TOK_S)
+    def tok_s(k):
+        send("tok", quarter(tok.at[x], k), quarter(tok.at[x], k), S_TOK + k, xp)
+
+    @op(TOK_R)
+    def tok_r():
+        for k in range(4):
+            arrive(quarter(tok.at[1 - x], k), S_TOK + k)
+
+    @op(END_S)
+    def end_s():
+        send("tok", ends.at[x], ends.at[x], S_END, xp)
+
+    @op(END_R)
+    def end_r():
+        arrive(ends.at[1 - x], S_END)
+
+    @op(DN2_S)
+    def dn2_s():
+        send("dn2", snd_dn2, rcv_dn2, S_DN2, xp)
+
+    @op(DN2_R)
+    def dn2_r():
+        arrive(rcv_dn2, S_DN2)
+
+    @op(OUT_S)
+    def out_s(k):
+        send("out", quarter(snd_out, k), quarter(rcv_out, k), S_OUT + k, xp)
+
+    @op(OUT_R)
+    def out_r():
+        for k in range(4):
+            arrive(quarter(rcv_out, k), S_OUT + k)
+
+    ffn_s = (s_d, s_ga, s_ua, s_gb, s_ub)
+    ffn_y = (y_d, y_ga, y_ua, y_gb, y_ub)
+    ffn_zb = (z_d, z_ga, z_ua, z_gb, z_ub)
+    ffn_x = (None, x_ga, x_ua, x_gb, x_ub)
+    out_cols = (None, *[pl.ds(starts[t], ffn[t].shape[-1]) for t in range(1, FFN)])
+    ffn_out = (None, *[gg_hbm, gu_hbm] * 2)
+
+    def pick(i):
+        return ((0, pl.ds(0, WIDTH)), (1, pl.ds(0, WIDTH)), (2, pl.ds(0, 512)), (2, pl.ds(512, 512)))[i - FFN]
+
+    def sib_part(i, other):
+        if i < FFN:
+            yy = rel(y, other)
+            return yy, ffn[i].at[1 - c, :, yy], ffn_s[i].at[yy], lambda zz: (ffn[i].at[c, zz, yy], ffn_s[i].at[yy, zz])
+        k, cl = pick(i)
+        if SUM_X_FIRST[i - FFN]:
+            xx = rel(x, other)
+            return (
+                xx,
+                pattn.at[k, xx, 1 - c, :, :, :, cl],
+                s_a.at[k, xx, :, :, :, cl],
+                lambda zz: (pattn.at[k, xx, c, zz, :, :, cl], s_a.at[k, xx, zz, :, :, cl]),
+            )
+        yy = rel(y, other)
+        return (
+            yy,
+            pattn.at[k, :, 1 - c, :, yy, :, cl],
+            s_a.at[k, :, :, yy, :, cl],
+            lambda zz: (pattn.at[k, :, c, zz, yy, :, cl], s_a.at[k, :, zz, yy, :, cl]),
+        )
+
+    def first_hop(i, d):
+        if i < FFN:
+            return yp, ffn[i].at[c, d, 1 - y], ffn_y[i].at[d]
+        k, cl = pick(i)
+        if SUM_X_FIRST[i - FFN]:
+            return xp, pattn.at[k, 1 - x, c, d, :, :, cl], x_a.at[k, d, :, :, cl]
+        return yp, pattn.at[k, :, c, d, 1 - y, :, cl], x_a.at[k, d, :, :, cl]
+
+    def line_blk(i, d):
+        if i < FFN:
+            return ffn[i].at[c, d, y]
+        k, cl = pick(i)
+        if SUM_X_FIRST[i - FFN]:
+            return pattn.at[k, x, c, d, :, :, cl]
+        return pattn.at[k, :, c, d, y, :, cl]
+
+    def line_buf(i, b):
+        if i < FFN:
+            return ffn_zb[i].at[b]
+        k, cl = pick(i)
+        return z_a.at[k, b, :, :, cl]
+
+    def last_hop(i):
+        if i < FFN:
+            return xp, ffn[i].at[c, z, y, 1 - x], ffn_x[i]
+        k, cl = pick(i)
+        if SUM_X_FIRST[i - FFN]:
+            return yp, pattn.at[k, x, c, z, 1 - y, :, cl], y_a.at[k, :, cl]
+        return xp, pattn.at[k, 1 - x, c, z, y, :, cl], y_a.at[k, :, cl]
+
+    @op(R_GO)
+    def r_go(i):
+        for other in (1, 0):
+            k, src, dst, _ = sib_part(i, other)
+            send("r", src, dst, S_R[i] + k, sib)
+
+    @op(R_S)
+    def r_s(i, other):
+        k, _, dst, pairs = sib_part(i, other)
+        arrive(dst, S_R[i] + k)
+        if not other:
+            for zz in range(4):
+                add(*pairs(zz))
+
+    @op(R_B)
+    def r_b(i, bits):
+        d = line(bits >> 1, bits & 1)
+        add(*sib_part(i, 1)[3](d))
+        target, src, buf = first_hop(i, d)
+        send("r", src, buf, S_R[i] + 2 + bits, target)
+
+    @op(R_A)
+    def r_a(i, bits):
+        d = line(bits >> 1, bits & 1)
+        _, _, buf = first_hop(i, d)
+        arrive(buf, S_R[i] + 2 + bits)
+        add(line_blk(i, d), buf)
+        if bits & 1:
+            send("r", line_blk(i, d), line_buf(i, bits >> 1), S_R[i] + 6 + (bits >> 1), z1)
+
+    @op(R_1)
+    def r_1(i, dh):
+        d = line(dh, 0)
+        arrive(line_buf(i, dh), S_R[i] + 6 + dh)
+        add(line_blk(i, d), line_buf(i, dh))
+        if dh:
+            send("r", line_blk(i, d), line_buf(i, 2), S_R[i] + 8, z2)
+
+    @op(R_2)
+    def r_2(i):
+        arrive(line_buf(i, 2), S_R[i] + 8)
+        add(line_blk(i, z), line_buf(i, 2))
+
+    @op(R_L)
+    def r_l(i):
+        if i == 0:
+            put(down_w.at[c, z, y], gd_hbm, PUT)
+            return
+        target, src, buf = last_hop(i)
+        send("r", src, buf, S_R[i] + 9, target)
+        if i < FFN:
+            put(ffn[i].at[c, z, y, x], ffn_out[i].at[x, :, out_cols[i]], PUT + i * 2)
+
+    @op(R_E)
+    def r_e(i):
+        _, _, buf = last_hop(i)
+        arrive(buf, S_R[i] + 9)
+        if i < FFN:
+            put(buf, ffn_out[i].at[1 - x, :, out_cols[i]], PUT + 1 + i * 2)
+        else:
+            k, cl = pick(i)
+            blk = pattn.at[k, x, c, z, y, :, cl]
+            add(blk, buf)
+            put(blk, at_hbm.at[k, :, cl], PUT + 4 + FFN + i)
+
+    def wait_out():
+        local(down_w.at[c, z, y], gd_hbm, PUT).wait()
+        for i in range(1, FFN):
+            local(ffn[i].at[c, z, y, x], ffn_out[i].at[x, :, out_cols[i]], PUT + i * 2).wait()
+            local(ffn_x[i], ffn_out[i].at[1 - x, :, out_cols[i]], PUT + 1 + i * 2).wait()
+        for i in range(FFN, FFN + 4):
+            k, cl = pick(i)
+            local(pattn.at[k, x, c, z, y, :, cl], at_hbm.at[k, :, cl], PUT + 4 + FFN + i).wait()
+
+    sum_to = (sib, yp, xp, z1, z2)
+
+    @op(SUM_S)
+    def sum_s(i):
+        copy(sum_own, sum_rcv.at[i], S_SUM + i, sum_to[i]).start()
+
+    @op(SUM_R)
+    def sum_r(i):
+        copy(sum_own, sum_rcv.at[i], S_SUM + i, sum_to[i]).wait_send()
+        arrive(sum_rcv.at[i], S_SUM + i)
+        add(sum_own, sum_rcv.at[i])
+
+    loads = [
+        (wq_hbm, attn.at[0, x, c, z, y]),
+        (wl_hbm, latw.at[x, c, z, y, :, pl.ds(0, 512)]),
+        (wk_hbm, latw.at[x, c, z, y, pl.ds(0, 16), pl.ds(512, 512)]),
+        (wv_hbm, latw.at[x, c, z, y, pl.ds(16, 16), pl.ds(512, 512)]),
+        (wo_hbm, attn.at[1, x, c, z, y]),
+        (tok_hbm, tok.at[x]),
+        (cot_hbm, dout.at[x]),
+        *[(ffn_hbm[t].at[:, half_cols(x, t)], ffn[t].at[c, z, y, x]) for t in range(1, FFN)],
+    ]
+    loads = [local(src, dst, k) for k, (src, dst) in enumerate(loads)]
+    for load in loads:
+        load.start()
+    bar = pltpu.get_barrier_semaphore()
+
+    def hello(target):
+        pl.semaphore_signal(bar, inc=1, device_id=target, device_id_type=MESH)
+
+    for target in (sib, xp, yp, z1, z2):
+        hello(target)
+
+    def piled(rows):
+        return jnp.concatenate([rows[:, 0:512], rows[:, 512:WIDTH]], axis=0).astype(BF16)
+
+    def stage_own():
+        down_w[c, z, y] = piled(wd_ref[...].astype(F32))
+        lane = lax.broadcasted_iota(jnp.int32, (16, 128), 1)
+        mine = lax.div(lane, 32) == lax.rem(fs, 4)
+        two = [ref[...].astype(F32).reshape(1, 32) for ref in (gain_one, gain_two)]
+        two = jnp.concatenate([*two, jnp.zeros((14, 32), F32)], axis=0)
+        two = jnp.where(mine, jnp.concatenate([two] * 4, axis=1), 0.0)
+        latw[x, c, z, y, pl.ds(0, 16), pl.ds(WIDTH, 128)] = two.astype(BF16)
+        latw[x, c, z, y, pl.ds(16, 16), pl.ds(WIDTH, 128)] = jnp.zeros((16, 128), BF16)
+
+    e0 = len_ref[0]
+    e1 = e0 + len_ref[1]
+    e2 = e1 + len_ref[2]
+    e3 = e2 + len_ref[3]
+
+    def stage_ends():
+        place = lax.broadcasted_iota(jnp.int32, (8, 128), 0)
+        ends[x] = sum(jnp.where(place == k, e, 0) for k, e in enumerate((e0, e1, e2, e3))).astype(F32)
+
+    stage_own()
+    stage_ends()
+    for load in loads[:5]:
+        load.wait()
+    pl.semaphore_wait(bar, 5)
+    gap(G_START)
+
+    for load in loads[5:]:
+        load.wait()
+
+    def mask_rows(k):
+        rows = pl.ds(pl.multiple_of(k * 64, 64), 64)
+        position = lax.broadcasted_iota(jnp.int32, (64, WIDTH), 0) + k * 64
+        dout[x, rows] = jnp.where(position < e3, dout[x, rows].astype(F32), 0.0).astype(BF16)
+
+    loop(4, (G_MASK, mask_rows))
+    gap(G_WEIGHTS)
+
+    def gain_rows(k):
+        g = latw.at[lax.div(k, 4), lax.div(lax.rem(k, 4), 2)]
+        part = g[pl.ds(lax.rem(k, 2) * 2, 2), :, 0:16, WIDTH : WIDTH + 128].astype(F32)
+        gain_full[:, pl.ds(pl.multiple_of(k * 128, 128), 128)] = part[0, 0] + part[0, 1] + part[1, 0] + part[1, 1]
+
+    loop(8, (G_GAIN, gain_rows))
+
+    low_half = lax.broadcasted_iota(jnp.int32, (ROWS, 128), 1) < HEAD_DIM
+    head_lane = lax.broadcasted_iota(jnp.int32, (ROWS, 128), 1)
+
+    def halves(v):
+        zero = jnp.zeros_like(v)
+        return (jnp.where(low_half, v, zero), jnp.where(low_half, zero, v))
+
+    def both(v):
+        return jnp.concatenate(halves(v), axis=0)
+
+    def scaled(v):
+        return (v.astype(F32) * SCALE).astype(BF16)
+
+    def up_weight(g, first):
+        return latw[g, :, :, :, pl.ds(first, 16), pl.ds(512, 512)].reshape(256, 512)
+
+    def segment(m, shape, axis):
+        position = lax.broadcasted_iota(jnp.int32, shape, axis).astype(F32)
+        return sum((position >= ends[m, pl.ds(k, 1), pl.ds(0, 1)]).astype(F32) for k in range(4))
+
+    def stage_masks(m):
+        row = lax.broadcasted_iota(jnp.int32, (ROWS, ROWS), 0)
+        col = lax.broadcasted_iota(jnp.int32, (ROWS, ROWS), 1)
+        same = segment(m, (ROWS, 1), 0) == segment(m, (1, ROWS), 1)
+        bias[m] = jnp.where(same & (col <= row), 0.0, -1e30)
+
+    def attention(m, own, at, normed, query, latent, keys, values, merged, middle):
+        at_norm, at_latent, at_keys, at_query, at_attend, at_middle, at_norm2 = at
+
+        def norm_rows(k):
+            rows = pl.ds(pl.multiple_of(k * 64, 64), 64)
+            val = tok[m, rows].astype(F32)
+            r1 = lax.rsqrt(jnp.mean(val * val, axis=1, keepdims=True) + EPSILON)
+            normed[rows] = (val * r1 * gain_full[0:1, :]).astype(BF16)
+
+        def latent_cols(n):
+            w = latw[:, :, :, :, :, cols(n)].reshape(WIDTH, 256)
+            latent[:, cols(n)] = nn(normed[...], w).astype(BF16)
+
+        def key_cols(g):
+            lat = latent[:, cols(g)]
+            keys[:, cols(g, 512)] = nn(lat, up_weight(g, 0)).astype(BF16)
+            values[:, cols(g, 512)] = nn(lat, up_weight(g, 16)).astype(BF16)
+
+        def query_cols(n):
+            w = attn[0, :, :, :, :, :, cols(n)].reshape(WIDTH, 256)
+            query[:, cols(n)] = nn(normed[...], w).astype(BF16)
+
+        def attend(j):
+            pair = cols(j, 128)
+            s = nt(both(scaled(query[:, pair])), keys[:, pair]) + jnp.concatenate([bias[m]] * 2, axis=0)
+            peak = jnp.max(s, axis=1, keepdims=True)
+            expo = jnp.exp(s - peak)
+            total = jnp.sum(expo, axis=1, keepdims=True)
+            res = nn((expo / total).astype(BF16), values[:, pair])
+            merged[:, pair] = jnp.where(low_half, res[0:ROWS], res[ROWS : 2 * ROWS]).astype(BF16)
+            if own:
+                logsum = peak + jnp.log(total)
+                lse[...] = jnp.where(
+                    head_lane == j * 2,
+                    logsum[0:ROWS],
+                    jnp.where(head_lane == j * 2 + 1, logsum[ROWS : 2 * ROWS], lse[...]),
+                )
+
+        def middle_cols(n):
+            w = attn[1, :, :, :, :, :, cols(n)].reshape(WIDTH, 256)
+            middle[:, cols(n)] = tok[m, :, cols(n)].astype(F32) + nn(merged[...], w)
+
+        def norm2_rows(k):
+            rows = pl.ds(pl.multiple_of(k * 64, 64), 64)
+            val = middle[rows]
+            r2 = lax.rsqrt(jnp.mean(val * val, axis=1, keepdims=True) + EPSILON)
+            normed2[m, rows] = (val * r2 * gain_full[1:2, :]).astype(BF16)
+
+        def first():
+            stage_masks(m)
+            loop(4, (at_norm, norm_rows))
+            loop(2, (at_latent, latent_cols), unroll=2)
+            loop(GROUPS, (at_keys, key_cols), unroll=2)
+
+        def second():
+            loop(4, (at_query, query_cols), unroll=2)
+            loop(8, (at_attend, attend), at=(4,), unroll=4)
+
+        def third():
+            loop(4, (at_middle, middle_cols), unroll=2)
+            loop(4, (at_norm2, norm2_rows))
+
+        return first, second, third
+
+    def compact(k):
+        pair = down_w.at[lax.div(k, 4), lax.rem(k, 4)]
+        one, two = pair[0].astype(F32), pair[1].astype(F32)
+        rows = pl.ds(pl.multiple_of(k * 2 * DOWN, 16), 2 * DOWN)
+        for half in range(2):
+            part = slice(half * DOWN, (half + 1) * DOWN)
+            down_c[rows, pl.ds(half * 512, 512)] = jnp.concatenate([one[part], two[part]], axis=0).astype(BF16)
+
+    at = (G_NORM, G_LATENT, G_KEYS, G_QUERY, G_ATTEND, G_MIDDLE, G_NORM2)
+    own = attention(x, True, at, normed, query, latent, keys, values, merged, middle)
+    at = (G_NORM_P, G_LATENT_P, G_KEYS_P, G_QUERY_P, G_ATTEND_P, G_MIDDLE_P, G_NORM2_P)
+    across = attention(1 - x, False, at, dmid_low, dquery, dlatent, dkeys, dvalues, dmerged, dmid)
+    own[0]()
+    gap(G_ACROSS)
+    across[0]()
+    gap(G_DOWN_W)
+    loop(8, (G_COMPACT, compact))
+    gap(G_QUERY)
+    own[1]()
+    across[1]()
+    gap(G_OUTPUT_W)
+    own[2]()
+    across[2]()
+    gap(G_FFN_A)
+
+    def ffn_w(ref, half, sl=slice(None)):
+        w = ref[:, :, :, half, :, sl]
+        return w.reshape(512, w.shape[-1])
+
+    def hidden(it, gate_w, up_w, base, widths):
+        m = rel(x, it)
+        rows = pl.ds(pl.multiple_of(m * ROWS, ROWS), ROWS)
+        for first, width in widths:
+            sl, at = pl.ds(first, width), pl.ds(base + first, width)
+            n2 = normed2[m]
+            gate = nn(n2[:, 0:512], ffn_w(gate_w, 0, sl)) + nn(n2[:, 512:1024], ffn_w(gate_w, 1, sl))
+            upper = nn(n2[:, 0:512], ffn_w(up_w, 0, sl)) + nn(n2[:, 512:1024], ffn_w(up_w, 1, sl))
+            dmix = nt(dout[m], down_c[at])
+            sig = jax.nn.sigmoid(gate)
+            silu = gate * sig
+            mixed[rows, at] = (silu * upper).astype(BF16)
+            dgate[rows, at] = (dmix * upper * sig * (1.0 + gate * (1.0 - sig))).astype(BF16)
+            dup[rows, at] = (dmix * silu).astype(BF16)
+
+    def dn_half(it, gate_w, up_w, at, more):
+        m = rel(x, it)
+        rows = pl.ds(pl.multiple_of(m * ROWS, ROWS), ROWS)
+        for half in range(2):
+            part = nt(dgate[rows, at], ffn_w(gate_w, half)) + nt(dup[rows, at], ffn_w(up_w, half))
+            to = (pl.ds(ROWS * it, ROWS), pl.ds(half * 512, 512))
+            if more:
+                part = part + tmp[to]
+            if more == 2 and it:
+                snd_dn2[:, pl.ds(half * 512, 512)] = part.astype(BF16)
+            else:
+                tmp[to] = part
+
+    def grad_gate_up(it, gate_w, up_w, at):
+        cc = jnp.where(it < 2, 1 - c, c)
+        half = lax.rem(it, 2)
+        sl = pl.ds(pl.multiple_of(half * 512 + cc * 256, 256), 256)
+        width = gate_w.shape[-1]
+        for src, dst in ((dgate, gate_w), (dup, up_w)):
+            g = nn(normed2[0, :, sl].T, src[pl.ds(0, ROWS), at]) + nn(normed2[1, :, sl].T, src[pl.ds(ROWS, ROWS), at])
+            dst[cc, :, :, half] = g.astype(BF16).reshape(4, 2, 32, width)
+
+    def grad_down(it):
+        cc = rel(c, it == 0)
+        wide = pl.ds(pl.multiple_of(cc * 640, 128), 768)
+        mt = mixed[:, wide].T
+        tmp[pl.ds(ROWS, 768)] = nn(mt[:, 0:256], dout[0]) + nn(mt[:, 256:512], dout[1])
+
+        def split(k, carry):
+            rows = tmp[pl.ds(pl.multiple_of(ROWS + cc * 64 + k * DOWN, 8), DOWN)]
+            down_w[cc, lax.div(k, 2), lax.rem(k, 2)] = piled(rows)
+            return carry
+
+        lax.fori_loop(0, 8, split, 0)
+
+    def hidden_a(it):
+        hidden(it, gate_a, up_a, 0, ((0, 512), (512, 256)))
+
+    def dn_a(it):
+        dn_half(it, gate_a, up_a, pl.ds(0, 768), 0)
+
+    def gateup_a(it):
+        grad_gate_up(it, gate_a, up_a, pl.ds(0, 768))
+
+    def hidden_b(it):
+        hidden(it, gate_b, up_b, 768, ((0, 512), (512, 128)))
+
+    def dn_b(it):
+        dn_half(it, gate_b, up_b, pl.ds(768, 640), 2)
+
+    def gateup_b(it):
+        grad_gate_up(it, gate_b, up_b, pl.ds(768, 640))
+
+    def out_half(it):
+        m = rel(x, it == 0)
+        rows = pl.ds(pl.multiple_of(m * ROWS, ROWS), ROWS)
+        part = nn(mixed[rows], down_c[...])
+        if it == 0:
+            snd_out[...] = part.astype(BF16)
+        else:
+            tmp[pl.ds(ROWS, ROWS)] = part
+
+    loop(2, (G_HIDDEN_A, hidden_a), at=(1,))
+    loop(2, (G_DN_A, dn_a), at=(1,))
+    drain("ffn1")
+    drain("ffn2")
+    loop(4, (G_GATEUP_A, gateup_a), at=(2,))
+    gap(G_FFN_B)
+    hidden_b(1)
+    gap((G_HIDDEN_B, 1))
+    dn_b(1)
+    gap((G_DN_B, 1))
+    hidden_b(0)
+    gap((G_HIDDEN_B, 0))
+    dn_b(0)
+    gap((G_DN_B, 0))
+    drain("ffn0")
+    loop(2, (G_DOWN, grad_down), at=(1,))
+    drain("ffn3")
+    drain("ffn4")
+    loop(4, (G_GATEUP_B, gateup_b), at=(2,))
+    loop(2, (G_OUT, out_half), at=(1,))
+    gap(G_BACK)
+
+    sum_own[...] = jnp.zeros((8, WIDTH), F32)
+
+    def back_two(k):
+        rows = pl.ds(pl.multiple_of(k * 32, 32), 32)
+        mid = middle[rows]
+        r2 = lax.rsqrt(jnp.mean(mid * mid, axis=1, keepdims=True) + EPSILON)
+        grad = tmp[rows] + rcv_dn2[rows].astype(F32)
+        sum_own[1:2] = sum_own[1:2] + jnp.sum(grad * mid * r2, axis=0, keepdims=True)
+        s = grad * gain_full[1:2, :]
+        res = dout[x, rows].astype(F32) + r2 * (s - mid * r2 * r2 * jnp.mean(s * mid, axis=1, keepdims=True))
+        dmid[rows] = res
+        dmid_low[rows] = res.astype(BF16)
+
+    loop(8, (G_NORM2B, back_two), unroll=2)
+
+    def dmerged_cols(k):
+        w = attn[1, lax.div(k, 2), lax.rem(k, 2)].reshape(256, WIDTH)
+        dmerged[:, cols(k)] = nt(dmid_low[...], w).astype(BF16)
+
+    loop(4, (G_DMERGED, dmerged_cols), unroll=2)
+
+    def grad_output(it):
+        cc = jnp.where(it < 2, 1 - c, c)
+        half = lax.rem(it, 2)
+        g = nn(merged[:, cols(half * 2 + cc)].T, dmid_low[...])
+        pattn[0, half, cc] = g.astype(BF16).reshape(4, 2, 32, WIDTH)
+
+    loop(4, (G_OUTPUT, grad_output), at=(2,), unroll=2)
+
+    drain("dn2")
+
+    def attend_back(j):
+        pair = cols(j, 128)
+        k_pair, v_pair = keys[:, pair], values[:, pair]
+        q, do = both(scaled(query[:, pair])), both(dmerged[:, pair])
+        logsum = jnp.concatenate(
+            [jnp.sum(jnp.where(head_lane == j * 2 + h, lse[...], 0.0), axis=1, keepdims=True) for h in (0, 1)], axis=0
+        )
+        probs = jnp.exp(nt(q, k_pair) + jnp.concatenate([bias[x]] * 2, axis=0) - logsum)
+        dprobs = nt(do, v_pair)
+        dvalues[:, pair] = tn(probs.astype(BF16), do).astype(BF16)
+        row_sum = jnp.sum(probs * dprobs, axis=1, keepdims=True)
+        dscores = (probs * (dprobs - row_sum)).astype(BF16)
+        dq = nn(dscores, k_pair)
+        dkeys[:, pair] = tn(dscores, q).astype(BF16)
+        dquery[:, pair] = (jnp.where(low_half, dq[0:ROWS], dq[ROWS : 2 * ROWS]) * SCALE).astype(BF16)
+
+    loop(8, (G_ATTENDB, attend_back), at=(4,), unroll=2)
+
+    def other_first(it):
+        cc = jnp.where(it < 2, 1 - c, c)
+        return lax.rem(it, 2), cc
+
+    def grad_query(it):
+        half, cc = other_first(it)
+        g = nn(normed[:, cols(half * 2 + cc)].T, dquery[...])
+        pattn[1, half, cc] = g.astype(BF16).reshape(4, 2, 32, WIDTH)
+
+    loop(4, (G_PROJQ, grad_query), at=(2,), unroll=2)
+
+    def latent_back(g):
+        dk, dv = dkeys[:, cols(g, 512)], dvalues[:, cols(g, 512)]
+        dlatent[:, cols(g)] = (nt(dk, up_weight(g, 0)) + nt(dv, up_weight(g, 16))).astype(BF16)
+        lat = latent[:, cols(g)].T
+        pattn[2, g, :, :, :, pl.ds(0, 16), pl.ds(512, 512)] = nn(lat, dk).astype(BF16).reshape(2, 4, 2, 16, 512)
+        pattn[2, g, :, :, :, pl.ds(16, 16), pl.ds(512, 512)] = nn(lat, dv).astype(BF16).reshape(2, 4, 2, 16, 512)
+
+    loop(GROUPS, (G_LATENTB, latent_back))
+
+    def grad_latent(it):
+        half, cc = other_first(it)
+        g = nn(normed[:, cols(half * 2 + cc)].T, dlatent[...])
+        pattn[2, half, cc, :, :, :, pl.ds(0, 512)] = g.astype(BF16).reshape(4, 2, 32, 512)
+
+    loop(4, (G_PROJL, grad_latent), at=(2,), unroll=2)
+
+    def dnormed_cols(k):
+        xx, cc = lax.div(k, 2), lax.rem(k, 2)
+        part = nt(dquery[...], attn[0, xx, cc].reshape(256, WIDTH))
+        part = part + nt(dlatent[...], latw[xx, cc, :, :, :, pl.ds(0, 512)].reshape(256, 512))
+        tmp[pl.ds(0, ROWS), cols(k)] = part
+
+    loop(4, (G_DNORMED, dnormed_cols), unroll=2)
+
+    def back_one(k):
+        rows = pl.ds(pl.multiple_of(k * 32, 32), 32)
+        val = tok[x, rows].astype(F32)
+        r1 = lax.rsqrt(jnp.mean(val * val, axis=1, keepdims=True) + EPSILON)
+        grad = tmp[rows]
+        sum_own[0:1] = sum_own[0:1] + jnp.sum(grad * val * r1, axis=0, keepdims=True)
+        s = grad * gain_full[0:1, :]
+        dmid[rows] = dmid[rows] + r1 * (s - val * r1 * r1 * jnp.mean(s * val, axis=1, keepdims=True))
+
+    loop(8, (G_NORM1B, back_one), unroll=2)
+    to_gtok = local(dmid, gtok_hbm, 0)
+    to_gtok.start()
+    gap(G_RESULT)
+
+    def out_rows(k):
+        rows = pl.ds(pl.multiple_of(k * 32, 32), 32)
+        part = tmp[pl.ds(pl.multiple_of(ROWS + k * 32, 32), 32)]
+        tok[x, rows] = (middle[rows] + (part + rcv_out[rows].astype(F32))).astype(BF16)
+
+    drain("tok")
+    loop(8, (G_RESULT, out_rows))
+    to_out = local(tok.at[x], out_hbm, 1)
+    to_out.start()
+    gap(G_TAIL)
+    to_gain = local(sum_own.at[:, pl.ds(pl.multiple_of((dp * 2 + lax.div(fs, 4)) * 128, 128), 128)], gain_hbm, 2)
+    to_gain.start()
+    for group in list(sent):
+        drain(group)
+    to_gtok.wait()
+    to_out.wait()
+    to_gain.wait()
+    wait_out()
+
+
+def finish_kernel(*refs):
+    given, outs, bufs, casts = refs[:7], refs[7:19], refs[19:26], refs[26:36]
+    in_sem, out_sem = refs[36:]
+    takes = [pltpu.make_async_copy(src, dst, in_sem.at[k]) for k, (src, dst) in enumerate(zip(given, bufs))]
+    gives = [pltpu.make_async_copy(src, dst, out_sem.at[k]) for k, (src, dst) in enumerate(zip([*bufs[:2], *casts], outs))]
+    for k in (1, 0, 4, 5, 6, 2, 3):
+        takes[k].start()
+    for k in (1, 0):
+        takes[k].wait()
+        gives[k].start()
+    _, _, at_ref, gain_ref, gg_ref, gu_ref, gd_ref = bufs
+    gq_o, gl_o, gk_o, gv_o, go_o, ga_o, gf_o, gg_o, gu_o, gd_o = casts
+    for k, src, dst in ((4, gg_ref, gg_o), (5, gu_ref, gu_o)):
+        takes[k].wait()
+        dst[:, 0:HALF] = src[0].astype(F32)
+        dst[:, HALF : 2 * HALF] = src[1].astype(F32)
+        gives[k + 5].start()
+    takes[6].wait()
+    gd = gd_ref[...].astype(F32)
+    gd_o[:, 0:512] = gd[0:DOWN]
+    gd_o[:, 512:WIDTH] = gd[DOWN : 2 * DOWN]
+    gives[11].start()
+    takes[2].wait()
+    go_o[...] = at_ref[0].astype(F32)
+    gq_o[...] = at_ref[1].astype(F32)
+    gl_o[...] = at_ref[2, :, 0:512].astype(F32)
+    gk_o[...] = at_ref[2, 0:16, 512:1024].astype(F32)
+    gv_o[...] = at_ref[2, 16:32, 512:1024].astype(F32)
+    takes[3].wait()
+    place = lax.rem(lax.axis_index("fsdp"), 4)
+    picked = sum(jnp.where(place == k, gain_ref[:, 32 * k : 32 * k + 32], 0.0) for k in range(4))
+    ga_o[...] = picked[0:1]
+    gf_o[...] = picked[1:2]
+    for k in range(2, 9):
+        gives[k].start()
+    for give in gives:
+        give.wait()
+
+
+def kernel_on_device(
+    tokens, seq_lengths, cotangent, w_query, w_latent, w_keyup, w_valup, w_output, norm_attn, norm_ffn,
+    w_gate, w_up, w_down,
+):
+    hbm, vmem = pl.BlockSpec(memory_space=pl.ANY), pl.BlockSpec(memory_space=pltpu.VMEM)
+    smem = pl.BlockSpec(memory_space=pltpu.SMEM)
+    shape = jax.ShapeDtypeStruct
+    outs = [
+        shape((ROWS, WIDTH), BF16), shape((ROWS, WIDTH), F32), shape((3, 32, WIDTH), BF16), shape((8, 128), F32),
+        shape((2, 32, HALF), BF16), shape((2, 32, HALF), BF16), shape((2 * DOWN, 512), BF16),
+    ]
+    V = pltpu.VMEM
+    units = [(2 * DOWN, 512), *[(2, 32, width) for width in PARTS for _ in range(2)]]
+    act = V((ROWS, WIDTH), BF16)
+    scratch = [
+        V((2, 2, 2, 4, 2, 32, WIDTH), BF16), V((2, 2, 4, 2, 32, WIDTH + 128), BF16),
+        *[V((2, 4, 2, *unit), BF16) for unit in units[1:]],
+        V((2, 4, 2, 2 * DOWN, 512), BF16), V((HALF, WIDTH), BF16), V((16, WIDTH), F32),
+        V((2, ROWS, WIDTH), BF16), V((2, 8, 128), F32), V((2, ROWS, ROWS), F32), act, act, V((ROWS, 512), BF16), act, act, act, V((ROWS, 128), F32),
+        V((ROWS, WIDTH), F32), V((2, ROWS, WIDTH), BF16), V((2, ROWS, WIDTH), BF16),
+        V((512, HALF), BF16), V((512, HALF), BF16), V((512, HALF), BF16), V((ROWS + 768, WIDTH), F32),
+        act, act, act,
+        V((ROWS, WIDTH), F32), act, act, act, act, act, V((ROWS, 512), BF16),
+        V((3, 2, 2, 4, 2, 32, WIDTH), BF16),
+        *[V((2, 4, *unit), BF16) for unit in units],
+        *[V((4, *unit), BF16) for unit in units],
+        *[V((3, *unit), BF16) for unit in units],
+        *[V(unit[1:], BF16) for unit in units[1:]],
+        V((3, 2, 4, 2, 32, WIDTH), BF16), V((3, 4, 2, 32, WIDTH), BF16),
+        V((3, 3, 2, 32, WIDTH), BF16), V((3, 32, WIDTH), BF16), V((8, WIDTH), F32), V((5, 8, WIDTH), F32),
+        pltpu.SemaphoreType.DMA((SLOTS.count,)), pltpu.SemaphoreType.DMA((SLOTS.count,)), pltpu.SemaphoreType.DMA((PUT + 8 + 2 * FFN,)),
+    ]
+    res = pl.pallas_call(
+        layer_kernel,
+        out_shape=outs,
+        in_specs=[hbm, smem, hbm, hbm, hbm, hbm, hbm, hbm, vmem, vmem, hbm, hbm, vmem],
+        out_specs=[hbm] * len(outs),
+        scratch_shapes=scratch,
+        compiler_params=pltpu.CompilerParams(
+            collective_id=0, has_side_effects=True, vmem_limit_bytes=63 * 2**20
+        ),
+    )(
+        tokens, seq_lengths, cotangent, w_query, w_latent, w_keyup, w_valup, w_output, norm_attn, norm_ffn,
+        w_gate, w_up, w_down,
+    )
+    final = [
+        shape((ROWS, WIDTH), BF16), shape((ROWS, WIDTH), F32), shape((32, WIDTH), F32), shape((32, 512), F32),
+        shape((16, 512), F32), shape((16, 512), F32), shape((32, WIDTH), F32), shape((1, 32), F32), shape((1, 32), F32),
+        shape((32, 2 * HALF), F32), shape((32, 2 * HALF), F32), shape((DOWN, WIDTH), F32),
+    ]
+    out = pl.pallas_call(
+        finish_kernel,
+        out_shape=final,
+        in_specs=[hbm] * 7,
+        out_specs=[hbm] * 12,
+        scratch_shapes=[
+            *[V(one.shape, one.dtype) for one in [*outs, *final[2:]]],
+            pltpu.SemaphoreType.DMA((7,)), pltpu.SemaphoreType.DMA((12,)),
+        ],
+    )(*res)
+    return tuple(out[:7]) + (out[7].reshape(32), out[8].reshape(32)) + tuple(out[9:])
+
+
 def solution(mesh):
+    fits = dict(mesh.shape) == {"dp": 4, "fsdp": 8}
     return jax.shard_map(
-        on_device,
+        kernel_on_device if fits else on_device,
         mesh=mesh,
         in_specs=(
             P(("dp", "fsdp"), None),

time: 1320 us -> 157 us (0.12)
  waiting for transfers between devices: 828 us -> 0 us
  blocking collectives: 219 us -> 0 us
  matrix products: 218 us -> 0 us
  Pallas kernels: 0 us -> 156 us
  other arithmetic: 17.2 us -> 0 us
  local copies, waits for them, and re-layouts: 15.2 us -> 0 us
  between operations: 14.2 us -> 0.86 us
    reduce_scatter x5 -> x0, waiting for transfers between devices: 688 us -> none  [the longest x1 248 us: on_device(): lax.psum_scatter(column_term(normed_two, packed_ffn), ('dp', 'fsdp'), sca...]
    dot_general x133 -> x0, matrix products: 218 us -> none  [the longest x37 74.4 us: matmul_left(): lax.dot_general(left, right, (((0,), (0,)), ((), ())), preferred_element_...]
    pallas_call x0 -> x2, Pallas kernels: none -> 156 us  [the longest x1 153 us: kernel_on_device(): pl.pallas_call(layer_kernel, out_shape=outs, in_specs=[hbm, smem, hbm, hb...]
    all_gather x2 -> x0, blocking collectives: 137 us -> none  [the longest x1 69.7 us: on_device(): lax.all_gather(w_keyup, ('dp', 'fsdp'), axis=0, tiled=True)]
    all_gather x6 -> x0, waiting for transfers between devices: 136 us -> none  [the longest x1 63.1 us: on_device(): lax.all_gather(w_down, ('dp', 'fsdp'), axis=0, tiled=True)]
    unnamed x2 -> x0, blocking collectives: 82.1 us -> none
  transfers between devices with their start and end apart: 11 -> 0, of which waited for: 8 -> 0; matrix products, arithmetic and copies ran while one was open for 8% -> 0% of each run, Pallas kernels for 0% -> 0%
where the time goes in v3:
time: 157 us
  Pallas kernels  156 us (99%)
    pallas_call x1, Pallas kernels, kernel_on_device(): pl.pallas_call(layer_kernel, out_shape=outs, in_specs=[hbm, smem, hbm, hb...  153 us

profile of v3, /device:TPU:0, one launch (start us, length us, event | category | flops | bytes accessed | tf_op | source)
XLA Modules:
  0.0 157.0 jit_solution(5154877459728470983)
XLA Ops:
  0.6 153.1 %shard_map.220 = (bf16[256,1024]{1,0:T(8,128)(2,1)}, f32[256,1024]{1,0:T(8,128)}, bf16[3,32,1024]{2,1,0:T(8,128)(2,1)}, f32[8,128]{1,0:T(8,128)}, bf16[2,32,1408...) custom-call(bf16[256,1024]{1,0:T(8,128)(2,1)} %tok_hbm.1, s32[4]{0:T(128)} %len_ref.1, ...), custom_call_target="tpu_custom_call" | custom-call | tf_op jit(solution)/shard_map/pallas_call | solution.py:1373
  153.8 3.0 %shard_map.221 = (bf16[256,1024]{1,0:T(8,128)(2,1)}, f32[256,1024]{1,0:T(8,128)}, f32[32,1024]{1,0:T(8,128)}, f32[32,512]{1,0:T(8,128)}, f32[16,512]{1,0:T(8,128...) custom-call(bf16[256,1024]{1,0:T(8,128)(2,1)} %get-tuple-element.31., ...), custom_call_target="tpu_custom_call" | custom-call | tf_op jit(solution)/shard_map/pallas_call | solution.py:1391

commit v4 on v3

--- a/solution.py
+++ b/solution.py
@@ -1,3 +1,5 @@
+import math
+
 import jax
 import jax.numpy as jnp
 from jax import lax
@@ -290,7 +292,7 @@
 HALF = 1408
 PARTS = (768, 640)
 FFN = 1 + 2 * len(PARTS)
-PUT = 20
+PUT = 3
 DOWN = 88
 
 
@@ -309,10 +311,10 @@
 
 
 SLOTS = Slots()
-S_A = [SLOTS.take(32) for _ in range(4)]
+S_A = [SLOTS.take(16) for _ in range(4)]
 S_HALF = SLOTS.take(FFN)
-S_F = [SLOTS.take(16) for _ in range(FFN)]
-S_COT, S_TOK, S_DN2, S_OUT, S_END = (SLOTS.take(n) for n in (4, 4, 1, 4, 1))
+S_F = [SLOTS.take(8) for _ in range(FFN)]
+S_COT, S_TOK, S_DN2, S_OUT, S_END = (SLOTS.take(1) for _ in range(5))
 S_R = [SLOTS.take(10) for _ in range(FFN + 4)]
 S_SUM = SLOTS.take(5)
 
@@ -558,38 +560,38 @@
     def line(dh, dl):
         return rel(zh, dh) * 2 + rel(zl, dl)
 
-    sent = {}
-    now = {"op": None, "wait": None}
-
-    def copy(src, dst, slot, target):
+    sent, groups = {}, []
+
+    def copy(src, dst, slot, target, group):
+        if group not in groups:
+            groups.append(group)
         return pltpu.make_async_remote_copy(
-            src_ref=src, dst_ref=dst, send_sem=send_sem.at[slot], recv_sem=recv_sem.at[slot],
+            src_ref=src, dst_ref=dst, send_sem=send_sem.at[groups.index(group)], recv_sem=recv_sem.at[slot],
             device_id=target, device_id_type=MESH,
         )
 
     def send(group, src, dst, slot, target):
-        if now["wait"] is None:
-            copy(src, dst, slot, target).start()
-            users = sent.setdefault(group, [])
-            if now["op"] not in users:
-                users.append(now["op"])
-        elif now["wait"] == group:
-            copy(src, dst, slot, target).wait_send()
+        copy(src, dst, slot, target, group).start()
+        sent[group] = sent.get(group, 0) + math.prod(src.shape) * src.dtype.itemsize
+
+    def drain(group):
+        tiles = sent.pop(group, 0) // 4096
+        if tiles:
+            wide = next(n for n in range(8, 0, -1) if tiles % n == 0 and tiles // n <= 128)
+            size = tmp.at[pl.ds(0, tiles // wide * 8), pl.ds(0, wide * 128)]
+            copy(size, size, 0, sib, group).wait_send()
 
     def arrive(dst, slot):
-        if now["wait"] is None:
-            copy(dst, dst, slot, sib).wait_recv()
+        copy(dst, dst, slot, sib, "sum").wait_recv()
 
     def local(src, dst, k):
         return pltpu.make_async_copy(src, dst, local_sem.at[k])
 
     def put(src, dst, k):
-        if now["wait"] is None:
-            local(src, dst, k).start()
+        local(src, dst, k).start()
 
     def add(dst, src):
-        if now["wait"] is None:
-            dst[...] = dst[...] + src[...]
+        dst[...] = dst[...] + src[...]
 
     def cols(n, width=256):
         return pl.ds(pl.multiple_of(n * width, width), width)
@@ -603,15 +605,9 @@
 
         return enter
 
-    def run(items, wait=None):
-        now["wait"] = wait
+    def run(items):
         for name, *rest in items:
-            now["op"] = (name, *rest)
             ops[name](*rest)
-        now["wait"] = None
-
-    def drain(group):
-        run(sent.pop(group, []), group)
 
     def gap(name):
         run(PLAN.get(name, ()))
@@ -648,7 +644,7 @@
 
     def a_send(w, bits, k):
         blk = a_blk(w, bits)
-        send("attn", blk, blk, S_A[w] + bits + (1 << k), ways[ROUTE[w][k]])
+        send("a%d" % w, blk, blk, S_A[w] + (bits + (1 << k) if k < 4 else 0), ways[ROUTE[w][k]])
 
     @op(AA)
     def aa(w, bits):
@@ -662,8 +658,9 @@
 
     @op(AT)
     def at(w):
-        for bits in range(16, 32):
-            arrive(a_blk(w, bits), S_A[w] + bits)
+        other = 1 - c
+        half = pl.ds(512 * (w - 2), 512)
+        arrive((latw.at[:, other], attn.at[0, :, other], attn.at[1, :, other, :, :, :, half])[min(w, 2)], S_A[w])
 
     ffn = (down_w, gate_a, up_a, gate_b, up_b)
     ffn_hbm = (None, wg_hbm, wu_hbm, wg_hbm, wu_hbm)
@@ -685,7 +682,7 @@
 
     def f_send(t, bits, k):
         blk = f_blk(t, bits)
-        send("ffn%d" % t, blk, blk, S_F[t] + bits + (1 << k), (z2, z1, yp, sib)[k])
+        send("ffn%d" % t, blk, blk, S_F[t] + (bits + (1 << k) if k < 3 else 0), (z2, z1, yp, sib)[k])
 
     @op(FA)
     def fa(t, bits):
@@ -699,29 +696,26 @@
 
     @op(FT)
     def ft(t):
-        for bits in range(8, 16):
-            arrive(f_blk(t, bits), S_F[t] + bits)
+        arrive(ffn[t].at[1 - c], S_F[t])
 
     def quarter(ref, k):
         return ref.at[pl.ds(k * 64, 64)]
 
     @op(COT_S)
     def cot_s(k):
-        send("cot", quarter(dout.at[x], k), quarter(dout.at[x], k), S_COT + k, xp)
+        send("cot", quarter(dout.at[x], k), quarter(dout.at[x], k), S_COT, xp)
 
     @op(COT_R)
     def cot_r():
-        for k in range(4):
-            arrive(quarter(dout.at[1 - x], k), S_COT + k)
+        arrive(dout.at[1 - x], S_COT)
 
     @op(TOK_S)
     def tok_s(k):
-        send("tok", quarter(tok.at[x], k), quarter(tok.at[x], k), S_TOK + k, xp)
+        send("tok", quarter(tok.at[x], k), quarter(tok.at[x], k), S_TOK, xp)
 
     @op(TOK_R)
     def tok_r():
-        for k in range(4):
-            arrive(quarter(tok.at[1 - x], k), S_TOK + k)
+        arrive(tok.at[1 - x], S_TOK)
 
     @op(END_S)
     def end_s():
@@ -741,12 +735,11 @@
 
     @op(OUT_S)
     def out_s(k):
-        send("out", quarter(snd_out, k), quarter(rcv_out, k), S_OUT + k, xp)
+        send("out", quarter(snd_out, k), quarter(rcv_out, k), S_OUT, xp)
 
     @op(OUT_R)
     def out_r():
-        for k in range(4):
-            arrive(quarter(rcv_out, k), S_OUT + k)
+        arrive(rcv_out, S_OUT)
 
     ffn_s = (s_d, s_ga, s_ua, s_gb, s_ub)
     ffn_y = (y_d, y_ga, y_ua, y_gb, y_ub)
@@ -813,7 +806,7 @@
     def r_go(i):
         for other in (1, 0):
             k, src, dst, _ = sib_part(i, other)
-            send("r", src, dst, S_R[i] + k, sib)
+            send("r%d" % i, src, dst, S_R[i] + k, sib)
 
     @op(R_S)
     def r_s(i, other):
@@ -828,7 +821,7 @@
         d = line(bits >> 1, bits & 1)
         add(*sib_part(i, 1)[3](d))
         target, src, buf = first_hop(i, d)
-        send("r", src, buf, S_R[i] + 2 + bits, target)
+        send("r%d" % i, src, buf, S_R[i] + 2 + bits, target)
 
     @op(R_A)
     def r_a(i, bits):
@@ -837,7 +830,7 @@
         arrive(buf, S_R[i] + 2 + bits)
         add(line_blk(i, d), buf)
         if bits & 1:
-            send("r", line_blk(i, d), line_buf(i, bits >> 1), S_R[i] + 6 + (bits >> 1), z1)
+            send("r%d" % i, line_blk(i, d), line_buf(i, bits >> 1), S_R[i] + 6 + (bits >> 1), z1)
 
     @op(R_1)
     def r_1(i, dh):
@@ -845,7 +838,7 @@
         arrive(line_buf(i, dh), S_R[i] + 6 + dh)
         add(line_blk(i, d), line_buf(i, dh))
         if dh:
-            send("r", line_blk(i, d), line_buf(i, 2), S_R[i] + 8, z2)
+            send("r%d" % i, line_blk(i, d), line_buf(i, 2), S_R[i] + 8, z2)
 
     @op(R_2)
     def r_2(i):
@@ -858,7 +851,7 @@
             put(down_w.at[c, z, y], gd_hbm, PUT)
             return
         target, src, buf = last_hop(i)
-        send("r", src, buf, S_R[i] + 9, target)
+        send("r%d" % i, src, buf, S_R[i] + 9, target)
         if i < FFN:
             put(ffn[i].at[c, z, y, x], ffn_out[i].at[x, :, out_cols[i]], PUT + i * 2)
 
@@ -887,11 +880,11 @@
 
     @op(SUM_S)
     def sum_s(i):
-        copy(sum_own, sum_rcv.at[i], S_SUM + i, sum_to[i]).start()
+        copy(sum_own, sum_rcv.at[i], S_SUM + i, sum_to[i], "sum").start()
 
     @op(SUM_R)
     def sum_r(i):
-        copy(sum_own, sum_rcv.at[i], S_SUM + i, sum_to[i]).wait_send()
+        copy(sum_own, sum_rcv.at[i], S_SUM + i, sum_to[i], "sum").wait_send()
         arrive(sum_rcv.at[i], S_SUM + i)
         add(sum_own, sum_rcv.at[i])
 
@@ -1368,7 +1361,7 @@
         *[V(unit[1:], BF16) for unit in units[1:]],
         V((3, 2, 4, 2, 32, WIDTH), BF16), V((3, 4, 2, 32, WIDTH), BF16),
         V((3, 3, 2, 32, WIDTH), BF16), V((3, 32, WIDTH), BF16), V((8, WIDTH), F32), V((5, 8, WIDTH), F32),
-        pltpu.SemaphoreType.DMA((SLOTS.count,)), pltpu.SemaphoreType.DMA((SLOTS.count,)), pltpu.SemaphoreType.DMA((PUT + 8 + 2 * FFN,)),
+        pltpu.SemaphoreType.DMA((2 * FFN + 14,)), pltpu.SemaphoreType.DMA((SLOTS.count,)), pltpu.SemaphoreType.DMA((PUT + 8 + 2 * FFN,)),
     ]
     res = pl.pallas_call(
         layer_kernel,

time: 157 us -> 153 us (0.975)
  Pallas kernels: 156 us -> 152 us
    pallas_call x1, Pallas kernels: 153 us -> 149 us  [kernel_on_device(): pl.pallas_call(layer_kernel, out_shape=outs, in_specs=[hbm, smem, hbm, hb...]
where the time goes in v4:
time: 153 us
  Pallas kernels  152 us (99%)
    pallas_call x1, Pallas kernels, kernel_on_device(): pl.pallas_call(layer_kernel, out_shape=outs, in_specs=[hbm, smem, hbm, hb...  149 us

profile of v4, /device:TPU:0, one launch (start us, length us, event | category | flops | bytes accessed | tf_op | source)
XLA Modules:
  0.0 153.1 jit_solution(17075233374947478477)
XLA Ops:
  0.6 149.2 %shard_map.220 = (bf16[256,1024]{1,0:T(8,128)(2,1)}, f32[256,1024]{1,0:T(8,128)}, bf16[3,32,1024]{2,1,0:T(8,128)(2,1)}, f32[8,128]{1,0:T(8,128)}, bf16[2,32,1408...) custom-call(bf16[256,1024]{1,0:T(8,128)(2,1)} %tok_hbm.1, s32[4]{0:T(128)} %len_ref.1, ...), custom_call_target="tpu_custom_call" | custom-call | tf_op jit(solution)/shard_map/pallas_call | solution.py:1366
  149.9 3.0 %shard_map.221 = (bf16[256,1024]{1,0:T(8,128)(2,1)}, f32[256,1024]{1,0:T(8,128)}, f32[32,1024]{1,0:T(8,128)}, f32[32,512]{1,0:T(8,128)}, f32[16,512]{1,0:T(8,128...) custom-call(bf16[256,1024]{1,0:T(8,128)(2,1)} %get-tuple-element.31., ...), custom_call_target="tpu_custom_call" | custom-call | tf_op jit(solution)/shard_map/pallas_call | solution.py:1384

commit v5 on v4

--- a/solution.py
+++ b/solution.py
@@ -297,7 +297,7 @@
 
 
 ROUTE = ("y21xs", "y21xs", "21xys", "21yxs")
-SUM_X_FIRST = (True, False, True, True)
+SUM_X_FIRST = (True, True, True, True)
 
 
 class Slots:
@@ -337,193 +337,196 @@
 ) = range(28)
 (
     G_START, G_WEIGHTS, G_ACROSS, G_DOWN_W, G_QUERY, G_OUTPUT_W, G_FFN_A, G_FFN_B, G_BACK, G_RESULT,
-    G_TAIL, G_MASK, G_NORM, G_LATENT, G_KEYS, G_NORM_P, G_LATENT_P, G_KEYS_P, G_COMPACT, G_ATTEND,
-    G_QUERY_P, G_ATTEND_P, G_MIDDLE, G_NORM2, G_MIDDLE_P, G_NORM2_P, G_HIDDEN_A, G_DN_A, G_GATEUP_A,
-    G_DN_B, G_HIDDEN_B, G_DOWN, G_GATEUP_B, G_OUT, G_OUTPUT, G_ATTENDB, G_PROJQ, G_PROJL, G_DNORMED,
-    G_NORM1B, G_GAIN, G_NORM2B, G_DMERGED, G_LATENTB,
+    G_TAIL, G_MASK, G_GAIN, G_NORM, G_LATENT, G_KEYS, G_NORM_P, G_LATENT_P, G_KEYS_P, G_COMPACT,
+    G_ATTEND, G_QUERY_P, G_ATTEND_P, G_MIDDLE, G_NORM2, G_MIDDLE_P, G_NORM2_P, G_HIDDEN_A, G_DN_A,
+    G_GATEUP_A, G_DN_B, G_DOWN, G_GATEUP_B, G_OUT, G_DMERGED, G_OUTPUT, G_ATTENDB, G_PROJQ, G_PROJL,
+    G_DNORMED, G_NORM1B, G_HIDDEN_B, G_NORM2B, G_LATENTB,
 ) = range(44)
 PLAN = {
     G_START: (
-        (H_S, 2), (AA, 2, 0), (AG, 2, 0, 1), (H_S, 1), (H_S, 4), (H_S, 3), (FA, 0, 0), (AA, 0, 0),
+        (H_S, 1), (AA, 2, 0), (AG, 2, 0, 1), (FA, 0, 0), (AA, 0, 0), (AA, 1, 0), (FG, 0, 0, 0),
+        (AG, 0, 0, 0), (FG, 0, 0, 2),
     ),
     (G_MASK, 3): (
-        (TOK_S, 2), (AA, 1, 0), (FG, 0, 0, 0), (FG, 0, 0, 1),
+        (AG, 2, 0, 2), (H_S, 2), (FG, 0, 0, 1), (TOK_S, 1), (AA, 0, 1), (TOK_S, 3), (H_S, 4),
     ),
     G_WEIGHTS: (
-        (AG, 1, 0, 0), (AG, 0, 0, 1), (H_R, 4), (AG, 0, 0, 2), (TOK_S, 1), (TOK_S, 0), (AA, 3, 0),
-        (FA, 4, 0), (AG, 0, 0, 0), (AA, 0, 1), (AG, 2, 0, 0), (AA, 1, 1), (AG, 3, 0, 1), (H_R, 2),
-        (H_R, 1), (TOK_S, 3), (FG, 0, 0, 2), (AG, 0, 1, 1), (FA, 0, 1), (FG, 0, 1, 2), (AG, 0, 1, 2),
-        (FA, 0, 2), (H_R, 3), (AG, 3, 0, 0), (AG, 0, 1, 3), (AA, 2, 1), (FA, 1, 0), (AA, 0, 2),
-        (AG, 0, 2, 2), (AG, 0, 0, 3), (AG, 2, 1, 2), (AG, 2, 1, 1), (FG, 1, 0, 2), (AA, 0, 3),
-        (FA, 2, 0), (AA, 3, 2), (AG, 1, 0, 1), (AG, 1, 0, 3), (FG, 2, 0, 2), (AG, 2, 1, 3),
-        (AG, 0, 2, 3), (AG, 3, 0, 2), (AA, 0, 4), (AG, 1, 0, 2), (AA, 2, 5), (FG, 4, 0, 2),
-        (AG, 0, 3, 2), (AA, 2, 2), (FA, 3, 0), (AG, 0, 3, 3), (AG, 1, 1, 1), (FA, 2, 4),
-        (FG, 0, 1, 1), (AG, 2, 5, 3), (AA, 1, 8), (FG, 1, 0, 0), (AA, 3, 1), (AA, 0, 8), (AA, 2, 3),
-        (AG, 2, 0, 2), (AG, 0, 4, 3), (FA, 0, 5), (AG, 1, 1, 2), (FG, 0, 2, 2), (AA, 0, 6),
-        (AA, 0, 5), (AG, 3, 1, 2), (AG, 0, 6, 3), (AA, 0, 7), (FA, 0, 4), (AA, 0, 11), (AG, 0, 5, 3),
-        (AG, 2, 3, 2), (AA, 0, 9), (AA, 3, 4), (AA, 1, 2), (AG, 3, 2, 2), (FA, 1, 4), (AA, 1, 3),
-        (AG, 3, 1, 1), (AG, 0, 7, 3), (AA, 0, 13), (AG, 2, 2, 3), (AG, 1, 1, 3), (AA, 1, 4),
-        (AA, 2, 9), (AA, 2, 4), (AG, 1, 2, 3), (AG, 1, 2, 2), (AG, 2, 2, 2), (AA, 2, 7), (AA, 2, 13),
-        (END_S,), (AA, 0, 10), (FA, 0, 3), (FG, 0, 3, 2), (AA, 0, 12), (AG, 1, 3, 2), (FA, 4, 4),
-        (AA, 0, 15), (FG, 2, 0, 0), (AA, 0, 14), (AG, 1, 3, 3), (TOK_R,), (AT, 0), (FG, 3, 0, 2),
-        (AA, 2, 10), (AA, 1, 5), (FA, 1, 1), (AG, 1, 4, 3), (FG, 1, 0, 1),
+        (AG, 0, 0, 1), (AG, 0, 0, 2), (AG, 0, 1, 3), (AG, 1, 0, 3), (H_R, 2), (H_S, 3),
+        (AG, 0, 0, 3), (AA, 3, 0), (AG, 3, 0, 1), (AG, 1, 0, 0), (FA, 0, 2), (FA, 0, 1),
+        (FG, 0, 2, 2), (TOK_S, 2), (AG, 2, 0, 0), (FG, 0, 1, 2), (AA, 0, 2), (AG, 0, 1, 2),
+        (AA, 0, 4), (H_R, 1), (AG, 0, 1, 1), (AG, 0, 2, 2), (AA, 2, 2), (AA, 3, 2), (H_R, 3),
+        (AG, 3, 0, 2), (AG, 0, 4, 3), (AG, 1, 0, 1), (AA, 2, 4), (AA, 1, 1), (AA, 0, 8),
+        (AG, 1, 1, 3), (FG, 0, 1, 1), (AA, 0, 5), (AG, 3, 0, 0), (AG, 2, 2, 2), (FA, 1, 0),
+        (AA, 0, 3), (AG, 0, 3, 3), (FA, 2, 0), (AG, 1, 1, 1), (H_R, 4), (FG, 1, 0, 2), (AG, 3, 2, 2),
+        (AG, 0, 3, 2), (AG, 0, 2, 3), (AG, 0, 5, 3), (TOK_S, 0), (AA, 0, 12), (AG, 2, 0, 3),
+        (AA, 0, 6), (AA, 2, 6), (FG, 2, 0, 2), (AA, 2, 1), (AG, 2, 1, 3), (AG, 1, 0, 2), (FA, 0, 3),
+        (AG, 2, 4, 3), (AG, 2, 1, 1), (AA, 1, 2), (AG, 0, 6, 3), (AA, 3, 1), (FA, 1, 4), (FA, 3, 0),
+        (AG, 1, 1, 2), (FG, 0, 3, 2), (AA, 0, 7), (AG, 3, 1, 1), (FG, 3, 0, 2), (FA, 4, 0),
+        (AG, 0, 7, 3), (AA, 3, 4), (AA, 2, 12), (AA, 1, 3), (AA, 0, 9), (FA, 0, 4), (FG, 2, 0, 0),
+        (FA, 0, 6), (AA, 1, 4), (AG, 1, 2, 2), (AA, 0, 10), (AG, 2, 1, 2), (AA, 0, 11), (AA, 0, 13),
+        (END_S,), (FA, 0, 5), (AA, 2, 3), (AG, 1, 3, 3), (AA, 0, 14), (AG, 3, 1, 2), (AG, 2, 2, 3),
+        (AG, 1, 3, 2), (AA, 1, 8), (AA, 1, 5), (AG, 2, 3, 3), (FG, 2, 0, 1), (AG, 1, 4, 3),
+        (AG, 2, 3, 2), (FG, 1, 0, 0), (FG, 4, 0, 2), (AA, 0, 15), (AA, 3, 6), (AG, 2, 6, 3),
+        (AA, 2, 5), (TOK_R,), (AT, 0),
+    ),
+    (G_GAIN, 7): (
+        (AA, 3, 5), (AG, 1, 2, 3),
     ),
     (G_NORM, 3): (
-        (AA, 3, 3), (AA, 3, 5), (AG, 2, 3, 3), (AG, 2, 4, 3),
+        (AA, 1, 6), (FA, 0, 7), (FG, 1, 0, 1), (AA, 2, 8), (FA, 2, 1), (AG, 1, 6, 3), (FG, 2, 1, 2),
     ),
     (G_LATENT, 1): (
-        (FG, 4, 0, 0), (AA, 1, 6), (AG, 1, 5, 3), (AA, 3, 6),
+        (AA, 1, 11), (AA, 2, 14), (AG, 2, 5, 3), (END_R,), (AG, 1, 5, 3), (FT, 0), (FA, 3, 4),
+        (AA, 3, 3), (AA, 2, 7), (FG, 3, 0, 0), (AA, 1, 7), (AG, 1, 7, 3),
     ),
     (G_KEYS, 1): (
-        (AG, 3, 3, 2), (FA, 0, 6), (AG, 2, 7, 3),
+        (AG, 3, 3, 3), (AG, 3, 4, 3),
     ),
     G_ACROSS: (
-        (AA, 2, 6), (FA, 0, 7), (AA, 1, 7), (AG, 1, 6, 3), (FG, 2, 0, 1), (FG, 1, 1, 1),
-        (FG, 1, 1, 2), (END_R,), (AA, 1, 9),
+        (AG, 3, 3, 2), (AG, 2, 7, 3),
     ),
     (G_NORM_P, 3): (
-        (AG, 1, 7, 3), (FT, 0),
+        (FA, 2, 2), (AA, 1, 14), (FG, 2, 1, 1), (FG, 2, 2, 2), (AG, 3, 1, 3), (AA, 1, 9),
     ),
     (G_LATENT_P, 1): (
-        (AA, 1, 12), (AA, 3, 7), (AG, 2, 0, 3), (AG, 3, 0, 3),
+        (AA, 1, 12),
     ),
     (G_KEYS_P, 1): (
-        (AG, 3, 5, 3), (FA, 2, 1), (AA, 1, 14),
+        (AA, 3, 7), (AA, 2, 11), (FA, 1, 1), (AA, 1, 10), (AG, 3, 2, 3), (AA, 1, 15), (FG, 1, 1, 2),
+        (AA, 1, 13), (FA, 2, 4), (AG, 3, 0, 3), (FG, 1, 1, 1), (AG, 3, 5, 3), (AG, 3, 7, 3),
     ),
     G_DOWN_W: (
-        (AA, 1, 11), (AG, 3, 4, 3), (AG, 3, 3, 3), (FG, 3, 0, 0), (FG, 2, 1, 2), (FG, 2, 1, 1),
-        (AA, 1, 13), (AG, 2, 6, 3),
+        (FG, 4, 0, 0), (AG, 3, 6, 3), (AA, 2, 13),
     ),
     (G_COMPACT, 7): (
-        (FG, 3, 0, 1), (AG, 3, 7, 3),
+        (FA, 1, 2), (COT_S, 2), (AT, 1),
     ),
     G_QUERY: (
-        (AG, 3, 6, 3), (AA, 1, 15), (AA, 1, 10), (FA, 1, 5), (AG, 3, 2, 3), (FA, 1, 2),
-        (FG, 1, 2, 2), (AG, 3, 1, 3), (AA, 2, 8), (COT_S, 2), (COT_S, 1), (AT, 1), (FA, 4, 1),
-        (AA, 2, 15), (AA, 2, 11),
+        (FG, 1, 2, 2), (FA, 2, 5), (FG, 3, 0, 1),
     ),
     (G_QUERY, 3): (
-        (AA, 2, 12),
+        (FA, 3, 1),
     ),
     (G_ATTEND, 3): (
-        (AA, 2, 14), (FG, 4, 1, 2), (AA, 3, 8), (AA, 3, 13),
+        (FG, 3, 1, 2), (COT_S, 0),
     ),
     (G_ATTEND, 7): (
-        (FA, 1, 3), (FG, 1, 3, 2), (FG, 4, 0, 1), (AA, 3, 12), (AA, 3, 10), (FA, 2, 2),
+        (FG, 3, 1, 1), (FA, 2, 3), (FA, 4, 4), (AA, 2, 10), (COT_S, 3), (FG, 4, 0, 1), (FG, 2, 3, 2),
+        (AA, 3, 13), (AA, 2, 15), (AA, 3, 14),
     ),
     (G_QUERY_P, 3): (
-        (FA, 1, 6), (AT, 2), (FG, 4, 1, 1), (AA, 3, 14), (FA, 2, 5), (AA, 3, 15), (COT_S, 3),
-        (AA, 3, 11), (FG, 2, 2, 2), (FA, 3, 1), (AA, 3, 9), (FG, 3, 1, 1),
+        (FA, 1, 3), (AA, 3, 15), (AA, 3, 9), (FG, 1, 3, 2),
     ),
     (G_ATTEND_P, 3): (
-        (FA, 2, 3), (AT, 3), (FG, 2, 3, 2),
+        (FA, 4, 1), (FA, 1, 6), (FA, 2, 6), (FG, 4, 1, 1), (AA, 3, 11), (FA, 3, 5), (AA, 3, 12),
+        (AA, 3, 10), (FG, 4, 1, 2), (AA, 3, 8), (COT_S, 1), (AA, 2, 9),
     ),
     G_OUTPUT_W: (
-        (COT_S, 0), (FA, 1, 7),
+        (AT, 3), (AT, 2),
     ),
     (G_MIDDLE, 3): (
-        (FA, 3, 2), (FG, 3, 2, 2),
+        (FA, 3, 3), (FA, 1, 7), (FA, 2, 7), (FG, 3, 3, 2),
     ),
     (G_NORM2, 3): (
-        (FG, 3, 1, 2), (FA, 4, 5), (FA, 2, 6), (FA, 4, 2),
+        (FA, 3, 2), (FA, 1, 5), (FG, 3, 2, 2),
     ),
     (G_MIDDLE_P, 3): (
-        (FA, 2, 7), (FG, 4, 2, 2),
+        (FA, 4, 2),
     ),
     (G_NORM2_P, 3): (
-        (FA, 3, 4), (FT, 1),
+        (FT, 2), (FT, 1), (FA, 4, 3), (FA, 4, 5),
     ),
     G_FFN_A: (
-        (FT, 2),
+        (FG, 4, 3, 2),
     ),
     (G_HIDDEN_A, 0): (
-        (FA, 3, 3), (FA, 4, 3), (FG, 3, 3, 2), (COT_R,),
-    ),
-    (G_DN_A, 0): (
-        (FG, 4, 3, 2),
+        (FG, 4, 2, 2), (FA, 3, 7), (COT_R,),
+    ),
+    (G_HIDDEN_A, 1): (
+        (FA, 3, 6),
+    ),
+    (G_DN_A, 1): (
+        (FA, 4, 7),
     ),
     (G_GATEUP_A, 1): (
-        (R_GO, 1), (FA, 3, 5),
-    ),
-    (G_GATEUP_A, 3): (
-        (FA, 4, 6), (FA, 3, 7), (FA, 3, 6), (R_S, 1, 1), (R_B, 1, 3),
+        (FA, 4, 6), (R_GO, 1), (R_GO, 2),
     ),
     G_FFN_B: (
-        (R_B, 1, 1), (FA, 4, 7), (R_B, 1, 2), (R_S, 1, 0), (R_GO, 2), (FT, 3), (FT, 4),
+        (FT, 4), (FT, 3), (R_S, 1, 1), (R_B, 1, 3),
     ),
     (G_DN_B, 1): (
-        (DN2_S,), (R_S, 2, 1),
-    ),
-    (G_HIDDEN_B, 0): (
-        (R_B, 2, 3),
+        (R_S, 2, 1), (DN2_S,), (R_B, 1, 1), (R_S, 1, 0), (R_B, 2, 3),
     ),
     (G_DN_B, 0): (
-        (R_B, 2, 1), (R_A, 1, 3),
+        (R_A, 1, 3),
     ),
     (G_DOWN, 0): (
-        (R_GO, 0), (R_A, 1, 1), (R_S, 2, 0),
+        (R_GO, 0), (R_B, 1, 2),
+    ),
+    (G_DOWN, 1): (
+        (R_A, 1, 1), (R_S, 2, 0), (R_S, 0, 1), (R_B, 0, 3),
     ),
     (G_GATEUP_B, 1): (
-        (R_S, 0, 1), (R_GO, 3), (R_B, 0, 3), (R_A, 2, 3), (R_A, 1, 2), (R_GO, 4), (R_S, 0, 0),
+        (R_A, 2, 3), (R_GO, 4), (R_B, 2, 1),
     ),
     (G_GATEUP_B, 3): (
-        (R_S, 3, 1), (R_A, 2, 1),
+        (R_A, 1, 2), (R_GO, 3), (R_B, 2, 2), (R_S, 0, 0), (R_1, 1, 1),
     ),
     (G_OUT, 0): (
-        (R_B, 2, 2), (OUT_S, 1), (OUT_S, 2), (R_S, 4, 1), (R_1, 1, 1), (R_B, 3, 1), (R_S, 3, 0),
+        (R_S, 4, 1), (OUT_S, 0), (OUT_S, 2),
     ),
     (G_OUT, 1): (
-        (R_B, 3, 3), (R_B, 0, 2), (OUT_S, 0), (R_B, 4, 3), (R_A, 0, 3), (R_B, 1, 0),
+        (R_B, 4, 3), (R_S, 4, 0), (OUT_S, 3), (R_A, 0, 3), (R_S, 3, 0),
     ),
     G_BACK: (
-        (DN2_R,),
-    ),
-    (G_OUTPUT, 1): (
-        (R_A, 2, 2), (R_1, 2, 1), (OUT_S, 3),
+        (DN2_R,), (R_S, 3, 1),
+    ),
+    (G_DMERGED, 3): (
+        (R_B, 3, 3), (R_A, 2, 1),
     ),
     (G_OUTPUT, 3): (
-        (R_GO, 5),
+        (R_B, 4, 1), (R_A, 2, 2), (R_B, 4, 0), (R_B, 3, 1), (R_GO, 5), (R_1, 2, 1), (R_B, 4, 2),
     ),
     (G_ATTENDB, 3): (
-        (R_A, 3, 1), (R_A, 3, 3),
+        (R_S, 5, 1), (R_B, 5, 3), (R_B, 0, 2), (R_B, 1, 0), (R_A, 3, 3), (R_A, 4, 3),
+    ),
+    (G_ATTENDB, 7): (
+        (R_B, 0, 1),
     ),
     (G_PROJQ, 1): (
-        (R_S, 5, 1), (R_A, 0, 2),
+        (R_A, 4, 1), (R_B, 5, 1), (R_S, 5, 0), (R_B, 5, 2),
     ),
     (G_PROJQ, 3): (
-        (R_B, 5, 1), (R_1, 0, 1), (R_S, 4, 0), (R_A, 4, 3), (R_B, 4, 1),
-    ),
-    (G_PROJL, 1): (
-        (R_B, 5, 3), (R_B, 4, 2), (R_S, 5, 0), (R_GO, 6), (R_B, 3, 2),
+        (R_GO, 6), (R_A, 5, 3),
     ),
     (G_PROJL, 3): (
-        (R_GO, 7), (R_B, 2, 0), (OUT_R,), (R_A, 5, 1), (R_B, 5, 0),
+        (R_B, 3, 0), (R_S, 6, 1),
     ),
     (G_DNORMED, 3): (
-        (R_S, 6, 1),
+        (R_A, 4, 2), (R_GO, 7), (R_1, 4, 1), (R_B, 6, 3),
     ),
     (G_NORM1B, 7): (
-        (R_B, 4, 0), (R_B, 3, 0), (R_A, 4, 2), (R_A, 5, 3), (R_GO, 8), (R_S, 7, 1), (R_S, 8, 0),
-        (R_B, 6, 3), (R_A, 1, 0),
+        (R_GO, 8), (R_A, 5, 1), (R_S, 8, 1), (SUM_S, 0), (R_A, 4, 0), (R_B, 3, 2), (R_S, 7, 1),
+        (R_A, 0, 2), (R_B, 5, 0), (R_A, 5, 2), (R_1, 5, 1), (R_1, 0, 1), (R_B, 2, 0), (R_B, 6, 2),
+        (R_B, 6, 1), (R_B, 7, 3), (R_S, 6, 0), (R_B, 7, 0), (SUM_R, 0), (R_1, 4, 0), (SUM_S, 1),
+        (R_A, 3, 1), (R_A, 6, 3), (R_A, 5, 0), (R_A, 6, 1), (R_1, 5, 0), (R_B, 7, 2), (R_B, 0, 0),
+        (R_A, 3, 2), (R_A, 6, 2),
     ),
     G_RESULT: (
-        (R_1, 4, 1), (R_1, 1, 0), (R_A, 4, 1), (R_B, 5, 2), (R_B, 6, 2), (R_B, 7, 1), (R_A, 2, 0),
+        (R_B, 8, 3), (R_B, 7, 1), (R_S, 8, 0), (R_2, 4), (R_2, 5), (SUM_R, 1), (R_A, 3, 0), (SUM_S, 2),
+        (R_1, 3, 1), (R_A, 1, 0), (R_A, 8, 3), (R_B, 6, 0), (R_B, 8, 2), (R_S, 7, 0), (R_1, 6, 1),
+        (R_A, 7, 0), (R_A, 2, 0), (R_A, 7, 2), (R_1, 2, 0), (R_1, 1, 0), (R_L, 5), (R_A, 7, 3),
+        (SUM_R, 2), (R_A, 7, 1), (R_B, 8, 1), (R_1, 3, 0), (R_L, 4), (R_A, 6, 0), (R_2, 2),
+        (OUT_S, 1), (R_1, 7, 1), (R_A, 0, 0), (R_A, 8, 1), (R_1, 6, 0), (R_2, 1), (R_A, 8, 2),
+        (R_2, 6), (R_B, 8, 0), (R_E, 4), (R_1, 8, 1), (R_L, 2), (SUM_S, 3), (R_2, 3), (R_1, 7, 0),
+        (R_2, 7), (R_L, 6), (R_A, 0, 1), (R_A, 8, 0), (R_L, 3), (R_1, 8, 0), (SUM_R, 3), (R_L, 7),
+        (R_E, 5), (OUT_R,), (SUM_S, 4),
     ),
     (G_RESULT, 7): (
-        (R_A, 3, 2), (SUM_S, 0), (R_B, 0, 0), (SUM_R, 0), (R_1, 3, 1), (R_A, 3, 0), (R_A, 4, 0),
-        (R_S, 8, 1), (R_S, 7, 0), (R_A, 5, 0), (R_B, 8, 3), (R_A, 5, 2), (SUM_S, 1), (R_B, 7, 2),
-        (R_B, 8, 0), (R_1, 3, 0), (R_S, 6, 0), (R_2, 1), (R_A, 6, 3), (R_1, 2, 0), (R_B, 6, 1),
-        (R_B, 8, 1), (R_B, 7, 0), (R_1, 5, 1), (R_A, 8, 3), (R_1, 5, 0), (R_A, 8, 0), (R_A, 6, 2),
-        (R_B, 0, 1), (R_B, 6, 0), (R_B, 8, 2), (R_B, 7, 3), (R_A, 8, 1), (R_2, 2),
+        (R_2, 8), (R_L, 8), (R_L, 1), (R_E, 1), (R_E, 8), (R_E, 3), (R_1, 0, 0), (R_E, 2),
     ),
     G_TAIL: (
-        (R_1, 6, 1), (R_A, 7, 1), (R_2, 3), (R_A, 8, 2), (R_1, 8, 0), (SUM_R, 1), (R_1, 4, 0),
-        (R_A, 7, 3), (SUM_S, 2), (R_1, 8, 1), (R_A, 6, 1), (R_L, 3), (R_A, 6, 0), (R_A, 7, 2),
-        (R_2, 4), (SUM_R, 2), (SUM_S, 3), (R_L, 1), (R_1, 7, 1), (R_2, 8), (R_A, 7, 0), (R_2, 5),
-        (R_L, 4), (R_L, 5), (R_L, 8), (R_E, 3), (R_A, 0, 0), (R_A, 0, 1), (R_L, 2), (SUM_R, 3),
-        (R_1, 7, 0), (R_E, 1), (R_1, 6, 0), (SUM_S, 4), (R_2, 6), (R_E, 2), (R_L, 6), (R_2, 7),
-        (R_L, 7), (R_1, 0, 0), (R_E, 4), (R_E, 5), (R_E, 8), (R_2, 0), (R_E, 7), (R_E, 6),
-        (SUM_R, 4), (R_L, 0),
+        (R_2, 0), (R_E, 6), (R_E, 7), (SUM_R, 4), (R_L, 0),
     ),
 }
 

time: 153 us -> 151 us (0.987)
  Pallas kernels: 152 us -> 150 us
    pallas_call x1, Pallas kernels: 149 us -> 147 us  [kernel_on_device(): pl.pallas_call(layer_kernel, out_shape=outs, in_specs=[hbm, smem, hbm, hb...]
where the time goes in v5:
time: 151 us
  Pallas kernels  150 us (99%)
    pallas_call x1, Pallas kernels, kernel_on_device(): pl.pallas_call(layer_kernel, out_shape=outs, in_specs=[hbm, smem, hbm, hb...  147 us
    pallas_call x1, Pallas kernels, kernel_on_device(): pl.pallas_call(finish_kernel, out_shape=final, in_specs=[hbm] * 7, out_sp...  3.02 us

profile of v5, /device:TPU:0, one launch (start us, length us, event | category | flops | bytes accessed | tf_op | source)
XLA Modules:
  0.0 151.2 jit_solution(14570331876847416105)
XLA Ops:
  0.6 147.4 %shard_map.220 = (bf16[256,1024]{1,0:T(8,128)(2,1)}, f32[256,1024]{1,0:T(8,128)}, bf16[3,32,1024]{2,1,0:T(8,128)(2,1)}, f32[8,128]{1,0:T(8,128)}, bf16[2,32,1408...) custom-call(bf16[256,1024]{1,0:T(8,128)(2,1)} %tok_hbm.1, s32[4]{0:T(128)} %len_ref.1, ...), custom_call_target="tpu_custom_call" | custom-call | tf_op jit(solution)/shard_map/pallas_call | solution.py:1369
  148.0 3.0 %shard_map.221 = (bf16[256,1024]{1,0:T(8,128)(2,1)}, f32[256,1024]{1,0:T(8,128)}, f32[32,1024]{1,0:T(8,128)}, f32[32,512]{1,0:T(8,128)}, f32[16,512]{1,0:T(8,128...) custom-call(bf16[256,1024]{1,0:T(8,128)(2,1)} %get-tuple-element.31., ...), custom_call_target="tpu_custom_call" | custom-call | tf_op jit(solution)/shard_map/pallas_call | solution.py:1387

commit v6 on v5

--- a/solution.py
+++ b/solution.py
@@ -1300,11 +1300,20 @@
     in_sem, out_sem = refs[36:]
     takes = [pltpu.make_async_copy(src, dst, in_sem.at[k]) for k, (src, dst) in enumerate(zip(given, bufs))]
     gives = [pltpu.make_async_copy(src, dst, out_sem.at[k]) for k, (src, dst) in enumerate(zip([*bufs[:2], *casts], outs))]
-    for k in (1, 0, 4, 5, 6, 2, 3):
+    slow = []
+    for k in (1, 0):
+        for p in range(4):
+            rows = pl.ds(p * 64, 64)
+            slot = 4 * k + p
+            come = pltpu.make_async_copy(given[k].at[rows], bufs[k].at[rows], in_sem.at[7 + slot])
+            leave = pltpu.make_async_copy(bufs[k].at[rows], outs[k].at[rows], out_sem.at[12 + slot])
+            come.start()
+            slow.append((come, leave))
+    for k in (4, 5, 6, 2, 3):
         takes[k].start()
-    for k in (1, 0):
-        takes[k].wait()
-        gives[k].start()
+    for come, leave in slow:
+        come.wait()
+        leave.start()
     _, _, at_ref, gain_ref, gg_ref, gu_ref, gd_ref = bufs
     gq_o, gl_o, gk_o, gv_o, go_o, ga_o, gf_o, gg_o, gu_o, gd_o = casts
     for k, src, dst in ((4, gg_ref, gg_o), (5, gu_ref, gu_o)):
@@ -1330,7 +1339,7 @@
     gf_o[...] = picked[1:2]
     for k in range(2, 9):
         gives[k].start()
-    for give in gives:
+    for give in [*gives[2:], *[leave for _, leave in slow]]:
         give.wait()
 
 
@@ -1391,7 +1400,7 @@
         out_specs=[hbm] * 12,
         scratch_shapes=[
             *[V(one.shape, one.dtype) for one in [*outs, *final[2:]]],
-            pltpu.SemaphoreType.DMA((7,)), pltpu.SemaphoreType.DMA((12,)),
+            pltpu.SemaphoreType.DMA((15,)), pltpu.SemaphoreType.DMA((20,)),
         ],
     )(*res)
     return tuple(out[:7]) + (out[7].reshape(32), out[8].reshape(32)) + tuple(out[9:])

time: 151 us -> 151 us (level)
  no operation moved by 1% of the time
where the time goes in v6:
time: 151 us
  Pallas kernels  150 us (99%)
    pallas_call x1, Pallas kernels, kernel_on_device(): pl.pallas_call(layer_kernel, out_shape=outs, in_specs=[hbm, smem, hbm, hb...  147 us

profile of v6, /device:TPU:0, one launch (start us, length us, event | category | flops | bytes accessed | tf_op | source)
XLA Modules:
  0.0 151.1 jit_solution(9366188823853686542)
XLA Ops:
  0.6 147.4 %shard_map.220 = (bf16[256,1024]{1,0:T(8,128)(2,1)}, f32[256,1024]{1,0:T(8,128)}, bf16[3,32,1024]{2,1,0:T(8,128)(2,1)}, f32[8,128]{1,0:T(8,128)}, bf16[2,32,1408...) custom-call(bf16[256,1024]{1,0:T(8,128)(2,1)} %tok_hbm.1, s32[4]{0:T(128)} %len_ref.1, ...), custom_call_target="tpu_custom_call" | custom-call | tf_op jit(solution)/shard_map/pallas_call | solution.py:1378
  148.0 2.9 %shard_map.221 = (bf16[256,1024]{1,0:T(8,128)(2,1)}, f32[256,1024]{1,0:T(8,128)}, f32[32,1024]{1,0:T(8,128)}, f32[32,512]{1,0:T(8,128)}, f32[16,512]{1,0:T(8,128...) custom-call(bf16[256,1024]{1,0:T(8,128)(2,1)} %get-tuple-element.31., ...), custom_call_target="tpu_custom_call" | custom-call | tf_op jit(solution)/shard_map/pallas_call | solution.py:1396
